TPU v7x, 32 devices: a whole 2x2x4 slice. The times are simulated.
32 devices in a mesh: dp: 4 (over y, core), ctx: 8 (over z, x).
Axes of the slice: x: 2, y: 2, z: 4, core: 2. Of those that a mesh axis runs over, the one named last changes fastest.
Arguments:
- context_query_rows: bfloat16 [4096, 4096], P(('dp', 'ctx')), parts along dimension 0, may hold values from -16 to 16
- context_key_rows: bfloat16 [4096, 512], P(('dp', 'ctx')), parts along dimension 0, may hold values from -6 to 6
- context_value_rows: bfloat16 [4096, 512], P(('dp', 'ctx')), parts along dimension 0, may hold values from -6 to 6
- question_query_rows: bfloat16 [1024, 4096], P(('dp', 'ctx')), parts along dimension 0, may hold values from -16 to 16
- token_mask: int32 [4096], P(('dp', 'ctx')), parts along dimension 0, may hold values 0 or 1
- live_blocks: int32 [4], P('dp'), parts along dimension 0, may hold values from 4 to 8
Outputs:
- context_output: bfloat16 [4096, 4096], P(('dp', 'ctx')), parts along dimension 0
- query_output: bfloat16 [1024, 4096], P(('dp', 'ctx')), parts along dimension 0
There are 4 independent parts, one for each index of `dp`. A program takes and returns all parts, laid end to end along the dimension named above; each array names one. Nothing has to cross between parts.
All inputs are finite; a program needn't handle non-finite values. No bound on the sum of `token_mask` on one device may be relied on, other than what follows from the above.
Results may differ from a plain program's by a relative error of at most 0.0026.
Values may be sent and summed in bfloat16 or wider, within the bound.
No kernel may reach another device: no remote copies, remote signals or barrier semaphores. Data moves between devices by JAX's collectives and lax.ppermute only.
A program may use at most 64 MiB of HBM per device.

v0:
```python
import jax
import jax.numpy as jnp
from jax import lax
from jax.sharding import PartitionSpec as P

QUERY_HEADS = 32
KEY_VALUE_HEADS = 4
HEAD_SIZE = 128


def from_root(value, axis, root):
    mine = lax.axis_index(axis) == root
    return lax.psum(jnp.where(mine, value, jnp.zeros_like(value)), axis)


def local(
    context_query_rows,
    context_key_rows,
    context_value_rows,
    question_query_rows,
    token_mask,
    live_blocks,
):
    inv_root = HEAD_SIZE ** (-0.5)
    heads_per_group = QUERY_HEADS // KEY_VALUE_HEADS
    width = heads_per_group * HEAD_SIZE
    device_count = lax.axis_size("ctx")
    block_index = lax.axis_index("ctx")
    block_rows = context_query_rows.shape[0]
    local_rows = jnp.arange(block_rows, dtype=jnp.int32)
    is_live = block_index < live_blocks[0]
    key_valid = ((token_mask != 0) | (block_index == 0) & (local_rows == 0)) & is_live
    leading_block_keys, leading_block_values, anchor_flag = (
        from_root(context_key_rows, "ctx", 0),
        from_root(context_value_rows, "ctx", 0),
        from_root(key_valid.astype(jnp.bfloat16), "ctx", 0),
    )
    anchor_valid = anchor_flag > 0.5
    causal = local_rows[None, :] <= local_rows[:, None]
    diagonal = local_rows[None, :] == local_rows[:, None]
    see_anchor = jnp.broadcast_to(
        anchor_valid[None, :] & (block_index > 0), (block_rows, block_rows)
    )
    see_own = key_valid[None, :] & causal | diagonal
    visible = jnp.concatenate([see_anchor, see_own], 1)
    all_keys = jnp.concatenate([leading_block_keys, context_key_rows], 0)
    all_vals = jnp.concatenate([leading_block_values, context_value_rows], 0)
    pieces = []
    for grouped_heads in range(KEY_VALUE_HEADS):
        query_lanes = context_query_rows[
            :, grouped_heads * width : (grouped_heads + 1) * width
        ].reshape(block_rows, heads_per_group, HEAD_SIZE)
        key_lanes = all_keys[:, grouped_heads * HEAD_SIZE : (grouped_heads + 1) * HEAD_SIZE]
        value_lanes = all_vals[:, grouped_heads * HEAD_SIZE : (grouped_heads + 1) * HEAD_SIZE]
        scores = (
            jnp.einsum("qgd,kd->gqk", query_lanes, key_lanes, preferred_element_type=jnp.float32)
            * inv_root
        )
        scores = jnp.where(visible[None], scores, -1e30)
        row_top = jnp.max(scores, axis=-1, keepdims=True)
        weights = jnp.where(visible[None], jnp.exp(scores - row_top), 0.0)
        row_total = jnp.sum(weights, axis=-1)
        rounded = weights.astype(jnp.bfloat16)
        mixed = jnp.einsum("gqk,kd->qgd", rounded, value_lanes, preferred_element_type=jnp.float32)
        mixed = mixed / jnp.transpose(row_total)[:, :, None]
        pieces.append(mixed.reshape(block_rows, width))
    context_output = (jnp.concatenate(pieces, 1) * is_live.astype(jnp.float32)).astype(jnp.bfloat16)
    all_queries = lax.all_gather(question_query_rows, "ctx", axis=0, tiled=True)
    query_rows = all_queries.shape[0]
    tops = []
    totals = []
    parts = []
    for grouped_heads in range(KEY_VALUE_HEADS):
        query_lanes = all_queries[:, grouped_heads * width : (grouped_heads + 1) * width].reshape(
            query_rows, heads_per_group, HEAD_SIZE
        )
        key_lanes = context_key_rows[:, grouped_heads * HEAD_SIZE : (grouped_heads + 1) * HEAD_SIZE]
        value_lanes = context_value_rows[
            :, grouped_heads * HEAD_SIZE : (grouped_heads + 1) * HEAD_SIZE
        ]
        scores = (
            jnp.einsum("qgd,kd->gqk", query_lanes, key_lanes, preferred_element_type=jnp.float32)
            * inv_root
        )
        scores = jnp.where(key_valid[None, None, :], scores, -1e30)
        row_top = jnp.max(scores, axis=-1)
        weights = jnp.where(key_valid[None, None, :], jnp.exp(scores - row_top[:, :, None]), 0.0)
        row_total = jnp.sum(weights, axis=-1)
        rounded = weights.astype(jnp.bfloat16)
        block_part = jnp.einsum(
            "gqk,kd->qgd", rounded, value_lanes, preferred_element_type=jnp.float32
        )
        tops.append(jnp.transpose(row_top))
        totals.append(jnp.transpose(row_total))
        parts.append(block_part.reshape(query_rows, width))
    local_top = jnp.concatenate(tops, 1)
    local_total = jnp.concatenate(totals, 1)
    local_part = jnp.concatenate(parts, 1)
    own_share = query_rows // device_count
    global_top = lax.pmax(local_top.astype(jnp.bfloat16), "ctx").astype(local_top.dtype)
    factor = jnp.exp(local_top - global_top)
    scaled_total = local_total * factor
    scaled_part = (
        local_part.reshape(query_rows, QUERY_HEADS, HEAD_SIZE) * factor[:, :, None]
    ).reshape(query_rows, QUERY_HEADS * HEAD_SIZE)
    numerator, denominator = lax.psum((scaled_part, scaled_total), "ctx")
    numerator = lax.dynamic_slice_in_dim(numerator, block_index * own_share, own_share, 0)
    denominator = lax.dynamic_slice_in_dim(denominator, block_index * own_share, own_share, 0)
    own_rows = numerator.shape[0]
    query_output = (
        (numerator.reshape(own_rows, QUERY_HEADS, HEAD_SIZE) / denominator[:, :, None])
        .reshape(own_rows, QUERY_HEADS * HEAD_SIZE)
        .astype(jnp.bfloat16)
    )
    return (context_output, query_output)


def solution(mesh):
    placed = (
        P(("dp", "ctx"), None),
        P(("dp", "ctx"), None),
        P(("dp", "ctx"), None),
        P(("dp", "ctx"), None),
        P(("dp", "ctx")),
        P("dp"),
    )
    return jax.shard_map(
        local,
        mesh=mesh,
        in_specs=placed,
        out_specs=(P(("dp", "ctx"), None), P(("dp", "ctx"), None)),
        check_vma=False,
    )
```

profile of v0, /device:TPU:18, one launch (start us, length us, event | category | flops | bytes accessed | tf_op | source)
XLA Modules:
  0.0 301.8 jit_solution(438108193003821185)
XLA Ops:
  7.2 0.7 all-gather.2.cloned.1.call-update
  8.0 0.7 broadcast_select_fusion
  9.4 0.7 broadcast_select_fusion.2
  10.1 15.2 %psum.36 = bf16[128]{0:T(256)(128)(2,1)S(1)} all-reduce(bf16[128]{0:T(256)(128)(2,1)S(1)} %get-tuple-element.10), channel_id=1, replica_groups=mesh['dp'=4,'ctx'=8] {'ctx'}, use_global_device_ids=true, to_apply=%region_1.2 | all-reduce | flops 128 | bytes 512 | tf_op jit(solution)/shard_map/psum | solution.py:13
  25.3 1.3 fusion.106
  26.6 0.9 copy.127
  27.4 0.8 copy.128
  28.3 0.8 copy.129
  29.1 0.8 copy.130
  30.0 29.2 %all-gather.2.cloned.1.call-done = bf16[256,4096]{1,0:T(8,128)(2,1)} async-done(((bf16[32,4096]{1,0:T(8,128)(2,1)}), bf16[256,4096]{1,0:T(8,128)(2,1)}) %all-gather.2.cloned.1.call-update) | async-done | bytes 2097168 | tf_op jit(solution)/shard_map/all_gather | solution.py:68
  59.2 2.6 fusion.105
  61.8 0.2 copy.132
  62.0 0.2 copy.134
  62.2 0.3 fusion.111
  62.5 0.3 fusion.112
  62.8 1.0 copy.136
  63.8 1.3 fusion.113
  65.2 2.0 copy.138
  67.2 1.3 fusion.114
  68.6 1.3 convolution_bitcast_fusion
  69.9 1.4 convolution_bitcast_fusion.1
  71.3 1.4 convolution_bitcast_fusion.2
  72.7 0.9 fusion.37
  73.6 0.4 convolution_bitcast_fusion.3
  74.0 29.9 %pmax.7 = bf16[256,32]{0,1:T(8,128)(2,1)S(1)} all-reduce(bf16[256,32]{0,1:T(8,128)(2,1)S(1)} %fusion.84), channel_id=1, replica_groups=mesh['dp'=4,'ctx'=8] {'ctx'}, use_global_device_ids=true, to_apply=%region_15.16 | all-reduce | flops 8192 | bytes 32768 | tf_op jit(solution)/shard_map/pmax | solution.py:100
  103.9 4.4 %maximum_multiply_fusion = f32[256,32,128]{0,2,1:T(8,128)} fusion(f32[256,8,128]{0,2,1:T(8,128)} %convolution_bitcast_fusion, f32[256,8,128]{0,2,1:T(8,128)} %convolution_bitcast_fusion.1, f32[256,8,128]{0,2,1:T(8,128)} %convolution_bitcast_fusion.2, f32[256,8,128]{0,2,1:T(8,128)S(1)} %convolution_bitcast_fusion.3, f32[256,32]{0,1:T(8,128)S(1)} %get-tuple-element.9), kind=kLoop, calls=%fused_computation.4 | loop fusion | flops 4194304 | bytes 8421376 | tf_op jit(solution)/shard_map/mul | solution.py:104
  108.3 5.6 %copy.101 = f32[256,4096]{1,0:T(8,128)} copy(f32[256,4096]{0,1:T(8,128)} %bitcast.188) | data formatting | bytes 8388608 | tf_op jit(solution)/shard_map/mul | solution.py:104
  114.1 18.7 %all-reduce.6.cloned.1.call-done = (bf16[128,512]{1,0:T(8,128)(2,1)}, bf16[128,512]{1,0:T(8,128)(2,1)}) async-done(((bf16[128,512]{1,0:T(8,128)(2,1)}, bf16[128,512]{1,0:T(8,128)(2,1)}), (bf16[128,512]{1,0:T(8,128)(2,1)}, bf16[128,512]{1,0:T(8,128)(2,1)})) %all-reduce.6.cloned.1.call-update) | async-done | bytes 262160 | tf_op jit(solution)/shard_map/psum | solution.py:13
  132.9 0.9 constant_dynamic-update-slice_fusion.3
  133.8 1.0 constant_dynamic-update-slice_fusion.1
  134.9 0.5 fusion.110
  135.4 0.3 fusion.32
  135.7 0.4 fusion.33
  136.1 0.2 copy.81
  136.3 0.5 fusion.109
  136.8 0.3 fusion.30
  137.1 0.4 fusion.34
  137.5 0.2 copy.82
  137.8 0.5 fusion.108
  138.3 0.3 fusion.28
  138.6 1.2 fusion.35
  140.0 0.5 fusion.107
  140.6 1.1 fusion.26
  141.7 1.2 fusion.36
  143.1 1.1 fusion.4
  144.3 31.4 %psum.39 = f32[256,32]{0,1:T(8,128)S(1)} all-reduce(f32[256,32]{0,1:T(8,128)S(1)} %get-tuple-element.8), channel_id=1, replica_groups=mesh['dp'=4,'ctx'=8] {'ctx'}, use_global_device_ids=true, to_apply=%region_21.22 | all-reduce | flops 8192 | bytes 65536 | tf_op jit(solution)/shard_map/psum | solution.py:106
  175.8 117.1 %all-reduce.4.cloned.1.call-done = f32[256,4096]{1,0:T(8,128)} async-done(((f32[256,4096]{1,0:T(8,128)}), f32[256,4096]{1,0:T(8,128)}) %all-reduce.4.cloned.1.call-update) | async-done | bytes 4194320 | tf_op jit(solution)/shard_map/psum | solution.py:106
  293.2 2.1 fusion.49
  (34 shorter events, 1.2 us)
Async XLA Ops:
  7.2 52.0 %all-gather.2.cloned.1.call-start = ((), (), s32[]{:S(2)}) async-start(), calls=%async_computation | async-start | bytes 2359296 | tf_op jit(solution)/shard_map/all_gather | solution.py:68
  7.9 125.0 %all-reduce.6.cloned.1.call-start = ((), (), s32[]{:S(2)}) async-start(), calls=%async_computation.2 | async-start | bytes 524288 | tf_op jit(solution)/shard_map/psum | solution.py:13
  8.7 284.2 %all-reduce.4.cloned.1.call-start = ((), (), s32[]{:S(2)}) async-start(), calls=%async_computation.1 | async-start | bytes 8388608 | tf_op jit(solution)/shard_map/psum | solution.py:106
  26.5 35.7 %copy-start.1 = (bf16[128,512]{1,0:T(8,128)(2,1)S(1)}, bf16[128,512]{1,0:T(8,128)(2,1)}, u32[]{:S(2)}) copy-start(bf16[128,512]{1,0:T(8,128)(2,1)} %param.7) | copy-start | bytes 393220
  62.2 6.4 %copy-start = (bf16[128,512]{1,0:T(8,128)(2,1)S(1)}, bf16[128,512]{1,0:T(8,128)(2,1)}, u32[]{:S(2)}) copy-start(bf16[128,512]{1,0:T(8,128)(2,1)} %param.8) | copy-start | bytes 393220
  113.9 21.0 %copy-start.5 = (bf16[128,1024]{0,1:T(8,128)(2,1)S(1)}, bf16[128,1024]{0,1:T(8,128)(2,1)}, u32[]{:S(2)}) copy-start(bf16[128,1024]{0,1:T(8,128)(2,1)} %copy.127) | copy-start | bytes 786436
  133.8 6.2 %copy-start.6 = (bf16[256,512]{1,0:T(8,128)(2,1)}, bf16[256,512]{1,0:T(8,128)(2,1)S(1)}, u32[]{:S(2)}) copy-start(bf16[256,512]{1,0:T(8,128)(2,1)S(1)} %constant_dynamic-update-slice_fusion.2) | copy-start | bytes 786436
  134.8 1.5 copy-start.4
  134.9 2.3 copy-start.7
  136.3 1.5 copy-start.3
  137.7 2.3 copy-start.2
Sparse Core Ops, SparseCore 0:
  10.1 49.0 all-gather.1
  62.7 70.1 all-reduce.5
  137.0 155.8 all-reduce.3
where the time goes:
time: 305 us; the launch traced here: 302 us
  waiting for transfers between devices  166 us (54%)
  blocking collectives  76.5 us (25%)
  local copies, waits for them, and re-layouts  19.4 us (6%)
  matrix products  15 us (5%)
  between operations  14.7 us (5%)
  other arithmetic  10.1 us (3%)
    psum x1, waiting for transfers between devices, local(): numerator, denominator = lax.psum((scaled_part, scaled_total), 'ctx')  117 us
    psum x1, blocking collectives, local(): numerator, denominator = lax.psum((scaled_part, scaled_total), 'ctx')  31.4 us
    pmax x1, blocking collectives, local(): lax.pmax(local_top.astype(jnp.bfloat16), 'ctx').astype(local_top.dtype)  29.9 us
    all_gather x1, waiting for transfers between devices, local(): all_queries = lax.all_gather(question_query_rows, 'ctx', axis=0, tiled=True)  29.2 us
    psum x1, waiting for transfers between devices, from_root(): return lax.psum(jnp.where(mine, value, jnp.zeros_like(value)), axis)  18.7 us
    psum x1, blocking collectives, from_root(): return lax.psum(jnp.where(mine, value, jnp.zeros_like(value)), axis)  15.2 us
    unnamed x26, local copies, waits for them, and re-layouts  8.79 us
    dot_general x8, matrix products, local(): jnp.einsum('gqk,kd->qgd', rounded, value_lanes, preferred_element_type=jn...  7.74 us
  transfers between devices with their start and end apart: 3, of which 3 were waited for; matrix products, arithmetic and copies ran while one was open for 14% of the time, Pallas kernels for 0%

commit v1 on v0

v1 whole, which is shorter than its diff:
```python
import functools

import jax
import jax.numpy as jnp
from jax import lax
from jax.experimental import pallas as pl
from jax.experimental.pallas import tpu as pltpu
from jax.sharding import PartitionSpec as P

HEAD = 128
FLAG_ROWS = 16
HIDDEN = -1e30
NT = (((1,), (1,)), ((), ()))


def whole():
    return pl.BlockSpec(memory_space=pltpu.VMEM)


def scalar():
    return pl.BlockSpec(memory_space=pltpu.SMEM)


def pack_kernel(live_ref, mask_ref, k_ref, v_ref, o_ref):
    rows, width = k_ref.shape
    groups = width // HEAD
    block = lax.axis_index("ctx")
    for g in range(groups):
        o_ref[g * rows : (g + 1) * rows, :] = k_ref[:, g * HEAD : (g + 1) * HEAD]
        o_ref[(groups + g) * rows : (groups + g + 1) * rows, :] = v_ref[:, g * HEAD : (g + 1) * HEAD]
    token = lax.broadcasted_iota(jnp.int32, (1, rows), 1)
    valid = ((mask_ref[...] != 0) | ((block == 0) & (token == 0))) & (block < live_ref[0])
    flags = jnp.where(valid, 1.0, 0.0).astype(jnp.bfloat16)
    o_ref[2 * groups * rows :, :] = jnp.broadcast_to(flags, (FLAG_ROWS, rows))


def pack(live_blocks, token_mask, k, v):
    rows, width = k.shape
    return pl.pallas_call(
        pack_kernel,
        out_shape=jax.ShapeDtypeStruct((2 * rows * width // HEAD + FLAG_ROWS, HEAD), jnp.bfloat16),
        in_specs=[scalar(), whole(), whole(), whole()],
        out_specs=whole(),
        name="pack",
    )(live_blocks, token_mask.reshape(1, rows), k, v)


def context_kernel(pieces, rows, groups, live_ref, q_ref, *refs):
    piece_refs, o_ref, anchor = refs[:pieces], refs[pieces], refs[pieces + 1]
    g = pl.program_id(0)
    block = lax.axis_index("ctx")

    @pl.when(g == 0)
    def _():
        for d in range(pieces):

            @pl.when(block == d)
            def _():
                anchor[...] = piece_refs[d][...]

    own = piece_refs[0]
    k_at = pl.ds(pl.multiple_of(g * rows, rows), rows)
    v_at = pl.ds(pl.multiple_of((groups + g) * rows, rows), rows)
    keys = jnp.concatenate([anchor[k_at, :], own[k_at, :]], 0)
    values = jnp.concatenate([anchor[v_at, :], own[v_at, :]], 0)
    flag_at = 2 * groups * rows
    i = lax.broadcasted_iota(jnp.int32, (rows, rows), 0)
    j = lax.broadcasted_iota(jnp.int32, (rows, rows), 1)
    anchor_flag = anchor[flag_at : flag_at + FLAG_ROWS, :].astype(jnp.float32)[:1]
    own_flag = own[flag_at : flag_at + FLAG_ROWS, :].astype(jnp.float32)[:1]
    see_anchor = jnp.broadcast_to(anchor_flag, (rows, rows)) * jnp.where(block > 0, 1.0, 0.0)
    see_own = jnp.where(j < i, jnp.broadcast_to(own_flag, (rows, rows)), jnp.where(i == j, 1.0, 0.0))
    visible = jnp.concatenate([see_anchor, see_own], 1) > 0.5
    alive = jnp.where(block < live_ref[0], 1.0, 0.0)
    for h in range(q_ref.shape[1] // HEAD):
        q = q_ref[:, h * HEAD : (h + 1) * HEAD]
        s = lax.dot_general(q, keys, NT, preferred_element_type=jnp.float32) * HEAD**-0.5
        s = jnp.where(visible, s, HIDDEN)
        m = jnp.max(s, axis=1, keepdims=True)
        p = jnp.where(visible, jnp.exp(s - m), 0.0)
        l = jnp.sum(p, axis=1, keepdims=True)
        a = jnp.dot(p.astype(jnp.bfloat16), values, preferred_element_type=jnp.float32)
        o_ref[:, h * HEAD : (h + 1) * HEAD] = (a * (alive / l)).astype(o_ref.dtype)


def context(live_blocks, q, pieces, groups):
    rows, width = q.shape
    share = width // groups
    return pl.pallas_call(
        functools.partial(context_kernel, len(pieces), rows, groups),
        out_shape=jax.ShapeDtypeStruct(q.shape, q.dtype),
        grid=(groups,),
        in_specs=[scalar(), pl.BlockSpec((rows, share), lambda g: (0, g))] + [whole()] * len(pieces),
        out_specs=pl.BlockSpec((rows, share), lambda g: (0, g)),
        scratch_shapes=[pltpu.VMEM(pieces[0].shape, pieces[0].dtype)],
        name="context",
    )(live_blocks, q, *pieces)


def query_kernel(pieces, rows, groups, q_ref, *refs):
    piece_refs, o_ref = refs[:pieces], refs[pieces]
    n_q, width = q_ref.shape
    heads = width // HEAD // groups
    flag_at = 2 * groups * rows
    for g in range(groups):
        first = g * heads
        q = jnp.concatenate(
            [q_ref[:, (first + h) * HEAD : (first + h + 1) * HEAD].astype(jnp.float32) for h in range(heads)], 0
        ).astype(jnp.bfloat16)
        tops, totals, parts = [], [], []
        for ref in piece_refs:
            flag = ref[flag_at : flag_at + FLAG_ROWS, :].astype(jnp.float32)[:1]
            valid = jnp.broadcast_to(flag, (q.shape[0], rows)) > 0.5
            s = lax.dot_general(q, ref[g * rows : (g + 1) * rows, :], NT, preferred_element_type=jnp.float32)
            s = jnp.where(valid, s * HEAD**-0.5, HIDDEN)
            m = jnp.max(s, axis=1, keepdims=True)
            p = jnp.where(valid, jnp.exp(s - m), 0.0)
            tops.append(m)
            totals.append(jnp.sum(p, axis=1, keepdims=True))
            v = ref[(groups + g) * rows : (groups + g + 1) * rows, :]
            parts.append(jnp.dot(p.astype(jnp.bfloat16), v, preferred_element_type=jnp.float32))
        top = functools.reduce(jnp.maximum, tops)
        factors = [jnp.exp(m - top) for m in tops]
        total = sum(f * l for f, l in zip(factors, totals))
        part = sum(f * a for f, a in zip(factors, parts)) / total
        for h in range(heads):
            o_ref[:, (first + h) * HEAD : (first + h + 1) * HEAD] = part[h * n_q : (h + 1) * n_q].astype(o_ref.dtype)


def query(q, pieces, rows, groups):
    return pl.pallas_call(
        functools.partial(query_kernel, len(pieces), rows, groups),
        out_shape=jax.ShapeDtypeStruct(q.shape, q.dtype),
        in_specs=[whole()] * (1 + len(pieces)),
        out_specs=whole(),
        name="query",
    )(q, *pieces)


def gather(own, n):
    def swap(value, d):
        return lax.ppermute(value, "ctx", [(i, i ^ d) for i in range(n)])

    pieces = {0: own}
    for d in range(2, n, 2):
        pieces[d] = swap(own, d)
    pieces[1] = swap(own, 1)
    for d in range(2, n, 2):
        pieces[d + 1] = swap(pieces[d], 1)
    return [pieces[d] for d in range(n)]


def local(context_q, context_k, context_v, question_q, token_mask, live_blocks):
    n = lax.axis_size("ctx")
    rows, width = context_k.shape
    groups = width // HEAD
    own = pack(live_blocks, token_mask, context_k, context_v)
    pieces = gather(own, n)
    context_output = context(live_blocks, context_q, pieces, groups)
    query_output = query(question_q, pieces, rows, groups)
    return context_output, query_output


def solution(mesh):
    rows = P(("dp", "ctx"), None)
    return jax.shard_map(
        local,
        mesh=mesh,
        in_specs=(rows, rows, rows, rows, P(("dp", "ctx")), P("dp")),
        out_specs=(rows, rows),
        check_vma=False,
    )
```

time: 305 us -> 50.6 us (0.17)
  waiting for transfers between devices: 166 us -> 28 us
  blocking collectives: 76.5 us -> 0 us
  local copies, waits for them, and re-layouts: 19.4 us -> 0.72 us
  matrix products: 15 us -> 0 us
  Pallas kernels: 0 us -> 14.2 us
  between operations: 14.7 us -> 1.35 us
  other arithmetic: 10.1 us -> 0 us
  starting transfers between devices: 0.12 us -> 5.62 us
    psum x2 -> x0, waiting for transfers between devices: 136 us -> none  [the longest x1 117 us: local(): numerator, denominator = lax.psum((scaled_part, scaled_total), 'ctx')]
    psum x2 -> x0, blocking collectives: 46.6 us -> none  [the longest x1 31.4 us: local(): numerator, denominator = lax.psum((scaled_part, scaled_total), 'ctx')]
    pmax x1 -> x0, blocking collectives: 29.9 us -> none  [local(): lax.pmax(local_top.astype(jnp.bfloat16), 'ctx').astype(local_top.dtype)]
    all_gather x1 -> x0, waiting for transfers between devices: 29.2 us -> none  [local(): all_queries = lax.all_gather(question_query_rows, 'ctx', axis=0, tiled=True)]
    ppermute x0 -> x7, waiting for transfers between devices: none -> 28 us  [swap(): return lax.ppermute(value, 'ctx', [(i, i ^ d) for i in range(n)])]
    pallas_call x0 -> x3, Pallas kernels: none -> 14.2 us  [the longest x1 6.46 us: query(): pl.pallas_call(functools.partial(query_kernel, len(pieces), rows, groups)...]
    dot_general x16 -> x0, matrix products: 13 us -> none  [the longest x8 7.74 us: local(): jnp.einsum('gqk,kd->qgd', rounded, value_lanes, preferred_element_type=jn...]
    unnamed x26 -> x14, local copies, waits for them, and re-layouts: 8.79 us -> 0.72 us
  transfers between devices with their start and end apart: 3 -> 7, of which waited for: 3 -> 4; matrix products, arithmetic and copies ran while one was open for 14% -> 0% of each run, Pallas kernels for 0% -> 0%
where the time goes in v1:
time: 50.6 us; the launch traced here: 49.9 us
  waiting for transfers between devices  28 us (55%)
  Pallas kernels  14.2 us (28%)
  starting transfers between devices  5.62 us (11%)
  between operations  1.35 us (3%)
  local copies, waits for them, and re-layouts  0.72 us (1%)
    ppermute x7, waiting for transfers between devices, swap(): return lax.ppermute(value, 'ctx', [(i, i ^ d) for i in range(n)])  28 us
    pallas_call x1, Pallas kernels, query(): pl.pallas_call(functools.partial(query_kernel, len(pieces), rows, groups)...  6.46 us
    pallas_call x1, Pallas kernels, context(): pl.pallas_call(functools.partial(context_kernel, len(pieces), rows, group...  5.98 us
    ppermute x7, starting transfers between devices, swap(): return lax.ppermute(value, 'ctx', [(i, i ^ d) for i in range(n)])  5.62 us
    pallas_call x1, Pallas kernels, pack(): pl.pallas_call(pack_kernel, out_shape=jax.ShapeDtypeStruct((2 * rows * wi...  1.75 us
  transfers between devices with their start and end apart: 7, of which 4 were waited for; matrix products, arithmetic and copies ran while one was open for 0% of the time, Pallas kernels for 0%

profile of v1, /device:TPU:18, one launch (start us, length us, event | category | flops | bytes accessed | tf_op | source)
XLA Modules:
  0.0 49.9 jit_solution(7473095760377004377)
XLA Ops:
  1.3 1.8 %pack.1.refs_0_ = bf16[1040,128]{1,0:T(8,128)(2,1)} custom-call(s32[1]{0:T(128)S(6)} %copy.8.live_ref, s32[1,128]{1,0:T(1,128)} %bitcast.1, bf16[128,512]{1,0:T(8,128)(2,1)} %k_ref.1, bf16[128,512]{1,0:T(8,128)(2,1)} %v_ref.1), custom_call_target="tpu_custom_call" | custom-call | tf_op jit(solution)/shard_map/pack/pallas_call | solution.py:39
  3.0 1.6 %collective-permute-start.1 = (bf16[1040,128]{1,0:T(8,128)(2,1)}, bf16[1040,128]{1,0:T(8,128)(2,1)S(1)}, u32[]{:S(2)}, u32[]{:S(2)}) collective-permute-start(bf16[1040,128]{1,0:T(8,128)(2,1)} %pack.1.refs_0_), channel_id=1, source_target_pairs={{0,2},{1,3},{2,0},{3,1},{4,6},{5,7},{6,4},{7,5},{8,10},{9,11},{10,... | collective-permute-start | bytes 798728 | tf_op jit(solution)/shard_map/ppermute | solution.py:142
  4.6 0.3 collective-permute-start.3
  4.9 1.6 %collective-permute-start.5 = (bf16[1040,128]{1,0:T(8,128)(2,1)}, bf16[1040,128]{1,0:T(8,128)(2,1)S(1)}, u32[]{:S(2)}, u32[]{:S(2)}) collective-permute-start(bf16[1040,128]{1,0:T(8,128)(2,1)} %pack.1.refs_0_), channel_id=1, source_target_pairs={{0,6},{1,7},{2,4},{3,5},{4,2},{5,3},{6,0},{7,1},{8,14},{9,15},{10,... | collective-permute-start | bytes 798728 | tf_op jit(solution)/shard_map/ppermute | solution.py:142
  6.5 0.5 %collective-permute-start = (bf16[1040,128]{1,0:T(8,128)(2,1)}, bf16[1040,128]{1,0:T(8,128)(2,1)S(1)}, u32[]{:S(2)}, u32[]{:S(2)}) collective-permute-start(bf16[1040,128]{1,0:T(8,128)(2,1)} %pack.1.refs_0_), channel_id=1, source_target_pairs={{0,1},{1,0},{2,3},{3,2},{4,5},{5,4},{6,7},{7,6},{8,9},{9,8},{10,11... | collective-permute-start | bytes 798728 | tf_op jit(solution)/shard_map/ppermute | solution.py:142
  7.1 7.9 %collective-permute-done.1.refs_2_ = bf16[1040,128]{1,0:T(8,128)(2,1)S(1)} collective-permute-done((bf16[1040,128]{1,0:T(8,128)(2,1)}, bf16[1040,128]{1,0:T(8,128)(2,1)S(1)}, u32[]{:S(2)}, u32[]{:S(2)}) %collective-permute-start.1) | collective-permute-done | bytes 266272 | tf_op jit(solution)/shard_map/ppermute | solution.py:142
  14.9 0.0 copy-start
  14.9 0.5 %collective-permute-start.2 = (bf16[1040,128]{1,0:T(8,128)(2,1)S(1)}, bf16[1040,128]{1,0:T(8,128)(2,1)S(1)}, u32[]{:S(2)}, u32[]{:S(2)}) collective-permute-start(bf16[1040,128]{1,0:T(8,128)(2,1)S(1)} %collective-permute-done.1.refs_2_), channel_id=1, source_target_pairs={{0,1},{1,0},{2,3},{3,2},{4,5},{5,4},{6,7},{7,6},{8,9},{9,8},{10,11... | collective-permute-start | bytes 798728 | tf_op jit(solution)/shard_map/ppermute | solution.py:142
  15.5 8.0 %collective-permute-done.3.refs_4_ = bf16[1040,128]{1,0:T(8,128)(2,1)S(1)} collective-permute-done((bf16[1040,128]{1,0:T(8,128)(2,1)}, bf16[1040,128]{1,0:T(8,128)(2,1)S(1)}, u32[]{:S(2)}, u32[]{:S(2)}) %collective-permute-start.3) | collective-permute-done | bytes 266272 | tf_op jit(solution)/shard_map/ppermute | solution.py:142
  23.5 0.0 copy-start.1
  23.5 0.5 %collective-permute-start.4 = (bf16[1040,128]{1,0:T(8,128)(2,1)S(1)}, bf16[1040,128]{1,0:T(8,128)(2,1)S(1)}, u32[]{:S(2)}, u32[]{:S(2)}) collective-permute-start(bf16[1040,128]{1,0:T(8,128)(2,1)S(1)} %collective-permute-done.3.refs_4_), channel_id=1, source_target_pairs={{0,1},{1,0},{2,3},{3,2},{4,5},{5,4},{6,7},{7,6},{8,9},{9,8},{10,11... | collective-permute-start | bytes 798728 | tf_op jit(solution)/shard_map/ppermute | solution.py:142
  24.0 5.7 %collective-permute-done.5.refs_6_ = bf16[1040,128]{1,0:T(8,128)(2,1)S(1)} collective-permute-done((bf16[1040,128]{1,0:T(8,128)(2,1)}, bf16[1040,128]{1,0:T(8,128)(2,1)S(1)}, u32[]{:S(2)}, u32[]{:S(2)}) %collective-permute-start.5) | collective-permute-done | bytes 266272 | tf_op jit(solution)/shard_map/ppermute | solution.py:142
  29.7 0.0 copy-start.2
  29.7 0.5 %collective-permute-start.6 = (bf16[1040,128]{1,0:T(8,128)(2,1)S(1)}, bf16[1040,128]{1,0:T(8,128)(2,1)S(1)}, u32[]{:S(2)}, u32[]{:S(2)}) collective-permute-start(bf16[1040,128]{1,0:T(8,128)(2,1)S(1)} %collective-permute-done.5.refs_6_), channel_id=1, source_target_pairs={{0,1},{1,0},{2,3},{3,2},{4,5},{5,4},{6,7},{7,6},{8,9},{9,8},{10,11... | collective-permute-start | bytes 798728 | tf_op jit(solution)/shard_map/ppermute | solution.py:142
  30.3 0.0 collective-permute-done.refs_1_
  30.3 0.0 copy-start.3
  30.3 0.0 collective-permute-done.2.refs_3_
  30.3 0.0 copy-start.4
  30.3 0.0 collective-permute-done.4.refs_5_
  30.3 0.0 copy-start.5
  30.3 6.4 %collective-permute-done.6.refs_7_ = bf16[1040,128]{1,0:T(8,128)(2,1)S(1)} collective-permute-done((bf16[1040,128]{1,0:T(8,128)(2,1)S(1)}, bf16[1040,128]{1,0:T(8,128)(2,1)S(1)}, u32[]{:S(2)}, u32[]{:S(2)}) %collective-permute-start.6) | collective-permute-done | bytes 266272 | tf_op jit(solution)/shard_map/ppermute | solution.py:142
  36.7 0.0 copy-done
  36.7 0.0 copy-done.1
  36.7 0.0 copy-done.2
  36.7 0.0 copy-done.3
  36.7 0.0 copy-done.4
  36.7 0.0 copy-done.5
  36.7 0.0 copy-start.6
  36.8 0.7 %copy-done.6 = bf16[1040,128]{1,0:T(8,128)(2,1)} copy-done((bf16[1040,128]{1,0:T(8,128)(2,1)}, bf16[1040,128]{1,0:T(8,128)(2,1)S(1)}, u32[]{:S(2)}) %copy-start.6) | copy-done | bytes 266264
  37.5 6.0 %context.1 = bf16[128,4096]{1,0:T(8,128)(2,1)} custom-call(s32[1]{0:T(128)S(6)} %copy.8.live_ref, bf16[128,4096]{1,0:T(8,128)(2,1)} %q_ref.2, bf16[1040,128]{1,0:T(8,128)(2,1)} %pack.1.refs_0_, bf16[1040,128]{1,0:T(8,128)(2,1)} %copy-done.3, bf16[1040,128]{1,0:T(8,128)(2,1)} %copy-done, bf16[1040,128]{1,0:T(8,128)(2,1)} %copy-done.4, ...), custom_call_target="tpu_custom_call" | custom-call | tf_op jit(solution)/shard_map/context/pallas_call | solution.py:89
  43.4 6.5 %query.1 = bf16[32,4096]{1,0:T(8,128)(2,1)} custom-call(bf16[32,4096]{1,0:T(8,128)(2,1)} %q_ref.3, bf16[1040,128]{1,0:T(8,128)(2,1)} %pack.1.refs_0_, bf16[1040,128]{1,0:T(8,128)(2,1)} %copy-done.3, bf16[1040,128]{1,0:T(8,128)(2,1)} %copy-done, bf16[1040,128]{1,0:T(8,128)(2,1)} %copy-done.4, bf16[1040,128]{1,0:T(8,128)(2,1)} %copy-done.1, ...), custom_call_target="tpu_custom_call" | custom-call | tf_op jit(solution)/shard_map/query/pallas_call | solution.py:131
Async XLA Ops:
  3.0 11.9 %collective-permute-start.1 = (bf16[1040,128]{1,0:T(8,128)(2,1)}, bf16[1040,128]{1,0:T(8,128)(2,1)S(1)}, u32[]{:S(2)}, u32[]{:S(2)}) collective-permute-start(bf16[1040,128]{1,0:T(8,128)(2,1)} %pack.1.refs_0_), channel_id=1, source_target_pairs={{0,2},{1,3},{2,0},{3,1},{4,6},{5,7},{6,4},{7,5},{8,10},{9,11},{10,... | collective-permute-start | bytes 798728 | tf_op jit(solution)/shard_map/ppermute | solution.py:142
  4.6 18.9 %collective-permute-start.3 = (bf16[1040,128]{1,0:T(8,128)(2,1)}, bf16[1040,128]{1,0:T(8,128)(2,1)S(1)}, u32[]{:S(2)}, u32[]{:S(2)}) collective-permute-start(bf16[1040,128]{1,0:T(8,128)(2,1)} %pack.1.refs_0_), channel_id=1, source_target_pairs={{0,4},{1,5},{2,6},{3,7},{4,0},{5,1},{6,2},{7,3},{8,12},{9,13},{10,... | collective-permute-start | bytes 798728 | tf_op jit(solution)/shard_map/ppermute | solution.py:142
  4.9 24.8 %collective-permute-start.5 = (bf16[1040,128]{1,0:T(8,128)(2,1)}, bf16[1040,128]{1,0:T(8,128)(2,1)S(1)}, u32[]{:S(2)}, u32[]{:S(2)}) collective-permute-start(bf16[1040,128]{1,0:T(8,128)(2,1)} %pack.1.refs_0_), channel_id=1, source_target_pairs={{0,6},{1,7},{2,4},{3,5},{4,2},{5,3},{6,0},{7,1},{8,14},{9,15},{10,... | collective-permute-start | bytes 798728 | tf_op jit(solution)/shard_map/ppermute | solution.py:142
  6.5 23.7 %collective-permute-start = (bf16[1040,128]{1,0:T(8,128)(2,1)}, bf16[1040,128]{1,0:T(8,128)(2,1)S(1)}, u32[]{:S(2)}, u32[]{:S(2)}) collective-permute-start(bf16[1040,128]{1,0:T(8,128)(2,1)} %pack.1.refs_0_), channel_id=1, source_target_pairs={{0,1},{1,0},{2,3},{3,2},{4,5},{5,4},{6,7},{7,6},{8,9},{9,8},{10,11... | collective-permute-start | bytes 798728 | tf_op jit(solution)/shard_map/ppermute | solution.py:142
  14.9 21.8 %copy-start = (bf16[1040,128]{1,0:T(8,128)(2,1)}, bf16[1040,128]{1,0:T(8,128)(2,1)S(1)}, u32[]{:S(2)}) copy-start(bf16[1040,128]{1,0:T(8,128)(2,1)S(1)} %collective-permute-done.1.refs_2_) | copy-start | bytes 798724
  14.9 15.3 %collective-permute-start.2 = (bf16[1040,128]{1,0:T(8,128)(2,1)S(1)}, bf16[1040,128]{1,0:T(8,128)(2,1)S(1)}, u32[]{:S(2)}, u32[]{:S(2)}) collective-permute-start(bf16[1040,128]{1,0:T(8,128)(2,1)S(1)} %collective-permute-done.1.refs_2_), channel_id=1, source_target_pairs={{0,1},{1,0},{2,3},{3,2},{4,5},{5,4},{6,7},{7,6},{8,9},{9,8},{10,11... | collective-permute-start | bytes 798728 | tf_op jit(solution)/shard_map/ppermute | solution.py:142
  23.5 13.2 %copy-start.1 = (bf16[1040,128]{1,0:T(8,128)(2,1)}, bf16[1040,128]{1,0:T(8,128)(2,1)S(1)}, u32[]{:S(2)}) copy-start(bf16[1040,128]{1,0:T(8,128)(2,1)S(1)} %collective-permute-done.3.refs_4_) | copy-start | bytes 798724
  23.5 6.8 %collective-permute-start.4 = (bf16[1040,128]{1,0:T(8,128)(2,1)S(1)}, bf16[1040,128]{1,0:T(8,128)(2,1)S(1)}, u32[]{:S(2)}, u32[]{:S(2)}) collective-permute-start(bf16[1040,128]{1,0:T(8,128)(2,1)S(1)} %collective-permute-done.3.refs_4_), channel_id=1, source_target_pairs={{0,1},{1,0},{2,3},{3,2},{4,5},{5,4},{6,7},{7,6},{8,9},{9,8},{10,11... | collective-permute-start | bytes 798728 | tf_op jit(solution)/shard_map/ppermute | solution.py:142
  29.7 7.0 %copy-start.2 = (bf16[1040,128]{1,0:T(8,128)(2,1)}, bf16[1040,128]{1,0:T(8,128)(2,1)S(1)}, u32[]{:S(2)}) copy-start(bf16[1040,128]{1,0:T(8,128)(2,1)S(1)} %collective-permute-done.5.refs_6_) | copy-start | bytes 798724
  29.7 7.0 %collective-permute-start.6 = (bf16[1040,128]{1,0:T(8,128)(2,1)S(1)}, bf16[1040,128]{1,0:T(8,128)(2,1)S(1)}, u32[]{:S(2)}, u32[]{:S(2)}) collective-permute-start(bf16[1040,128]{1,0:T(8,128)(2,1)S(1)} %collective-permute-done.5.refs_6_), channel_id=1, source_target_pairs={{0,1},{1,0},{2,3},{3,2},{4,5},{5,4},{6,7},{7,6},{8,9},{9,8},{10,11... | collective-permute-start | bytes 798728 | tf_op jit(solution)/shard_map/ppermute | solution.py:142
  30.3 6.5 %copy-start.3 = (bf16[1040,128]{1,0:T(8,128)(2,1)}, bf16[1040,128]{1,0:T(8,128)(2,1)S(1)}, u32[]{:S(2)}) copy-start(bf16[1040,128]{1,0:T(8,128)(2,1)S(1)} %collective-permute-done.refs_1_) | copy-start | bytes 798724
  30.3 6.5 %copy-start.4 = (bf16[1040,128]{1,0:T(8,128)(2,1)}, bf16[1040,128]{1,0:T(8,128)(2,1)S(1)}, u32[]{:S(2)}) copy-start(bf16[1040,128]{1,0:T(8,128)(2,1)S(1)} %collective-permute-done.2.refs_3_) | copy-start | bytes 798724
  30.3 6.5 %copy-start.5 = (bf16[1040,128]{1,0:T(8,128)(2,1)}, bf16[1040,128]{1,0:T(8,128)(2,1)S(1)}, u32[]{:S(2)}) copy-start(bf16[1040,128]{1,0:T(8,128)(2,1)S(1)} %collective-permute-done.4.refs_5_) | copy-start | bytes 798724
  36.7 0.7 %copy-start.6 = (bf16[1040,128]{1,0:T(8,128)(2,1)}, bf16[1040,128]{1,0:T(8,128)(2,1)S(1)}, u32[]{:S(2)}) copy-start(bf16[1040,128]{1,0:T(8,128)(2,1)S(1)} %collective-permute-done.6.refs_7_) | copy-start | bytes 798724

commit v2 on v1

v2 whole, which is shorter than its diff:
```python
import functools
import math

import jax
import jax.numpy as jnp
from jax import lax
from jax.experimental import pallas as pl
from jax.experimental.pallas import tpu as pltpu
from jax.sharding import PartitionSpec as P

HEAD = 128
FLAG_ROWS = 16
HIDDEN = -1e30
SCALE = HEAD**-0.5 / math.log(2.0)
NT = (((1,), (1,)), ((), ()))
F32 = jnp.float32
BF16 = jnp.bfloat16
LIMIT = pltpu.CompilerParams(vmem_limit_bytes=24 * 1024 * 1024)


def whole():
    return pl.BlockSpec(memory_space=pltpu.VMEM)


def scalar():
    return pl.BlockSpec(memory_space=pltpu.SMEM)


def anywhere():
    return pl.BlockSpec(memory_space=pl.ANY)


def transposed_flags(ref, groups, rows):
    at = 2 * groups * rows
    flags = ref[at : at + FLAG_ROWS, :].astype(F32)[:1]
    return jnp.transpose(jnp.broadcast_to(flags, (rows, rows)))


def pack_kernel(live_ref, mask_ref, k_ref, v_ref, o_ref):
    rows, width = k_ref.shape
    groups = width // HEAD
    block = lax.axis_index("ctx")
    for g in range(groups):
        o_ref[g * rows : (g + 1) * rows, :] = k_ref[:, g * HEAD : (g + 1) * HEAD]
        o_ref[(groups + g) * rows : (groups + g + 1) * rows, :] = jnp.transpose(v_ref[:, g * HEAD : (g + 1) * HEAD])
    token = lax.broadcasted_iota(jnp.int32, (1, rows), 1)
    valid = ((mask_ref[...] != 0) | ((block == 0) & (token == 0))) & (block < live_ref[0])
    flags = jnp.where(valid, 1.0, 0.0).astype(BF16)
    o_ref[2 * groups * rows :, :] = jnp.broadcast_to(flags, (FLAG_ROWS, rows))


def pack(live_blocks, token_mask, k, v):
    rows, width = k.shape
    return pl.pallas_call(
        pack_kernel,
        out_shape=jax.ShapeDtypeStruct((2 * rows * width // HEAD + FLAG_ROWS, HEAD), BF16),
        in_specs=[scalar(), whole(), whole(), whole()],
        out_specs=whole(),
        compiler_params=LIMIT,
        name="pack",
    )(live_blocks, token_mask.reshape(1, rows), k, v)


def attend(ref, g, groups, rows, q, seen):
    s = lax.dot_general(ref[g * rows : (g + 1) * rows, :], q, NT, preferred_element_type=F32)
    s = jnp.where(seen, s, HIDDEN)
    m = jnp.max(s, axis=0, keepdims=True)
    p = jnp.exp2((s - m) * SCALE)
    l = jnp.sum(p, axis=0, keepdims=True)
    v = ref[(groups + g) * rows : (groups + g + 1) * rows, :]
    return m, l, jnp.dot(v, p.astype(BF16), preferred_element_type=F32)


def merge(one, two):
    top = jnp.maximum(one[0], two[0])
    f, h = jnp.exp2((one[0] - top) * SCALE), jnp.exp2((two[0] - top) * SCALE)
    return top, one[1] * f + two[1] * h, one[2] * f + two[2] * h


def seen_by_all(ref, groups, rows, lanes):
    flags = transposed_flags(ref, groups, rows)
    while flags.shape[1] < lanes:
        flags = jnp.concatenate([flags, flags], 1)
    return flags[:, :lanes] > 0.5


def load_state(acc_ref, stat_ref, g):
    return stat_ref[2 * g : 2 * g + 1, :], stat_ref[2 * g + 1 : 2 * g + 2, :], acc_ref[g * HEAD : (g + 1) * HEAD, :]


def store_state(acc_ref, stat_ref, g, state):
    stat_ref[2 * g : 2 * g + 1, :] = state[0]
    stat_ref[2 * g + 1 : 2 * g + 2, :] = state[1]
    acc_ref[g * HEAD : (g + 1) * HEAD, :] = state[2]


def first_kernel(groups, rows, q_ref, piece, stacked, acc, stat):
    n_q, width = q_ref.shape
    heads = width // HEAD // groups
    lanes = heads * n_q
    seen = seen_by_all(piece, groups, rows, lanes)
    for g in range(groups):
        q = jnp.concatenate(
            [q_ref[:, (g * heads + h) * HEAD : (g * heads + h + 1) * HEAD].astype(F32) for h in range(heads)], 0
        ).astype(BF16)
        stacked[g * lanes : (g + 1) * lanes, :] = q
        store_state(acc, stat, g, attend(piece, g, groups, rows, q, seen))


def state_shapes(groups, lanes):
    return [
        jax.ShapeDtypeStruct((groups * HEAD, lanes), F32),
        jax.ShapeDtypeStruct((2 * groups, lanes), F32),
    ]


def query_first(q, piece, groups, rows):
    n_q, width = q.shape
    lanes = n_q * width // HEAD // groups
    return pl.pallas_call(
        functools.partial(first_kernel, groups, rows),
        out_shape=[jax.ShapeDtypeStruct((groups * lanes, HEAD), BF16)] + state_shapes(groups, lanes),
        in_specs=[whole()] * 2,
        out_specs=[whole()] * 3,
        compiler_params=LIMIT,
        name="query_first",
    )(q, piece)


def more_kernel(groups, rows, count, stacked, acc_in, stat_in, *refs):
    pieces, (acc, stat) = refs[:count], refs[count:]
    lanes = stacked.shape[0] // groups
    seen = [seen_by_all(piece, groups, rows, lanes) for piece in pieces]
    for g in range(groups):
        q = stacked[g * lanes : (g + 1) * lanes, :]
        state = load_state(acc_in, stat_in, g)
        for piece, mask in zip(pieces, seen):
            state = merge(state, attend(piece, g, groups, rows, q, mask))
        store_state(acc, stat, g, state)


def query_more(stacked, acc, stat, pieces, groups, rows):
    return pl.pallas_call(
        functools.partial(more_kernel, groups, rows, len(pieces)),
        out_shape=state_shapes(groups, stacked.shape[0] // groups),
        in_specs=[whole()] * (3 + len(pieces)),
        out_specs=[whole()] * 2,
        input_output_aliases={1: 0, 2: 1},
        compiler_params=LIMIT,
        name="query_more",
    )(stacked, acc, stat, *pieces)


def last_kernel(groups, rows, count, stacked, acc_in, stat_in, *refs):
    pieces, o_ref = refs[:count], refs[count]
    lanes = stacked.shape[0] // groups
    n_q, width = o_ref.shape
    heads = width // HEAD // groups
    seen = [seen_by_all(piece, groups, rows, lanes) for piece in pieces]
    for g in range(groups):
        q = stacked[g * lanes : (g + 1) * lanes, :]
        state = load_state(acc_in, stat_in, g)
        for piece, mask in zip(pieces, seen):
            state = merge(state, attend(piece, g, groups, rows, q, mask))
        out = jnp.transpose(state[2] / state[1])
        for h in range(heads):
            o_ref[:, (g * heads + h) * HEAD : (g * heads + h + 1) * HEAD] = out[h * n_q : (h + 1) * n_q].astype(BF16)


def query_last(stacked, acc, stat, pieces, groups, rows, shape):
    return pl.pallas_call(
        functools.partial(last_kernel, groups, rows, len(pieces)),
        out_shape=shape,
        in_specs=[whole()] * (3 + len(pieces)),
        out_specs=whole(),
        compiler_params=LIMIT,
        name="query_last",
    )(stacked, acc, stat, *pieces)


def context_body(groups, rows, live_ref, q_ref, anchor, own, o_ref, q_buf, o_buf, in_sems, out_sems):
    block = lax.axis_index("ctx")
    share = q_ref.shape[1] // groups
    loads = [
        pltpu.make_async_copy(q_ref.at[:, pl.ds(g * share, share)], q_buf.at[:, pl.ds(g * share, share)], in_sems.at[g])
        for g in range(groups)
    ]
    stores = [
        pltpu.make_async_copy(o_buf.at[:, pl.ds(g * share, share)], o_ref.at[:, pl.ds(g * share, share)], out_sems.at[g])
        for g in range(groups)
    ]
    for load in loads:
        load.start()
    key = lax.broadcasted_iota(jnp.int32, (rows, rows), 0)
    row = lax.broadcasted_iota(jnp.int32, (rows, rows), 1)
    see_anchor = transposed_flags(anchor, groups, rows) * jnp.where(block > 0, 1.0, 0.0)
    see_own = jnp.where(key < row, transposed_flags(own, groups, rows), jnp.where(key == row, 1.0, 0.0))
    visible = jnp.concatenate([see_anchor, see_own], 0) > 0.5
    alive = jnp.where(block < live_ref[0], 1.0, 0.0)
    for g in range(groups):
        k_at = slice(g * rows, (g + 1) * rows)
        v_at = slice((groups + g) * rows, (groups + g + 1) * rows)
        keys = jnp.concatenate([anchor[k_at, :], own[k_at, :]], 0)
        values = jnp.concatenate([anchor[v_at, :], own[v_at, :]], 1)
        loads[g].wait()
        for h in range(share // HEAD):
            at = slice(g * share + h * HEAD, g * share + (h + 1) * HEAD)
            s = lax.dot_general(keys, q_buf[:, at], NT, preferred_element_type=F32)
            s = jnp.where(visible, s, HIDDEN)
            m = jnp.max(s, axis=0, keepdims=True)
            p = jnp.exp2((s - m) * SCALE)
            l = jnp.sum(p, axis=0, keepdims=True)
            a = jnp.dot(values, p.astype(BF16), preferred_element_type=F32)
            o_buf[:, at] = jnp.transpose(a * (alive / l)).astype(BF16)
        stores[g].start()
    for store in stores:
        store.wait()


def context_kernel(groups, rows, blocks, aliased, live_ref, q_ref, own, *refs):
    count = len(blocks)
    pieces, rest = refs[:count], refs[count + aliased :]
    o_ref, anchor, q_buf, o_buf, in_sems, out_sems = rest
    block = lax.axis_index("ctx")
    for b, piece in zip(blocks, pieces):

        @pl.when(block == b)
        def _():
            anchor[...] = piece[...]

    mine = functools.reduce(jnp.logical_or, [block == b for b in blocks])

    @pl.when(mine)
    def _():
        context_body(groups, rows, live_ref, q_ref, anchor, own, o_ref, q_buf, o_buf, in_sems, out_sems)


def context(live_blocks, q, own, anchors, groups, before=None):
    rows, width = q.shape
    blocks, pieces = zip(*anchors)
    extra = [] if before is None else [before]
    return pl.pallas_call(
        functools.partial(context_kernel, groups, rows, blocks, len(extra)),
        out_shape=jax.ShapeDtypeStruct(q.shape, q.dtype),
        in_specs=[scalar(), anywhere()] + [whole()] * (1 + len(pieces)) + [anywhere()] * len(extra),
        out_specs=anywhere(),
        input_output_aliases={3 + len(pieces): 0} if extra else {},
        scratch_shapes=[
            pltpu.VMEM(own.shape, own.dtype),
            pltpu.VMEM(q.shape, q.dtype),
            pltpu.VMEM(q.shape, q.dtype),
            pltpu.SemaphoreType.DMA((groups,)),
            pltpu.SemaphoreType.DMA((groups,)),
        ],
        compiler_params=LIMIT,
        name="context",
    )(live_blocks, q, own, *pieces, *extra)


def local(context_q, context_k, context_v, question_q, token_mask, live_blocks):
    n = lax.axis_size("ctx")
    rows, width = context_k.shape
    groups = width // HEAD
    ring = list(range(0, n, 2)) + list(range(n - 1, 0, -2))
    forth = [(ring[i], ring[(i + 1) % n]) for i in range(n)]
    back = [(b, a) for a, b in forth]

    own = pack(live_blocks, token_mask, context_k, context_v)
    half = n // 2
    left = right = own
    anchors = [(ring[0], own)]
    arrived = []
    for step in range(1, half + 1):
        left = lax.ppermute(left, "ctx", forth)
        late = [(ring[step], left)]
        if step < half:
            right = lax.ppermute(right, "ctx", back)
            late.append((ring[n - step], right))
        if step == 1:
            state = query_first(question_q, own, groups, rows)
        else:
            state = [state[0], *query_more(*state, arrived, groups, rows)]
        if step == half:
            context_output = context(live_blocks, context_q, own, anchors, groups)
        else:
            left, right, state = lax.optimization_barrier((left, right, state))
            late = [(late[0][0], left), (late[1][0], right)]
            arrived = [left, right]
            anchors += late
    query_output = query_last(*state, [left], groups, rows, jax.ShapeDtypeStruct(question_q.shape, BF16))
    context_output = context(live_blocks, context_q, own, late, groups, context_output)
    return context_output, query_output


def solution(mesh):
    rows = P(("dp", "ctx"), None)
    return jax.shard_map(
        local,
        mesh=mesh,
        in_specs=(rows, rows, rows, rows, P(("dp", "ctx")), P("dp")),
        out_specs=(rows, rows),
        check_vma=False,
    )
```

time: 50.6 us -> 39.2 us (0.77)
  the two profiles are of different devices: /device:TPU:18 before, /device:TPU:0 now
where the time goes in v2:
time: 39.2 us; the launch traced here: 39 us
  waiting for transfers between devices  17.7 us (45%)
  Pallas kernels  8.89 us (23%)
  starting transfers between devices  8.62 us (22%)
  local copies, waits for them, and re-layouts  2.46 us (6%)
  between operations  1.35 us (3%)
    ppermute x4, waiting for transfers between devices, local(): left = lax.ppermute(left, 'ctx', forth)  13.2 us
    ppermute x4, starting transfers between devices, local(): left = lax.ppermute(left, 'ctx', forth)  7.72 us
    ppermute x3, waiting for transfers between devices, local(): right = lax.ppermute(right, 'ctx', back)  4.42 us
    pallas_call x2, Pallas kernels, context(): pl.pallas_call(functools.partial(context_kernel, groups, rows, blocks, le...  4.15 us
    pallas_call x3, Pallas kernels, query_more(): pl.pallas_call(functools.partial(more_kernel, groups, rows, len(pieces)),...  2.53 us
    unnamed x10, local copies, waits for them, and re-layouts  2.46 us
    pallas_call x1, Pallas kernels, query_last(): pl.pallas_call(functools.partial(last_kernel, groups, rows, len(pieces)),...  1.46 us
    ppermute x3, starting transfers between devices, local(): right = lax.ppermute(right, 'ctx', back)  0.9 us
  transfers between devices with their start and end apart: 7, of which 6 were waited for; matrix products, arithmetic and copies ran while one was open for 0% of the time, Pallas kernels for 19%

profile of v2, /device:TPU:0, one launch (start us, length us, event | category | flops | bytes accessed | tf_op | source)
XLA Modules:
  0.0 39.0 jit_solution(1423491206678109322)
XLA Ops:
  1.3 0.0 copy-start.4
  1.3 0.6 %copy-done.4 = s32[128]{0:T(128)S(1)} copy-done((s32[128]{0:T(128)S(1)}, s32[128]{0:T(128)}, u32[]{:S(2)}) %copy-start.4) | copy-done | bytes 536
  1.9 0.0 copy-start.2
  1.9 0.9 %copy-done.2 = bf16[128,512]{1,0:T(8,128)(2,1)S(1)} copy-done((bf16[128,512]{1,0:T(8,128)(2,1)S(1)}, bf16[128,512]{1,0:T(8,128)(2,1)}, u32[]{:S(2)}) %copy-start.2) | copy-done | bytes 131096
  2.8 0.0 copy-start.3
  2.8 0.9 %copy-done.3 = bf16[128,512]{1,0:T(8,128)(2,1)S(1)} copy-done((bf16[128,512]{1,0:T(8,128)(2,1)S(1)}, bf16[128,512]{1,0:T(8,128)(2,1)}, u32[]{:S(2)}) %copy-start.3) | copy-done | bytes 131096
  3.7 0.0 copy-start.1
  3.7 0.1 pack.1.piece.own.refs_0_
  3.8 3.1 %collective-permute-start = (bf16[1040,128]{1,0:T(8,128)(2,1)S(1)}, bf16[1040,128]{1,0:T(8,128)(2,1)S(1)}, u32[]{:S(2)}, u32[]{:S(2)}) collective-permute-start(bf16[1040,128]{1,0:T(8,128)(2,1)S(1)} %pack.1.piece.own.refs_0_), channel_id=1, source_target_pairs={{0,2},{2,4},{4,6},{6,7},{7,5},{5,3},{3,1},{1,0},{8,10},{10,12},{12... | collective-permute-start | bytes 798728 | tf_op jit(solution)/shard_map/ppermute | solution.py:274
  6.9 0.0 collective-permute-start.1
  6.9 0.0 copy-done.1
  6.9 0.7 %query_first.1 = (bf16[1024,128]{1,0:T(8,128)(2,1)S(1)}, f32[512,256]{1,0:T(8,128)S(1)}, f32[8,256]{1,0:T(8,128)S(1)}) custom-call(bf16[32,4096]{1,0:T(8,128)(2,1)S(1)} %copy-done.1, bf16[1040,128]{1,0:T(8,128)(2,1)S(1)} %pack.1.piece.own.refs_0_), custom_call_target="tpu_custom_call" | custom-call | tf_op jit(solution)/shard_map/query_first/pallas_call | solution.py:120
  7.6 5.6 %collective-permute-done.refs_0_.refs_1_ = bf16[1040,128]{1,0:T(8,128)(2,1)S(1)} collective-permute-done((bf16[1040,128]{1,0:T(8,128)(2,1)S(1)}, bf16[1040,128]{1,0:T(8,128)(2,1)S(1)}, u32[]{:S(2)}, u32[]{:S(2)}) %collective-permute-start) | collective-permute-done | bytes 266272 | tf_op jit(solution)/shard_map/ppermute | solution.py:274
  13.2 1.5 %collective-permute-done.1.refs_1_.refs_2_ = bf16[1040,128]{1,0:T(8,128)(2,1)S(1)} collective-permute-done((bf16[1040,128]{1,0:T(8,128)(2,1)S(1)}, bf16[1040,128]{1,0:T(8,128)(2,1)S(1)}, u32[]{:S(2)}, u32[]{:S(2)}) %collective-permute-start.1) | collective-permute-done | bytes 266272 | tf_op jit(solution)/shard_map/ppermute | solution.py:277
  14.8 0.0 copy-start
  14.8 1.6 %collective-permute-start.2 = (bf16[1040,128]{1,0:T(8,128)(2,1)S(1)}, bf16[1040,128]{1,0:T(8,128)(2,1)S(1)}, u32[]{:S(2)}, u32[]{:S(2)}) collective-permute-start(bf16[1040,128]{1,0:T(8,128)(2,1)S(1)} %collective-permute-done.refs_0_.refs_1_), channel_id=1, source_target_pairs={{0,2},{2,4},{4,6},{6,7},{7,5},{5,3},{3,1},{1,0},{8,10},{10,12},{12... | collective-permute-start | bytes 798728 | tf_op jit(solution)/shard_map/ppermute | solution.py:274
  16.3 0.4 %collective-permute-start.3 = (bf16[1040,128]{1,0:T(8,128)(2,1)S(1)}, bf16[1040,128]{1,0:T(8,128)(2,1)S(1)}, u32[]{:S(2)}, u32[]{:S(2)}) collective-permute-start(bf16[1040,128]{1,0:T(8,128)(2,1)S(1)} %collective-permute-done.1.refs_1_.refs_2_), channel_id=1, source_target_pairs={{2,0},{4,2},{6,4},{7,6},{5,7},{3,5},{1,3},{0,1},{10,8},{12,10},{14... | collective-permute-start | bytes 798728 | tf_op jit(solution)/shard_map/ppermute | solution.py:277
  16.8 0.8 %query_more.3 = (f32[512,256]{1,0:T(8,128)S(1)}, f32[8,256]{1,0:T(8,128)S(1)}) custom-call(bf16[1024,128]{1,0:T(8,128)(2,1)S(1)} %get-tuple-element.45.stacked, f32[512,256]{1,0:T(8,128)S(1)} %get-tuple-element.32.acc_in, f32[8,256]{1,0:T(8,128)S(1)} %get-tuple-element.33.stat_in, ...), custom_call_target="tpu_custom_call", output_to_operand_aliasing={{0}: (1, {}), {1}: (2, {})} | custom-call | tf_op jit(solution)/shard_map/query_more/pallas_call | solution.py:143
  17.6 4.1 %collective-permute-done.2.refs_0_.refs_3_ = bf16[1040,128]{1,0:T(8,128)(2,1)S(1)} collective-permute-done((bf16[1040,128]{1,0:T(8,128)(2,1)S(1)}, bf16[1040,128]{1,0:T(8,128)(2,1)S(1)}, u32[]{:S(2)}, u32[]{:S(2)}) %collective-permute-start.2) | collective-permute-done | bytes 266272 | tf_op jit(solution)/shard_map/ppermute | solution.py:274
  21.7 1.3 %collective-permute-done.3.refs_1_.refs_4_ = bf16[1040,128]{1,0:T(8,128)(2,1)S(1)} collective-permute-done((bf16[1040,128]{1,0:T(8,128)(2,1)S(1)}, bf16[1040,128]{1,0:T(8,128)(2,1)S(1)}, u32[]{:S(2)}, u32[]{:S(2)}) %collective-permute-start.3) | collective-permute-done | bytes 266272 | tf_op jit(solution)/shard_map/ppermute | solution.py:277
  23.0 1.6 %collective-permute-start.4 = (bf16[1040,128]{1,0:T(8,128)(2,1)S(1)}, bf16[1040,128]{1,0:T(8,128)(2,1)S(1)}, u32[]{:S(2)}, u32[]{:S(2)}) collective-permute-start(bf16[1040,128]{1,0:T(8,128)(2,1)S(1)} %collective-permute-done.2.refs_0_.refs_3_), channel_id=1, source_target_pairs={{0,2},{2,4},{4,6},{6,7},{7,5},{5,3},{3,1},{1,0},{8,10},{10,12},{12... | collective-permute-start | bytes 798728 | tf_op jit(solution)/shard_map/ppermute | solution.py:274
  24.6 0.4 %collective-permute-start.5 = (bf16[1040,128]{1,0:T(8,128)(2,1)S(1)}, bf16[1040,128]{1,0:T(8,128)(2,1)S(1)}, u32[]{:S(2)}, u32[]{:S(2)}) collective-permute-start(bf16[1040,128]{1,0:T(8,128)(2,1)S(1)} %collective-permute-done.3.refs_1_.refs_4_), channel_id=1, source_target_pairs={{2,0},{4,2},{6,4},{7,6},{5,7},{3,5},{1,3},{0,1},{10,8},{12,10},{14... | collective-permute-start | bytes 798728 | tf_op jit(solution)/shard_map/ppermute | solution.py:277
  25.0 0.8 %query_more.4 = (f32[512,256]{1,0:T(8,128)S(1)}, f32[8,256]{1,0:T(8,128)S(1)}) custom-call(bf16[1024,128]{1,0:T(8,128)(2,1)S(1)} %get-tuple-element.45.stacked, f32[512,256]{1,0:T(8,128)S(1)} %get-tuple-element.39.acc_in, f32[8,256]{1,0:T(8,128)S(1)} %get-tuple-element.40.stat_in, ...), custom_call_target="tpu_custom_call", output_to_operand_aliasing={{0}: (1, {}), {1}: (2, {})} | custom-call | tf_op jit(solution)/shard_map/query_more/pallas_call | solution.py:143
  25.9 3.5 %collective-permute-done.4.refs_5_.refs_0_ = bf16[1040,128]{1,0:T(8,128)(2,1)S(1)} collective-permute-done((bf16[1040,128]{1,0:T(8,128)(2,1)S(1)}, bf16[1040,128]{1,0:T(8,128)(2,1)S(1)}, u32[]{:S(2)}, u32[]{:S(2)}) %collective-permute-start.4) | collective-permute-done | bytes 266272 | tf_op jit(solution)/shard_map/ppermute | solution.py:274
  29.4 1.6 %collective-permute-done.5.refs_6_.refs_1_ = bf16[1040,128]{1,0:T(8,128)(2,1)S(1)} collective-permute-done((bf16[1040,128]{1,0:T(8,128)(2,1)S(1)}, bf16[1040,128]{1,0:T(8,128)(2,1)S(1)}, u32[]{:S(2)}, u32[]{:S(2)}) %collective-permute-start.5) | collective-permute-done | bytes 266272 | tf_op jit(solution)/shard_map/ppermute | solution.py:277
  31.0 1.5 %collective-permute-start.6 = (bf16[1040,128]{1,0:T(8,128)(2,1)S(1)}, bf16[1040,128]{1,0:T(8,128)(2,1)S(1)}, u32[]{:S(2)}, u32[]{:S(2)}) collective-permute-start(bf16[1040,128]{1,0:T(8,128)(2,1)S(1)} %collective-permute-done.4.refs_5_.refs_0_), channel_id=1, source_target_pairs={{0,2},{2,4},{4,6},{6,7},{7,5},{5,3},{3,1},{1,0},{8,10},{10,12},{12... | collective-permute-start | bytes 798728 | tf_op jit(solution)/shard_map/ppermute | solution.py:274
  32.5 0.0 copy-done
  32.5 4.1 %context.2.refs_1_ = bf16[128,4096]{1,0:T(8,128)(2,1)} custom-call(s32[1]{0:T(128)S(6)} %copy.22.live_ref, bf16[128,4096]{1,0:T(8,128)(2,1)S(1)} %copy-done, bf16[1040,128]{1,0:T(8,128)(2,1)S(1)} %pack.1.piece.own.refs_0_, bf16[1040,128]{1,0:T(8,128)(2,1)S(1)} %pack.1.piece.own.refs_0_, bf16[1040,128]{1,0:T(8,128)(2,1)S(1)} %collective-permute-done.refs_0_.refs_1_, ...), custom_call_target="tpu_custom_call" | custom-call | tf_op jit(solution)/shard_map/context/pallas_call | solution.py:242
  36.6 0.8 %query_more.5 = (f32[512,256]{1,0:T(8,128)S(1)}, f32[8,256]{1,0:T(8,128)S(1)}) custom-call(bf16[1024,128]{1,0:T(8,128)(2,1)S(1)} %get-tuple-element.45.stacked, f32[512,256]{1,0:T(8,128)S(1)} %get-tuple-element.46.acc_in, f32[8,256]{1,0:T(8,128)S(1)} %get-tuple-element.47.stat_in, ...), custom_call_target="tpu_custom_call", output_to_operand_aliasing={{0}: (1, {}), {1}: (2, {})} | custom-call | tf_op jit(solution)/shard_map/query_more/pallas_call | solution.py:143
  37.4 0.0 collective-permute-done.6.refs_0_
  37.4 0.1 context.3
  37.5 1.5 %query_last.1 = bf16[32,4096]{1,0:T(8,128)(2,1)} custom-call(bf16[1024,128]{1,0:T(8,128)(2,1)S(1)} %get-tuple-element.45.stacked, f32[512,256]{1,0:T(8,128)S(1)} %get-tuple-element.48.acc_in, f32[8,256]{1,0:T(8,128)S(1)} %get-tuple-element.49.stat_in, bf16[1040,128]{1,0:T(8,128)(2,1)S(1)} %collective-permute-done.6.refs_0_), custom_call_target="tpu_custom_call" | custom-call | tf_op jit(solution)/shard_map/query_last/pallas_call | solution.py:171
Async XLA Ops:
  1.3 0.7 %copy-start.4 = (s32[128]{0:T(128)S(1)}, s32[128]{0:T(128)}, u32[]{:S(2)}) copy-start(s32[128]{0:T(128)} %param.10) | copy-start | bytes 1540
  1.9 0.9 %copy-start.2 = (bf16[128,512]{1,0:T(8,128)(2,1)S(1)}, bf16[128,512]{1,0:T(8,128)(2,1)}, u32[]{:S(2)}) copy-start(bf16[128,512]{1,0:T(8,128)(2,1)} %k_ref.1) | copy-start | bytes 393220
  2.8 0.9 %copy-start.3 = (bf16[128,512]{1,0:T(8,128)(2,1)S(1)}, bf16[128,512]{1,0:T(8,128)(2,1)}, u32[]{:S(2)}) copy-start(bf16[128,512]{1,0:T(8,128)(2,1)} %v_ref.1) | copy-start | bytes 393220
  3.7 3.2 %copy-start.1 = (bf16[32,4096]{1,0:T(8,128)(2,1)S(1)}, bf16[32,4096]{1,0:T(8,128)(2,1)}, u32[]{:S(2)}) copy-start(bf16[32,4096]{1,0:T(8,128)(2,1)} %q_ref.3) | copy-start | bytes 786436
  3.8 9.4 %collective-permute-start = (bf16[1040,128]{1,0:T(8,128)(2,1)S(1)}, bf16[1040,128]{1,0:T(8,128)(2,1)S(1)}, u32[]{:S(2)}, u32[]{:S(2)}) collective-permute-start(bf16[1040,128]{1,0:T(8,128)(2,1)S(1)} %pack.1.piece.own.refs_0_), channel_id=1, source_target_pairs={{0,2},{2,4},{4,6},{6,7},{7,5},{5,3},{3,1},{1,0},{8,10},{10,12},{12... | collective-permute-start | bytes 798728 | tf_op jit(solution)/shard_map/ppermute | solution.py:274
  6.9 7.9 %collective-permute-start.1 = (bf16[1040,128]{1,0:T(8,128)(2,1)S(1)}, bf16[1040,128]{1,0:T(8,128)(2,1)S(1)}, u32[]{:S(2)}, u32[]{:S(2)}) collective-permute-start(bf16[1040,128]{1,0:T(8,128)(2,1)S(1)} %pack.1.piece.own.refs_0_), channel_id=1, source_target_pairs={{2,0},{4,2},{6,4},{7,6},{5,7},{3,5},{1,3},{0,1},{10,8},{12,10},{14... | collective-permute-start | bytes 798728 | tf_op jit(solution)/shard_map/ppermute | solution.py:277
  14.8 17.7 %copy-start = (bf16[128,4096]{1,0:T(8,128)(2,1)S(1)}, bf16[128,4096]{1,0:T(8,128)(2,1)}, u32[]{:S(2)}) copy-start(bf16[128,4096]{1,0:T(8,128)(2,1)} %q_ref.5) | copy-start | bytes 3145732
  14.8 6.9 %collective-permute-start.2 = (bf16[1040,128]{1,0:T(8,128)(2,1)S(1)}, bf16[1040,128]{1,0:T(8,128)(2,1)S(1)}, u32[]{:S(2)}, u32[]{:S(2)}) collective-permute-start(bf16[1040,128]{1,0:T(8,128)(2,1)S(1)} %collective-permute-done.refs_0_.refs_1_), channel_id=1, source_target_pairs={{0,2},{2,4},{4,6},{6,7},{7,5},{5,3},{3,1},{1,0},{8,10},{10,12},{12... | collective-permute-start | bytes 798728 | tf_op jit(solution)/shard_map/ppermute | solution.py:274
  16.3 6.7 %collective-permute-start.3 = (bf16[1040,128]{1,0:T(8,128)(2,1)S(1)}, bf16[1040,128]{1,0:T(8,128)(2,1)S(1)}, u32[]{:S(2)}, u32[]{:S(2)}) collective-permute-start(bf16[1040,128]{1,0:T(8,128)(2,1)S(1)} %collective-permute-done.1.refs_1_.refs_2_), channel_id=1, source_target_pairs={{2,0},{4,2},{6,4},{7,6},{5,7},{3,5},{1,3},{0,1},{10,8},{12,10},{14... | collective-permute-start | bytes 798728 | tf_op jit(solution)/shard_map/ppermute | solution.py:277
  23.0 6.4 %collective-permute-start.4 = (bf16[1040,128]{1,0:T(8,128)(2,1)S(1)}, bf16[1040,128]{1,0:T(8,128)(2,1)S(1)}, u32[]{:S(2)}, u32[]{:S(2)}) collective-permute-start(bf16[1040,128]{1,0:T(8,128)(2,1)S(1)} %collective-permute-done.2.refs_0_.refs_3_), channel_id=1, source_target_pairs={{0,2},{2,4},{4,6},{6,7},{7,5},{5,3},{3,1},{1,0},{8,10},{10,12},{12... | collective-permute-start | bytes 798728 | tf_op jit(solution)/shard_map/ppermute | solution.py:274
  24.6 6.4 %collective-permute-start.5 = (bf16[1040,128]{1,0:T(8,128)(2,1)S(1)}, bf16[1040,128]{1,0:T(8,128)(2,1)S(1)}, u32[]{:S(2)}, u32[]{:S(2)}) collective-permute-start(bf16[1040,128]{1,0:T(8,128)(2,1)S(1)} %collective-permute-done.3.refs_1_.refs_4_), channel_id=1, source_target_pairs={{2,0},{4,2},{6,4},{7,6},{5,7},{3,5},{1,3},{0,1},{10,8},{12,10},{14... | collective-permute-start | bytes 798728 | tf_op jit(solution)/shard_map/ppermute | solution.py:277
  31.0 6.4 %collective-permute-start.6 = (bf16[1040,128]{1,0:T(8,128)(2,1)S(1)}, bf16[1040,128]{1,0:T(8,128)(2,1)S(1)}, u32[]{:S(2)}, u32[]{:S(2)}) collective-permute-start(bf16[1040,128]{1,0:T(8,128)(2,1)S(1)} %collective-permute-done.4.refs_5_.refs_0_), channel_id=1, source_target_pairs={{0,2},{2,4},{4,6},{6,7},{7,5},{5,3},{3,1},{1,0},{8,10},{10,12},{12... | collective-permute-start | bytes 798728 | tf_op jit(solution)/shard_map/ppermute | solution.py:274

commit v3 on v2

v3 whole, which is shorter than its diff:
```python
import functools
import math

import jax
import jax.numpy as jnp
from jax import lax
from jax.experimental import pallas as pl
from jax.experimental.pallas import tpu as pltpu
from jax.sharding import PartitionSpec as P

HEAD = 128
FLAG_ROWS = 16
HIDDEN = -1e30
SCALE = HEAD**-0.5 / math.log(2.0)
NT = (((1,), (1,)), ((), ()))
F32 = jnp.float32
BF16 = jnp.bfloat16
LIMIT = pltpu.CompilerParams(vmem_limit_bytes=24 * 1024 * 1024)


def whole():
    return pl.BlockSpec(memory_space=pltpu.VMEM)


class Block:
    def __init__(self, refs, groups, rows):
        self.groups, self.rows = groups, rows
        self.k_ref, self.v_ref = refs[0], refs[-1]
        self.v_base = key_rows(groups, rows) if len(refs) == 1 else 0

    def keys(self, g):
        return self.k_ref[g * self.rows : (g + 1) * self.rows, :]

    def values(self, g):
        at = self.v_base + g * self.rows
        return jnp.transpose(self.v_ref[at : at + self.rows, :])

    def flag_rows(self):
        at = self.groups * self.rows
        return self.k_ref[at : at + FLAG_ROWS, :].astype(F32)

    def flags(self):
        return jnp.transpose(jnp.broadcast_to(self.flag_rows()[:1], (self.rows, self.rows)))

    def alive(self):
        return self.flag_rows()[FLAG_ROWS // 2 : FLAG_ROWS // 2 + 1]

    def seen(self, lanes):
        flags = self.flags()
        while flags.shape[1] < lanes:
            flags = jnp.concatenate([flags, flags], 1)
        return flags[:, :lanes] > 0.5


def outside():
    return pl.BlockSpec(memory_space=pltpu.HBM)


def key_rows(groups, rows):
    return groups * rows + FLAG_ROWS


def take(refs, parts, groups, rows):
    blocks, at = [], 0
    for count in parts:
        blocks.append(Block(refs[at : at + count], groups, rows))
        at += count
    return blocks, refs[at:]


def pack(live_blocks, token_mask, k, v):
    rows, width = k.shape
    groups = width // HEAD
    block = lax.axis_index("ctx")
    token = lax.broadcasted_iota(jnp.int32, (FLAG_ROWS, rows), 1)
    row = lax.broadcasted_iota(jnp.int32, (FLAG_ROWS, rows), 0)
    valid = (token_mask[None, :] != 0) | ((block == 0) & (token == 0)) | (row >= FLAG_ROWS // 2)
    flags = (valid & (block < live_blocks[0])).astype(BF16)

    def by_head(x):
        return x.reshape(rows, groups, HEAD).transpose(1, 0, 2).reshape(groups * rows, HEAD)

    return jnp.concatenate([by_head(k), flags, by_head(v)], 0)


def attend(block, g, q, seen):
    s = lax.dot_general(block.keys(g), q, NT, preferred_element_type=F32)
    s = jnp.where(seen, s, HIDDEN)
    m = jnp.max(s, axis=0, keepdims=True)
    p = jnp.exp2((s - m) * SCALE)
    l = jnp.sum(p, axis=0, keepdims=True)
    return m, l, jnp.dot(block.values(g), p.astype(BF16), preferred_element_type=F32)


def merge(one, two):
    top = jnp.maximum(one[0], two[0])
    f, h = jnp.exp2((one[0] - top) * SCALE), jnp.exp2((two[0] - top) * SCALE)
    return top, one[1] * f + two[1] * h, one[2] * f + two[2] * h


def load_state(acc_ref, stat_ref, g):
    return stat_ref[2 * g : 2 * g + 1, :], stat_ref[2 * g + 1 : 2 * g + 2, :], acc_ref[g * HEAD : (g + 1) * HEAD, :]


def store_state(acc_ref, stat_ref, g, state):
    stat_ref[2 * g : 2 * g + 1, :] = state[0]
    stat_ref[2 * g + 1 : 2 * g + 2, :] = state[1]
    acc_ref[g * HEAD : (g + 1) * HEAD, :] = state[2]


def first_kernel(groups, rows, q_ref, piece, stacked, acc, stat):
    n_q, width = q_ref.shape
    heads = width // HEAD // groups
    lanes = heads * n_q
    block = Block([piece], groups, rows)
    seen = block.seen(lanes)
    for g in range(groups):
        q = jnp.concatenate(
            [q_ref[:, (g * heads + h) * HEAD : (g * heads + h + 1) * HEAD].astype(F32) for h in range(heads)], 0
        ).astype(BF16)
        stacked[g * lanes : (g + 1) * lanes, :] = q
        store_state(acc, stat, g, attend(block, g, q, seen))


def state_shapes(groups, lanes):
    return [
        jax.ShapeDtypeStruct((groups * HEAD, lanes), F32),
        jax.ShapeDtypeStruct((2 * groups, lanes), F32),
    ]


def query_first(q, piece, groups, rows):
    n_q, width = q.shape
    lanes = n_q * width // HEAD // groups
    return pl.pallas_call(
        functools.partial(first_kernel, groups, rows),
        out_shape=[jax.ShapeDtypeStruct((groups * lanes, HEAD), BF16)] + state_shapes(groups, lanes),
        in_specs=[whole()] * 2,
        out_specs=[whole()] * 3,
        compiler_params=LIMIT,
        name="query_first",
    )(q, piece)


def more_kernel(groups, rows, parts, stacked, acc_in, stat_in, *refs):
    blocks, (acc, stat) = take(refs, parts, groups, rows)
    lanes = stacked.shape[0] // groups
    seen = [block.seen(lanes) for block in blocks]
    for g in range(groups):
        q = stacked[g * lanes : (g + 1) * lanes, :]
        state = load_state(acc_in, stat_in, g)
        for block, mask in zip(blocks, seen):
            state = merge(state, attend(block, g, q, mask))
        store_state(acc, stat, g, state)


def query_more(stacked, acc, stat, pieces, groups, rows):
    return pl.pallas_call(
        functools.partial(more_kernel, groups, rows, [len(piece) for piece in pieces]),
        out_shape=state_shapes(groups, stacked.shape[0] // groups),
        in_specs=[whole()] * (3 + sum(len(piece) for piece in pieces)),
        out_specs=[whole()] * 2,
        input_output_aliases={1: 0, 2: 1},
        compiler_params=LIMIT,
        name="query_more",
    )(stacked, acc, stat, *[part for piece in pieces for part in piece])


def context_body(groups, rows, resident, q_ref, anchor, own, o_ref, q_buf, o_buf, in_sems, out_sems):
    here = lax.axis_index("ctx")
    share = q_ref.shape[1] // groups
    spans = [pl.ds(g * share, share) for g in range(groups)]
    stores = [pltpu.make_async_copy(o_buf.at[:, at], o_ref.at[:, at], out_sems.at[g]) for g, at in enumerate(spans)]
    loads = []
    if not resident:
        loads = [pltpu.make_async_copy(q_ref.at[:, at], q_buf.at[:, at], in_sems.at[g]) for g, at in enumerate(spans)]
        q_ref = q_buf
    for load in loads:
        load.start()
    key = lax.broadcasted_iota(jnp.int32, (rows, rows), 0)
    row = lax.broadcasted_iota(jnp.int32, (rows, rows), 1)
    see_anchor = anchor.flags() * jnp.where(here > 0, 1.0, 0.0)
    see_own = jnp.where(key < row, own.flags(), jnp.where(key == row, 1.0, 0.0))
    visible = jnp.concatenate([see_anchor, see_own], 0) > 0.5
    alive = own.alive()
    for g in range(groups):
        keys = jnp.concatenate([anchor.keys(g), own.keys(g)], 0)
        values = jnp.concatenate([anchor.values(g), own.values(g)], 1)
        if loads:
            loads[g].wait()
        for h in range(share // HEAD):
            at = slice(g * share + h * HEAD, g * share + (h + 1) * HEAD)
            s = lax.dot_general(keys, q_ref[:, at], NT, preferred_element_type=F32)
            s = jnp.where(visible, s, HIDDEN)
            m = jnp.max(s, axis=0, keepdims=True)
            p = jnp.exp2((s - m) * SCALE)
            l = jnp.sum(p, axis=0, keepdims=True)
            a = jnp.dot(values, p.astype(BF16), preferred_element_type=F32)
            o_buf[:, at] = jnp.transpose(a * (alive / l)).astype(BF16)
        stores[g].start()
    for store in stores:
        store.wait()


def context_kernel(groups, rows, devices, parts, aliased, q_ref, own, *refs):
    blocks, rest = take(refs, parts, groups, rows)
    o_ref, anchor, *buffers = rest[aliased:]
    here = lax.axis_index("ctx")
    if len(blocks) == 1:
        first = blocks[0]
    else:
        first = Block([anchor], groups, rows)
        for device, block in zip(devices, blocks):

            @pl.when(here == device)
            def _():
                anchor[...] = block.k_ref[...]

    @pl.when(functools.reduce(jnp.logical_or, [here == device for device in devices]))
    def _():
        context_body(groups, rows, False, q_ref, first, Block([own], groups, rows), o_ref, *buffers)


def context(q, own, anchors, groups, before=None):
    rows, width = q.shape
    devices, pieces = zip(*anchors)
    parts = [len(piece) for piece in pieces]
    operands = [part for piece in pieces for part in piece]
    extra = [] if before is None else [before]
    return pl.pallas_call(
        functools.partial(context_kernel, groups, rows, devices, parts, len(extra)),
        out_shape=jax.ShapeDtypeStruct(q.shape, q.dtype),
        in_specs=[outside()] + [whole()] * (1 + len(operands)) + [outside()] * len(extra),
        out_specs=outside(),
        input_output_aliases={2 + len(operands): 0} if extra else {},
        scratch_shapes=[
            pltpu.VMEM(own.shape, own.dtype),
            pltpu.VMEM(q.shape, q.dtype),
            pltpu.VMEM(q.shape, q.dtype),
            pltpu.SemaphoreType.DMA((groups,)),
            pltpu.SemaphoreType.DMA((groups,)),
        ],
        compiler_params=LIMIT,
        name="context",
    )(q, own, *operands, *extra)


def finish_kernel(
    groups, rows, device, parts, stacked, acc, stat, q_ref, own, *refs
):
    (block,), rest = take(refs, parts, groups, rows)
    _, query_ref, context_ref, buffer, out_sems, *buffers = rest
    lanes = stacked.shape[0] // groups
    n_q, width = buffer.shape
    heads = width // HEAD // groups
    share = heads * HEAD
    spans = [pl.ds(g * share, share) for g in range(groups)]
    stores = [
        pltpu.make_async_copy(buffer.at[:, at], query_ref.at[:, at], out_sems.at[g]) for g, at in enumerate(spans)
    ]
    seen = block.seen(lanes)
    for g in range(groups):
        q = stacked[g * lanes : (g + 1) * lanes, :]
        _, total, part = merge(load_state(acc, stat, g), attend(block, g, q, seen))
        out = jnp.transpose(part / total)
        for h in range(heads):
            at = g * share + h * HEAD
            buffer[:, at : at + HEAD] = out[h * n_q : (h + 1) * n_q].astype(BF16)
        stores[g].start()

    @pl.when(lax.axis_index("ctx") == device)
    def _():
        context_body(groups, rows, True, q_ref, block, Block([own], groups, rows), context_ref, *buffers)

    for store in stores:
        store.wait()


def finish(stacked, acc, stat, q, own, last, groups, shape, before):
    rows, width = q.shape
    device, piece = last
    return pl.pallas_call(
        functools.partial(finish_kernel, groups, rows, device, [len(piece)]),
        out_shape=[shape, jax.ShapeDtypeStruct(q.shape, q.dtype)],
        in_specs=[whole()] * (5 + len(piece)) + [outside()],
        out_specs=[outside()] * 2,
        input_output_aliases={5 + len(piece): 1},
        scratch_shapes=[
            pltpu.VMEM(shape.shape, shape.dtype),
            pltpu.SemaphoreType.DMA((groups,)),
            pltpu.VMEM((FLAG_ROWS, HEAD), q.dtype),
            pltpu.VMEM(q.shape, q.dtype),
            pltpu.SemaphoreType.DMA((groups,)),
            pltpu.SemaphoreType.DMA((groups,)),
        ],
        compiler_params=LIMIT,
        name="finish",
    )(stacked, acc, stat, q, own, *piece, before)


def local(context_q, context_k, context_v, question_q, token_mask, live_blocks):
    n = lax.axis_size("ctx")
    rows, width = context_k.shape
    groups = width // HEAD
    ring = list(range(0, n, 2)) + list(range(n - 1, 0, -2))
    forth = [(ring[i], ring[(i + 1) % n]) for i in range(n)]
    back = [(b, a) for a, b in forth]

    own = pack(live_blocks, token_mask, context_k, context_v)
    half = n // 2
    split = key_rows(groups, rows)
    left = right = own
    arrived = [(ring[0], (own,))]
    context_output = state = None
    for step in range(1, half + 1):
        if step < half:
            left = lax.ppermute(left, "ctx", forth)
            right = lax.ppermute(right, "ctx", back)
        else:
            left = lax.ppermute(left[:split], "ctx", forth)
            right = lax.ppermute(right[split:], "ctx", back)
        pieces = [piece for _, piece in arrived]
        if state is None:
            state = query_first(question_q, own, groups, rows)
        else:
            state = [state[0], *query_more(*state, pieces, groups, rows)]
        context_output = context(context_q, own, arrived, groups, context_output)
        if step < half:
            left = lax.optimization_barrier((left, state, context_output))[0]
            right, state, context_output = lax.optimization_barrier((right, state, context_output))
            arrived = [(ring[step], (left,)), (ring[n - step], (right,))]
    query_output, context_output = finish(
        *state,
        context_q,
        own,
        (ring[half], (left, right)),
        groups,
        jax.ShapeDtypeStruct(question_q.shape, BF16),
        context_output,
    )
    return context_output, query_output


def solution(mesh):
    rows = P(("dp", "ctx"), None)
    return jax.shard_map(
        local,
        mesh=mesh,
        in_specs=(rows, rows, rows, rows, P(("dp", "ctx")), P("dp")),
        out_specs=(rows, rows),
        check_vma=False,
    )
```

time: 39.2 us -> 35.5 us (0.906)
  waiting for transfers between devices: 17.7 us -> 12.6 us
  other arithmetic: 0 us -> 0.77 us
  starting transfers between devices: 8.62 us -> 9.26 us
  local copies, waits for them, and re-layouts: 2.46 us -> 2.06 us
    ppermute x3, waiting for transfers between devices: 4.42 us -> 0.01 us  [local(): right = lax.ppermute(right, 'ctx', back)]
    ppermute x4 -> x3, waiting for transfers between devices: 13.2 us -> 8.92 us  [local(): left = lax.ppermute(left, 'ctx', forth)]
    ppermute x0 -> x2, waiting for transfers between devices: none -> 3.64 us  [the longest x1 3.63 us: local(): right = lax.ppermute(right[split:], 'ctx', back)]
    ppermute x0 -> x2, starting transfers between devices: none -> 2.13 us  [the longest x1 1.67 us: local(): left = lax.ppermute(left[:split], 'ctx', forth)]
    unnamed x10 -> x6, local copies, waits for them, and re-layouts: 2.46 us -> 1.08 us
    ppermute x4 -> x3, starting transfers between devices: 7.72 us -> 6.41 us  [local(): left = lax.ppermute(left, 'ctx', forth)]
    reshape x0 -> x2, local copies, waits for them, and re-layouts: none -> 0.95 us  [by_head(): x.reshape(rows, groups, HEAD).transpose(1, 0, 2)]
    or x0 -> x1, other arithmetic: none -> 0.67 us  [pack(): (token_mask[None, :] != 0) | (block == 0) & (token == 0)]
  transfers between devices with their start and end apart: 7 -> 8, of which waited for: 6 -> 4; matrix products, arithmetic and copies ran while one was open for 0% -> 0% of each run, Pallas kernels for 19% -> 21%
where the time goes in v3:
time: 35.5 us; the launch traced here: 35.3 us
  waiting for transfers between devices  12.6 us (35%)
  starting transfers between devices  9.26 us (26%)
  Pallas kernels  8.97 us (25%)
  local copies, waits for them, and re-layouts  2.06 us (6%)
  between operations  1.65 us (5%)
  other arithmetic  0.77 us (2%)
    ppermute x3, waiting for transfers between devices, local(): left = lax.ppermute(left, 'ctx', forth)  8.92 us
    ppermute x3, starting transfers between devices, local(): left = lax.ppermute(left, 'ctx', forth)  6.41 us
    pallas_call x4, Pallas kernels, context(): pl.pallas_call(functools.partial(context_kernel, groups, rows, devices, p...  4.28 us
    ppermute x1, waiting for transfers between devices, local(): right = lax.ppermute(right[split:], 'ctx', back)  3.63 us
    pallas_call x3, Pallas kernels, query_more(): pl.pallas_call(functools.partial(more_kernel, groups, rows, [len(piece) f...  2.54 us
    ppermute x1, starting transfers between devices, local(): left = lax.ppermute(left[:split], 'ctx', forth)  1.67 us
    pallas_call x1, Pallas kernels, finish(): pl.pallas_call(functools.partial(finish_kernel, groups, rows, device, [le...  1.49 us
    unnamed x6, local copies, waits for them, and re-layouts  1.08 us
  transfers between devices with their start and end apart: 8, of which 4 were waited for; matrix products, arithmetic and copies ran while one was open for 0% of the time, Pallas kernels for 21%

profile of v3, /device:TPU:0, one launch (start us, length us, event | category | flops | bytes accessed | tf_op | source)
XLA Modules:
  0.0 35.3 jit_solution(2747166165227245761)
XLA Ops:
  0.6 0.0 copy-start
  0.6 0.0 copy-start.1
  1.4 0.1 copy-done
  1.6 0.9 %copy_bitcast_fusion = bf16[128,4,128]{2,0,1:T(8,128)(2,1)S(1)} fusion(bf16[128,512]{1,0:T(8,128)(2,1)} %param.8), kind=kLoop, calls=%fused_computation.1 | loop fusion | bytes 262144 | tf_op jit(solution)/shard_map/reshape | solution.py:81
  2.5 0.7 %and_or_fusion = pred[128]{0:T(512)(128)(4,1)S(1)} fusion(s32[128]{0:T(128)} %param.10, pred[]{:T(512)S(6)} %eq.8), kind=kLoop, calls=%fused_computation.4 | loop fusion | flops 512 | bytes 641 | tf_op jit(solution)/shard_map/or | solution.py:77
  3.2 0.1 and_convert_fusion
  3.3 3.1 %collective-permute-start.2 = (bf16[1040,128]{1,0:T(8,128)(2,1)S(1)}, bf16[1040,128]{1,0:T(8,128)(2,1)S(1)}, u32[]{:S(2)}, u32[]{:S(2)}) collective-permute-start(bf16[1040,128]{1,0:T(8,128)(2,1)S(1)} %pad_maximum_fusion.piece.own.refs_0_), channel_id=1, source_target_pairs={{0,2},{2,4},{4,6},{6,7},{7,5},{5,3},{3,1},{1,0},{8,10},{10,12},{12... | collective-permute-start | bytes 798728 | tf_op jit(solution)/shard_map/ppermute | solution.py:317
  6.3 0.0 collective-permute-start
  6.3 0.0 copy-start.2
  6.4 0.9 %copy-done.2 = bf16[32,4096]{1,0:T(8,128)(2,1)S(1)} copy-done((bf16[32,4096]{1,0:T(8,128)(2,1)S(1)}, bf16[32,4096]{1,0:T(8,128)(2,1)}, u32[]{:S(2)}) %copy-start.2) | copy-done | bytes 262168
  7.3 0.7 %query_first.1 = (bf16[1024,128]{1,0:T(8,128)(2,1)S(1)}, f32[512,256]{1,0:T(8,128)S(1)}, f32[8,256]{1,0:T(8,128)S(1)}) custom-call(bf16[32,4096]{1,0:T(8,128)(2,1)S(1)} %copy-done.2, bf16[1040,128]{1,0:T(8,128)(2,1)S(1)} %pad_maximum_fusion.piece.own.refs_0_), custom_call_target="tpu_custom_call" | custom-call | tf_op jit(solution)/shard_map/query_first/pallas_call | solution.py:135
  8.0 0.0 copy-done.1
  8.0 4.1 %context.4.refs_2_ = bf16[128,4096]{1,0:T(8,128)(2,1)} custom-call(bf16[128,4096]{1,0:T(8,128)(2,1)S(1)} %copy-done.1, bf16[1040,128]{1,0:T(8,128)(2,1)S(1)} %pad_maximum_fusion.piece.own.refs_0_, bf16[1040,128]{1,0:T(8,128)(2,1)S(1)} %pad_maximum_fusion.piece.own.refs_0_), custom_call_target="tpu_custom_call" | custom-call | tf_op jit(solution)/shard_map/context/pallas_call | solution.py:230
  12.1 0.6 %collective-permute-done.2.refs_0_ = bf16[1040,128]{1,0:T(8,128)(2,1)S(1)} collective-permute-done((bf16[1040,128]{1,0:T(8,128)(2,1)S(1)}, bf16[1040,128]{1,0:T(8,128)(2,1)S(1)}, u32[]{:S(2)}, u32[]{:S(2)}) %collective-permute-start.2) | collective-permute-done | bytes 266272 | tf_op jit(solution)/shard_map/ppermute | solution.py:317
  12.7 1.8 %collective-permute-start.4 = (bf16[1040,128]{1,0:T(8,128)(2,1)S(1)}, bf16[1040,128]{1,0:T(8,128)(2,1)S(1)}, u32[]{:S(2)}, u32[]{:S(2)}) collective-permute-start(bf16[1040,128]{1,0:T(8,128)(2,1)S(1)} %collective-permute-done.2.refs_0_), channel_id=1, source_target_pairs={{0,2},{2,4},{4,6},{6,7},{7,5},{5,3},{3,1},{1,0},{8,10},{10,12},{12... | collective-permute-start | bytes 798728 | tf_op jit(solution)/shard_map/ppermute | solution.py:317
  14.5 0.0 collective-permute-done.refs_1_
  14.5 0.2 collective-permute-start.1
  14.7 0.1 context.5.refs_2_
  14.8 0.8 %query_more.3 = (f32[512,256]{1,0:T(8,128)S(1)}, f32[8,256]{1,0:T(8,128)S(1)}) custom-call(bf16[1024,128]{1,0:T(8,128)(2,1)S(1)} %get-tuple-element.50.stacked, f32[512,256]{1,0:T(8,128)S(1)} %get-tuple-element.36.acc_in, f32[8,256]{1,0:T(8,128)S(1)} %get-tuple-element.37.stat_in, ...), custom_call_target="tpu_custom_call", output_to_operand_aliasing={{0}: (1, {}), {1}: (2, {})} | custom-call | tf_op jit(solution)/shard_map/query_more/pallas_call | solution.py:158
  15.6 4.6 %collective-permute-done.4.refs_0_ = bf16[1040,128]{1,0:T(8,128)(2,1)S(1)} collective-permute-done((bf16[1040,128]{1,0:T(8,128)(2,1)S(1)}, bf16[1040,128]{1,0:T(8,128)(2,1)S(1)}, u32[]{:S(2)}, u32[]{:S(2)}) %collective-permute-start.4) | collective-permute-done | bytes 266272 | tf_op jit(solution)/shard_map/ppermute | solution.py:317
  20.2 1.5 %collective-permute-start.5 = (bf16[1040,128]{1,0:T(8,128)(2,1)S(1)}, bf16[1040,128]{1,0:T(8,128)(2,1)S(1)}, u32[]{:S(2)}, u32[]{:S(2)}) collective-permute-start(bf16[1040,128]{1,0:T(8,128)(2,1)S(1)} %collective-permute-done.4.refs_0_), channel_id=1, source_target_pairs={{0,2},{2,4},{4,6},{6,7},{7,5},{5,3},{3,1},{1,0},{8,10},{10,12},{12... | collective-permute-start | bytes 798728 | tf_op jit(solution)/shard_map/ppermute | solution.py:317
  21.7 0.0 collective-permute-done.1.refs_1_
  21.7 0.5 %collective-permute-start.3 = (bf16[1040,128]{1,0:T(8,128)(2,1)S(1)}, bf16[1040,128]{1,0:T(8,128)(2,1)S(1)}, u32[]{:S(2)}, u32[]{:S(2)}) collective-permute-start(bf16[1040,128]{1,0:T(8,128)(2,1)S(1)} %collective-permute-done.1.refs_1_), channel_id=1, source_target_pairs={{2,0},{4,2},{6,4},{7,6},{5,7},{3,5},{1,3},{0,1},{10,8},{12,10},{14... | collective-permute-start | bytes 798728 | tf_op jit(solution)/shard_map/ppermute | solution.py:318
  22.3 0.1 context.6.refs_2_
  22.3 0.8 %query_more.4 = (f32[512,256]{1,0:T(8,128)S(1)}, f32[8,256]{1,0:T(8,128)S(1)}) custom-call(bf16[1024,128]{1,0:T(8,128)(2,1)S(1)} %get-tuple-element.50.stacked, f32[512,256]{1,0:T(8,128)S(1)} %get-tuple-element.44.acc_in, f32[8,256]{1,0:T(8,128)S(1)} %get-tuple-element.45.stat_in, ...), custom_call_target="tpu_custom_call", output_to_operand_aliasing={{0}: (1, {}), {1}: (2, {})} | custom-call | tf_op jit(solution)/shard_map/query_more/pallas_call | solution.py:158
  23.2 3.7 %collective-permute-done.5.refs_0_ = bf16[1040,128]{1,0:T(8,128)(2,1)S(1)} collective-permute-done((bf16[1040,128]{1,0:T(8,128)(2,1)S(1)}, bf16[1040,128]{1,0:T(8,128)(2,1)S(1)}, u32[]{:S(2)}, u32[]{:S(2)}) %collective-permute-start.5) | collective-permute-done | bytes 266272 | tf_op jit(solution)/shard_map/ppermute | solution.py:317
  26.9 1.7 %collective-permute-start.6 = (bf16[528,128]{1,0:T(8,128)(2,1)S(1)}, bf16[528,128]{1,0:T(8,128)(2,1)S(1)}, u32[]{:S(2)}, u32[]{:S(2)}) collective-permute-start(bf16[528,128]{1,0:T(8,128)(2,1)S(1)} %slice.6), channel_id=1, source_target_pairs={{0,2},{2,4},{4,6},{6,7},{7,5},{5,3},{3,1},{1,0},{8,10},{10,12},{12... | collective-permute-start | bytes 405512 | tf_op jit(solution)/shard_map/ppermute | solution.py:320
  28.6 0.0 collective-permute-done.3.refs_1_
  28.6 0.5 %collective-permute-start.7 = (bf16[512,128]{1,0:T(8,128)(2,1)S(1)}, bf16[512,128]{1,0:T(8,128)(2,1)S(1)}, u32[]{:S(2)}, u32[]{:S(2)}) collective-permute-start(bf16[512,128]{1,0:T(8,128)(2,1)S(1)} %slice.7), channel_id=1, source_target_pairs={{2,0},{4,2},{6,4},{7,6},{5,7},{3,5},{1,3},{0,1},{10,8},{12,10},{14... | collective-permute-start | bytes 393224 | tf_op jit(solution)/shard_map/ppermute | solution.py:321
  29.1 0.1 context.7.refs_2_
  29.1 0.8 %query_more.5 = (f32[512,256]{1,0:T(8,128)S(1)}, f32[8,256]{1,0:T(8,128)S(1)}) custom-call(bf16[1024,128]{1,0:T(8,128)(2,1)S(1)} %get-tuple-element.50.stacked, f32[512,256]{1,0:T(8,128)S(1)} %get-tuple-element.51.acc_in, f32[8,256]{1,0:T(8,128)S(1)} %get-tuple-element.52.stat_in, ...), custom_call_target="tpu_custom_call", output_to_operand_aliasing={{0}: (1, {}), {1}: (2, {})} | custom-call | tf_op jit(solution)/shard_map/query_more/pallas_call | solution.py:158
  30.0 3.6 %collective-permute-done.7.refs_1_ = bf16[512,128]{1,0:T(8,128)(2,1)S(1)} collective-permute-done((bf16[512,128]{1,0:T(8,128)(2,1)S(1)}, bf16[512,128]{1,0:T(8,128)(2,1)S(1)}, u32[]{:S(2)}, u32[]{:S(2)}) %collective-permute-start.7) | collective-permute-done | bytes 131104 | tf_op jit(solution)/shard_map/ppermute | solution.py:321
  33.6 0.0 collective-permute-done.6.refs_0_
  33.6 1.5 %finish.1 = (bf16[32,4096]{1,0:T(8,128)(2,1)}, bf16[128,4096]{1,0:T(8,128)(2,1)}) custom-call(bf16[1024,128]{1,0:T(8,128)(2,1)S(1)} %get-tuple-element.50.stacked, f32[512,256]{1,0:T(8,128)S(1)} %get-tuple-element.55.acc, f32[8,256]{1,0:T(8,128)S(1)} %get-tuple-element.56.stat, bf16[128,4096]{1,0:T(8,128)(2,1)S(1)} %copy-done.1, ...), custom_call_target="tpu_custom_call", output_to_operand_aliasing={{1}: (7, {})} | custom-call | tf_op jit(solution)/shard_map/finish/pallas_call | solution.py:282
  (5 shorter events, 0.1 us)
Async XLA Ops:
  0.6 0.9 %copy-start = (bf16[128,512]{1,0:T(8,128)(2,1)S(1)}, bf16[128,512]{1,0:T(8,128)(2,1)}, u32[]{:S(2)}) copy-start(bf16[128,512]{1,0:T(8,128)(2,1)} %param.7) | copy-start | bytes 393220
  0.6 7.3 %copy-start.1 = (bf16[128,4096]{1,0:T(8,128)(2,1)S(1)}, bf16[128,4096]{1,0:T(8,128)(2,1)}, u32[]{:S(2)}) copy-start(bf16[128,4096]{1,0:T(8,128)(2,1)} %q_ref.11) | copy-start | bytes 3145732
  3.3 9.4 %collective-permute-start.2 = (bf16[1040,128]{1,0:T(8,128)(2,1)S(1)}, bf16[1040,128]{1,0:T(8,128)(2,1)S(1)}, u32[]{:S(2)}, u32[]{:S(2)}) collective-permute-start(bf16[1040,128]{1,0:T(8,128)(2,1)S(1)} %pad_maximum_fusion.piece.own.refs_0_), channel_id=1, source_target_pairs={{0,2},{2,4},{4,6},{6,7},{7,5},{5,3},{3,1},{1,0},{8,10},{10,12},{12... | collective-permute-start | bytes 798728 | tf_op jit(solution)/shard_map/ppermute | solution.py:317
  6.3 8.1 %collective-permute-start = (bf16[1040,128]{1,0:T(8,128)(2,1)S(1)}, bf16[1040,128]{1,0:T(8,128)(2,1)S(1)}, u32[]{:S(2)}, u32[]{:S(2)}) collective-permute-start(bf16[1040,128]{1,0:T(8,128)(2,1)S(1)} %pad_maximum_fusion.piece.own.refs_0_), channel_id=1, source_target_pairs={{2,0},{4,2},{6,4},{7,6},{5,7},{3,5},{1,3},{0,1},{10,8},{12,10},{14... | collective-permute-start | bytes 798728 | tf_op jit(solution)/shard_map/ppermute | solution.py:318
  6.3 1.0 %copy-start.2 = (bf16[32,4096]{1,0:T(8,128)(2,1)S(1)}, bf16[32,4096]{1,0:T(8,128)(2,1)}, u32[]{:S(2)}) copy-start(bf16[32,4096]{1,0:T(8,128)(2,1)} %q_ref.6) | copy-start | bytes 786436
  12.7 7.6 %collective-permute-start.4 = (bf16[1040,128]{1,0:T(8,128)(2,1)S(1)}, bf16[1040,128]{1,0:T(8,128)(2,1)S(1)}, u32[]{:S(2)}, u32[]{:S(2)}) collective-permute-start(bf16[1040,128]{1,0:T(8,128)(2,1)S(1)} %collective-permute-done.2.refs_0_), channel_id=1, source_target_pairs={{0,2},{2,4},{4,6},{6,7},{7,5},{5,3},{3,1},{1,0},{8,10},{10,12},{12... | collective-permute-start | bytes 798728 | tf_op jit(solution)/shard_map/ppermute | solution.py:317
  14.5 7.3 %collective-permute-start.1 = (bf16[1040,128]{1,0:T(8,128)(2,1)S(1)}, bf16[1040,128]{1,0:T(8,128)(2,1)S(1)}, u32[]{:S(2)}, u32[]{:S(2)}) collective-permute-start(bf16[1040,128]{1,0:T(8,128)(2,1)S(1)} %collective-permute-done.refs_1_), channel_id=1, source_target_pairs={{2,0},{4,2},{6,4},{7,6},{5,7},{3,5},{1,3},{0,1},{10,8},{12,10},{14... | collective-permute-start | bytes 798728 | tf_op jit(solution)/shard_map/ppermute | solution.py:318
  20.2 6.7 %collective-permute-start.5 = (bf16[1040,128]{1,0:T(8,128)(2,1)S(1)}, bf16[1040,128]{1,0:T(8,128)(2,1)S(1)}, u32[]{:S(2)}, u32[]{:S(2)}) collective-permute-start(bf16[1040,128]{1,0:T(8,128)(2,1)S(1)} %collective-permute-done.4.refs_0_), channel_id=1, source_target_pairs={{0,2},{2,4},{4,6},{6,7},{7,5},{5,3},{3,1},{1,0},{8,10},{10,12},{12... | collective-permute-start | bytes 798728 | tf_op jit(solution)/shard_map/ppermute | solution.py:317
  21.7 6.8 %collective-permute-start.3 = (bf16[1040,128]{1,0:T(8,128)(2,1)S(1)}, bf16[1040,128]{1,0:T(8,128)(2,1)S(1)}, u32[]{:S(2)}, u32[]{:S(2)}) collective-permute-start(bf16[1040,128]{1,0:T(8,128)(2,1)S(1)} %collective-permute-done.1.refs_1_), channel_id=1, source_target_pairs={{2,0},{4,2},{6,4},{7,6},{5,7},{3,5},{1,3},{0,1},{10,8},{12,10},{14... | collective-permute-start | bytes 798728 | tf_op jit(solution)/shard_map/ppermute | solution.py:318
  26.9 6.7 %collective-permute-start.6 = (bf16[528,128]{1,0:T(8,128)(2,1)S(1)}, bf16[528,128]{1,0:T(8,128)(2,1)S(1)}, u32[]{:S(2)}, u32[]{:S(2)}) collective-permute-start(bf16[528,128]{1,0:T(8,128)(2,1)S(1)} %slice.6), channel_id=1, source_target_pairs={{0,2},{2,4},{4,6},{6,7},{7,5},{5,3},{3,1},{1,0},{8,10},{10,12},{12... | collective-permute-start | bytes 405512 | tf_op jit(solution)/shard_map/ppermute | solution.py:320
  28.6 5.0 %collective-permute-start.7 = (bf16[512,128]{1,0:T(8,128)(2,1)S(1)}, bf16[512,128]{1,0:T(8,128)(2,1)S(1)}, u32[]{:S(2)}, u32[]{:S(2)}) collective-permute-start(bf16[512,128]{1,0:T(8,128)(2,1)S(1)} %slice.7), channel_id=1, source_target_pairs={{2,0},{4,2},{6,4},{7,6},{5,7},{3,5},{1,3},{0,1},{10,8},{12,10},{14... | collective-permute-start | bytes 393224 | tf_op jit(solution)/shard_map/ppermute | solution.py:321

commit v4 on v3

--- a/solution.py
+++ b/solution.py
@@ -26,9 +26,11 @@
     def __init__(self, refs, groups, rows):
         self.groups, self.rows = groups, rows
         self.k_ref, self.v_ref = refs[0], refs[-1]
-        self.v_base = key_rows(groups, rows) if len(refs) == 1 else 0
+        self.v_base = groups * rows if len(refs) == 1 else 0
 
     def keys(self, g):
+        if self.k_ref.shape[1] > HEAD:
+            return self.k_ref[:, g * HEAD : (g + 1) * HEAD]
         return self.k_ref[g * self.rows : (g + 1) * self.rows, :]
 
     def values(self, g):
@@ -36,8 +38,8 @@
         return jnp.transpose(self.v_ref[at : at + self.rows, :])
 
     def flag_rows(self):
-        at = self.groups * self.rows
-        return self.k_ref[at : at + FLAG_ROWS, :].astype(F32)
+        at = self.v_base + self.groups * self.rows
+        return self.v_ref[at : at + FLAG_ROWS, :].astype(F32)
 
     def flags(self):
         return jnp.transpose(jnp.broadcast_to(self.flag_rows()[:1], (self.rows, self.rows)))
@@ -54,10 +56,6 @@
 
 def outside():
     return pl.BlockSpec(memory_space=pltpu.HBM)
-
-
-def key_rows(groups, rows):
-    return groups * rows + FLAG_ROWS
 
 
 def take(refs, parts, groups, rows):
@@ -68,19 +66,16 @@
     return blocks, refs[at:]
 
 
-def pack(live_blocks, token_mask, k, v):
-    rows, width = k.shape
+def pack(live_blocks, token_mask, v):
+    rows, width = v.shape
     groups = width // HEAD
     block = lax.axis_index("ctx")
     token = lax.broadcasted_iota(jnp.int32, (FLAG_ROWS, rows), 1)
     row = lax.broadcasted_iota(jnp.int32, (FLAG_ROWS, rows), 0)
     valid = (token_mask[None, :] != 0) | ((block == 0) & (token == 0)) | (row >= FLAG_ROWS // 2)
     flags = (valid & (block < live_blocks[0])).astype(BF16)
-
-    def by_head(x):
-        return x.reshape(rows, groups, HEAD).transpose(1, 0, 2).reshape(groups * rows, HEAD)
-
-    return jnp.concatenate([by_head(k), flags, by_head(v)], 0)
+    by_head = v.reshape(rows, groups, HEAD).transpose(1, 0, 2).reshape(groups * rows, HEAD)
+    return jnp.concatenate([by_head, flags], 0)
 
 
 def attend(block, g, q, seen):
@@ -108,11 +103,11 @@
     acc_ref[g * HEAD : (g + 1) * HEAD, :] = state[2]
 
 
-def first_kernel(groups, rows, q_ref, piece, stacked, acc, stat):
+def first_kernel(groups, rows, q_ref, k_ref, v_ref, stacked, acc, stat):
     n_q, width = q_ref.shape
     heads = width // HEAD // groups
     lanes = heads * n_q
-    block = Block([piece], groups, rows)
+    block = Block([k_ref, v_ref], groups, rows)
     seen = block.seen(lanes)
     for g in range(groups):
         q = jnp.concatenate(
@@ -129,17 +124,18 @@
     ]
 
 
-def query_first(q, piece, groups, rows):
+def query_first(q, k, v, groups, rows):
     n_q, width = q.shape
     lanes = n_q * width // HEAD // groups
     return pl.pallas_call(
         functools.partial(first_kernel, groups, rows),
         out_shape=[jax.ShapeDtypeStruct((groups * lanes, HEAD), BF16)] + state_shapes(groups, lanes),
-        in_specs=[whole()] * 2,
+        in_specs=[whole()] * 3,
         out_specs=[whole()] * 3,
+        cost_estimate=pl.CostEstimate(flops=0, bytes_accessed=0, transcendentals=0),
         compiler_params=LIMIT,
         name="query_first",
-    )(q, piece)
+    )(q, k, v)
 
 
 def more_kernel(groups, rows, parts, stacked, acc_in, stat_in, *refs):
@@ -166,17 +162,11 @@
     )(stacked, acc, stat, *[part for piece in pieces for part in piece])
 
 
-def context_body(groups, rows, resident, q_ref, anchor, own, o_ref, q_buf, o_buf, in_sems, out_sems):
+def context_body(groups, rows, q_ref, anchor, own, o_ref, o_buf, out_sems):
     here = lax.axis_index("ctx")
     share = q_ref.shape[1] // groups
     spans = [pl.ds(g * share, share) for g in range(groups)]
     stores = [pltpu.make_async_copy(o_buf.at[:, at], o_ref.at[:, at], out_sems.at[g]) for g, at in enumerate(spans)]
-    loads = []
-    if not resident:
-        loads = [pltpu.make_async_copy(q_ref.at[:, at], q_buf.at[:, at], in_sems.at[g]) for g, at in enumerate(spans)]
-        q_ref = q_buf
-    for load in loads:
-        load.start()
     key = lax.broadcasted_iota(jnp.int32, (rows, rows), 0)
     row = lax.broadcasted_iota(jnp.int32, (rows, rows), 1)
     see_anchor = anchor.flags() * jnp.where(here > 0, 1.0, 0.0)
@@ -186,8 +176,6 @@
     for g in range(groups):
         keys = jnp.concatenate([anchor.keys(g), own.keys(g)], 0)
         values = jnp.concatenate([anchor.values(g), own.values(g)], 1)
-        if loads:
-            loads[g].wait()
         for h in range(share // HEAD):
             at = slice(g * share + h * HEAD, g * share + (h + 1) * HEAD)
             s = lax.dot_general(keys, q_ref[:, at], NT, preferred_element_type=F32)
@@ -202,23 +190,21 @@
         store.wait()
 
 
-def context_kernel(groups, rows, devices, parts, aliased, q_ref, own, *refs):
+def context_kernel(groups, rows, devices, parts, aliased, q_ref, own_k, own_v, *refs):
     blocks, rest = take(refs, parts, groups, rows)
-    o_ref, anchor, *buffers = rest[aliased:]
+    o_ref, anchor_k, anchor_v, *buffers = rest[aliased:]
     here = lax.axis_index("ctx")
-    if len(blocks) == 1:
-        first = blocks[0]
-    else:
-        first = Block([anchor], groups, rows)
-        for device, block in zip(devices, blocks):
-
-            @pl.when(here == device)
-            def _():
-                anchor[...] = block.k_ref[...]
+    first = Block([anchor_k, anchor_v], groups, rows)
+    for device, block in zip(devices, blocks):
+
+        @pl.when(here == device)
+        def _():
+            anchor_k[...] = block.k_ref[...]
+            anchor_v[...] = block.v_ref[...]
 
     @pl.when(functools.reduce(jnp.logical_or, [here == device for device in devices]))
     def _():
-        context_body(groups, rows, False, q_ref, first, Block([own], groups, rows), o_ref, *buffers)
+        context_body(groups, rows, q_ref, first, Block([own_k, own_v], groups, rows), o_ref, *buffers)
 
 
 def context(q, own, anchors, groups, before=None):
@@ -230,23 +216,22 @@
     return pl.pallas_call(
         functools.partial(context_kernel, groups, rows, devices, parts, len(extra)),
         out_shape=jax.ShapeDtypeStruct(q.shape, q.dtype),
-        in_specs=[outside()] + [whole()] * (1 + len(operands)) + [outside()] * len(extra),
+        in_specs=[whole()] * (3 + len(operands)) + [outside()] * len(extra),
         out_specs=outside(),
-        input_output_aliases={2 + len(operands): 0} if extra else {},
+        input_output_aliases={3 + len(operands): 0} if extra else {},
         scratch_shapes=[
-            pltpu.VMEM(own.shape, own.dtype),
+            pltpu.VMEM(own[0].shape, BF16),
+            pltpu.VMEM(own[1].shape, BF16),
             pltpu.VMEM(q.shape, q.dtype),
-            pltpu.VMEM(q.shape, q.dtype),
-            pltpu.SemaphoreType.DMA((groups,)),
             pltpu.SemaphoreType.DMA((groups,)),
         ],
         compiler_params=LIMIT,
         name="context",
-    )(q, own, *operands, *extra)
+    )(q, *own, *operands, *extra)
 
 
 def finish_kernel(
-    groups, rows, device, parts, stacked, acc, stat, q_ref, own, *refs
+    groups, rows, device, parts, stacked, acc, stat, q_ref, own_k, own_v, *refs
 ):
     (block,), rest = take(refs, parts, groups, rows)
     _, query_ref, context_ref, buffer, out_sems, *buffers = rest
@@ -270,7 +255,7 @@
 
     @pl.when(lax.axis_index("ctx") == device)
     def _():
-        context_body(groups, rows, True, q_ref, block, Block([own], groups, rows), context_ref, *buffers)
+        context_body(groups, rows, q_ref, block, Block([own_k, own_v], groups, rows), context_ref, *buffers)
 
     for store in stores:
         store.wait()
@@ -282,20 +267,18 @@
     return pl.pallas_call(
         functools.partial(finish_kernel, groups, rows, device, [len(piece)]),
         out_shape=[shape, jax.ShapeDtypeStruct(q.shape, q.dtype)],
-        in_specs=[whole()] * (5 + len(piece)) + [outside()],
+        in_specs=[whole()] * (6 + len(piece)) + [outside()],
         out_specs=[outside()] * 2,
-        input_output_aliases={5 + len(piece): 1},
+        input_output_aliases={6 + len(piece): 1},
         scratch_shapes=[
             pltpu.VMEM(shape.shape, shape.dtype),
             pltpu.SemaphoreType.DMA((groups,)),
-            pltpu.VMEM((FLAG_ROWS, HEAD), q.dtype),
             pltpu.VMEM(q.shape, q.dtype),
-            pltpu.SemaphoreType.DMA((groups,)),
             pltpu.SemaphoreType.DMA((groups,)),
         ],
         compiler_params=LIMIT,
         name="finish",
-    )(stacked, acc, stat, q, own, *piece, before)
+    )(stacked, acc, stat, q, *own, *piece, before)
 
 
 def local(context_q, context_k, context_v, question_q, token_mask, live_blocks):
@@ -306,29 +289,33 @@
     forth = [(ring[i], ring[(i + 1) % n]) for i in range(n)]
     back = [(b, a) for a, b in forth]
 
-    own = pack(live_blocks, token_mask, context_k, context_v)
     half = n // 2
-    split = key_rows(groups, rows)
-    left = right = own
-    arrived = [(ring[0], (own,))]
-    context_output = state = None
+
+    def send(value, pairs):
+        return lax.ppermute(value, "ctx", pairs)
+
+    packed = pack(live_blocks, token_mask, context_v)
+    own = (context_k, packed)
+    left_k = right_k = context_k
+    left_v = right_v = packed
+    state = None
+    arrived, anchors = [], [(ring[0], own)]
     for step in range(1, half + 1):
+        left_k, right_v = send(left_k, forth), send(right_v, back)
         if step < half:
-            left = lax.ppermute(left, "ctx", forth)
-            right = lax.ppermute(right, "ctx", back)
+            left_v, right_k = send(left_v, forth), send(right_k, back)
+        if step == 1:
+            state = query_first(question_q, *own, groups, rows)
         else:
-            left = lax.ppermute(left[:split], "ctx", forth)
-            right = lax.ppermute(right[split:], "ctx", back)
-        pieces = [piece for _, piece in arrived]
-        if state is None:
-            state = query_first(question_q, own, groups, rows)
-        else:
-            state = [state[0], *query_more(*state, pieces, groups, rows)]
-        context_output = context(context_q, own, arrived, groups, context_output)
+            state = [state[0], *query_more(*state, [piece for _, piece in arrived], groups, rows)]
         if step < half:
-            left = lax.optimization_barrier((left, state, context_output))[0]
-            right, state, context_output = lax.optimization_barrier((right, state, context_output))
-            arrived = [(ring[step], (left,)), (ring[n - step], (right,))]
+            right_k, state = lax.optimization_barrier((right_k, state))
+            arrived = [(ring[step], (left_k, left_v)), (ring[n - step], (right_k, right_v))]
+        if step < half - 1:
+            anchors += arrived
+    context_output = context(context_q, own, anchors, groups)
+    context_output = context(context_q, own, arrived, groups, context_output)
+    left, right = left_k, right_v
     query_output, context_output = finish(
         *state,
         context_q,

time: 35.5 us -> 33 us (0.930)
  the two profiles are of different devices: /device:TPU:0 before, /device:TPU:18 now
where the time goes in v4:
time: 33 us; the launch traced here: 32.8 us
  starting transfers between devices  13.1 us (40%)
  waiting for transfers between devices  9.95 us (30%)
  Pallas kernels  7.57 us (23%)
  between operations  1.43 us (4%)
  local copies, waits for them, and re-layouts  0.68 us (2%)
    ppermute x14, starting transfers between devices, send(): return lax.ppermute(value, 'ctx', pairs)  13.1 us
    ppermute x14, waiting for transfers between devices, send(): return lax.ppermute(value, 'ctx', pairs)  9.95 us
    pallas_call x2, Pallas kernels, context(): pl.pallas_call(functools.partial(context_kernel, groups, rows, devices, p...  2.91 us
    pallas_call x3, Pallas kernels, query_more(): pl.pallas_call(functools.partial(more_kernel, groups, rows, [len(piece) f...  2.54 us
    pallas_call x1, Pallas kernels, finish(): pl.pallas_call(functools.partial(finish_kernel, groups, rows, device, [le...  1.46 us
    pallas_call x1, Pallas kernels, query_first(): pl.pallas_call(functools.partial(first_kernel, groups, rows), out_shape=[...  0.66 us
  transfers between devices with their start and end apart: 14, of which 9 were waited for; matrix products, arithmetic and copies ran while one was open for 0% of the time, Pallas kernels for 19%

profile of v4, /device:TPU:18, one launch (start us, length us, event | category | flops | bytes accessed | tf_op | source)
XLA Modules:
  0.0 32.8 jit_solution(6881938583673360919)
XLA Ops:
  0.6 0.0 copy-start
  1.3 0.0 copy-start.4
  1.4 0.2 copy-done
  1.6 0.0 copy-start.3
  1.6 0.4 %copy-done.4 = s32[128]{0:T(128)S(1)} copy-done((s32[128]{0:T(128)S(1)}, s32[128]{0:T(128)}, u32[]{:S(2)}) %copy-start.4) | copy-done | bytes 536
  2.0 0.0 copy-start.2
  2.0 0.1 and_convert_fusion
  2.1 0.0 copy-start.1
  2.1 1.6 %collective-permute-start.4 = (bf16[528,128]{1,0:T(8,128)(2,1)S(1)}, bf16[528,128]{1,0:T(8,128)(2,1)S(1)}, u32[]{:S(2)}, u32[]{:S(2)}) collective-permute-start(bf16[528,128]{1,0:T(8,128)(2,1)S(1)} %pad_maximum_fusion.v_ref.own_v.refs_1_), channel_id=1, source_target_pairs={{2,0},{4,2},{6,4},{7,6},{5,7},{3,5},{1,3},{0,1},{10,8},{12,10},{14... | collective-permute-start | bytes 405512 | tf_op jit(solution)/shard_map/ppermute | solution.py:295
  3.8 0.0 copy-done.2
  3.8 0.4 %collective-permute-start.2 = (bf16[128,512]{1,0:T(8,128)(2,1)S(1)}, bf16[128,512]{1,0:T(8,128)(2,1)S(1)}, u32[]{:S(2)}, u32[]{:S(2)}) collective-permute-start(bf16[128,512]{1,0:T(8,128)(2,1)S(1)} %copy-done.2), channel_id=1, source_target_pairs={{0,2},{2,4},{4,6},{6,7},{7,5},{5,3},{3,1},{1,0},{8,10},{10,12},{12... | collective-permute-start | bytes 393224 | tf_op jit(solution)/shard_map/ppermute | solution.py:295
  4.2 0.4 %collective-permute-start.3 = (bf16[528,128]{1,0:T(8,128)(2,1)S(1)}, bf16[528,128]{1,0:T(8,128)(2,1)S(1)}, u32[]{:S(2)}, u32[]{:S(2)}) collective-permute-start(bf16[528,128]{1,0:T(8,128)(2,1)S(1)} %pad_maximum_fusion.v_ref.own_v.refs_1_), channel_id=1, source_target_pairs={{0,2},{2,4},{4,6},{6,7},{7,5},{5,3},{3,1},{1,0},{8,10},{10,12},{12... | collective-permute-start | bytes 405512 | tf_op jit(solution)/shard_map/ppermute | solution.py:295
  4.7 2.8 %collective-permute-done.4.refs_3_.refs_5_ = bf16[528,128]{1,0:T(8,128)(2,1)S(1)} collective-permute-done((bf16[528,128]{1,0:T(8,128)(2,1)S(1)}, bf16[528,128]{1,0:T(8,128)(2,1)S(1)}, u32[]{:S(2)}, u32[]{:S(2)}) %collective-permute-start.4) | collective-permute-done | bytes 135200 | tf_op jit(solution)/shard_map/ppermute | solution.py:295
  7.5 1.6 %collective-permute-start.8 = (bf16[528,128]{1,0:T(8,128)(2,1)S(1)}, bf16[528,128]{1,0:T(8,128)(2,1)S(1)}, u32[]{:S(2)}, u32[]{:S(2)}) collective-permute-start(bf16[528,128]{1,0:T(8,128)(2,1)S(1)} %collective-permute-done.4.refs_3_.refs_5_), channel_id=1, source_target_pairs={{2,0},{4,2},{6,4},{7,6},{5,7},{3,5},{1,3},{0,1},{10,8},{12,10},{14... | collective-permute-start | bytes 405512 | tf_op jit(solution)/shard_map/ppermute | solution.py:295
  9.1 0.5 %collective-permute-start = (bf16[128,512]{1,0:T(8,128)(2,1)S(1)}, bf16[128,512]{1,0:T(8,128)(2,1)S(1)}, u32[]{:S(2)}, u32[]{:S(2)}) collective-permute-start(bf16[128,512]{1,0:T(8,128)(2,1)S(1)} %copy-done.2), channel_id=1, source_target_pairs={{2,0},{4,2},{6,4},{7,6},{5,7},{3,5},{1,3},{0,1},{10,8},{12,10},{14... | collective-permute-start | bytes 393224 | tf_op jit(solution)/shard_map/ppermute | solution.py:295
  9.6 0.5 %collective-permute-done.2.refs_0_.refs_2_ = bf16[128,512]{1,0:T(8,128)(2,1)S(1)} collective-permute-done((bf16[128,512]{1,0:T(8,128)(2,1)S(1)}, bf16[128,512]{1,0:T(8,128)(2,1)S(1)}, u32[]{:S(2)}, u32[]{:S(2)}) %collective-permute-start.2) | collective-permute-done | bytes 131104 | tf_op jit(solution)/shard_map/ppermute | solution.py:295
  10.2 0.9 %collective-permute-start.6 = (bf16[128,512]{1,0:T(8,128)(2,1)S(1)}, bf16[128,512]{1,0:T(8,128)(2,1)S(1)}, u32[]{:S(2)}, u32[]{:S(2)}) collective-permute-start(bf16[128,512]{1,0:T(8,128)(2,1)S(1)} %collective-permute-done.2.refs_0_.refs_2_), channel_id=1, source_target_pairs={{0,2},{2,4},{4,6},{6,7},{7,5},{5,3},{3,1},{1,0},{8,10},{10,12},{12... | collective-permute-start | bytes 393224 | tf_op jit(solution)/shard_map/ppermute | solution.py:295
  11.1 1.4 %collective-permute-done.3.refs_1_.refs_3_ = bf16[528,128]{1,0:T(8,128)(2,1)S(1)} collective-permute-done((bf16[528,128]{1,0:T(8,128)(2,1)S(1)}, bf16[528,128]{1,0:T(8,128)(2,1)S(1)}, u32[]{:S(2)}, u32[]{:S(2)}) %collective-permute-start.3) | collective-permute-done | bytes 135200 | tf_op jit(solution)/shard_map/ppermute | solution.py:295
  12.5 0.0 collective-permute-start.7
  12.5 0.9 %collective-permute-done.8.refs_3_.refs_9_ = bf16[528,128]{1,0:T(8,128)(2,1)S(1)} collective-permute-done((bf16[528,128]{1,0:T(8,128)(2,1)S(1)}, bf16[528,128]{1,0:T(8,128)(2,1)S(1)}, u32[]{:S(2)}, u32[]{:S(2)}) %collective-permute-start.8) | collective-permute-done | bytes 135200 | tf_op jit(solution)/shard_map/ppermute | solution.py:295
  13.4 1.6 %collective-permute-start.11 = (bf16[528,128]{1,0:T(8,128)(2,1)S(1)}, bf16[528,128]{1,0:T(8,128)(2,1)S(1)}, u32[]{:S(2)}, u32[]{:S(2)}) collective-permute-start(bf16[528,128]{1,0:T(8,128)(2,1)S(1)} %collective-permute-done.8.refs_3_.refs_9_), channel_id=1, source_target_pairs={{2,0},{4,2},{6,4},{7,6},{5,7},{3,5},{1,3},{0,1},{10,8},{12,10},{14... | collective-permute-start | bytes 405512 | tf_op jit(solution)/shard_map/ppermute | solution.py:295
  15.0 0.0 copy-done.3
  15.0 0.7 %query_first.1 = (bf16[1024,128]{1,0:T(8,128)(2,1)S(1)}, f32[512,256]{1,0:T(8,128)S(1)}, f32[8,256]{1,0:T(8,128)S(1)}) custom-call(bf16[32,4096]{1,0:T(8,128)(2,1)S(1)} %copy-done.3, bf16[128,512]{1,0:T(8,128)(2,1)S(1)} %copy-done.2, bf16[528,128]{1,0:T(8,128)(2,1)S(1)} %pad_maximum_fusion.v_ref.own_v.refs_1_), custom_call_target="tpu_custom_call" | custom-call | tf_op jit(solution)/shard_map/query_first/pallas_call | solution.py:130
  15.7 0.6 %collective-permute-done.refs_2_.refs_4_ = bf16[128,512]{1,0:T(8,128)(2,1)S(1)} collective-permute-done((bf16[128,512]{1,0:T(8,128)(2,1)S(1)}, bf16[128,512]{1,0:T(8,128)(2,1)S(1)}, u32[]{:S(2)}, u32[]{:S(2)}) %collective-permute-start) | collective-permute-done | bytes 131104 | tf_op jit(solution)/shard_map/ppermute | solution.py:295
  16.2 1.6 %collective-permute-start.1 = (bf16[128,512]{1,0:T(8,128)(2,1)S(1)}, bf16[128,512]{1,0:T(8,128)(2,1)S(1)}, u32[]{:S(2)}, u32[]{:S(2)}) collective-permute-start(bf16[128,512]{1,0:T(8,128)(2,1)S(1)} %collective-permute-done.refs_2_.refs_4_), channel_id=1, source_target_pairs={{2,0},{4,2},{6,4},{7,6},{5,7},{3,5},{1,3},{0,1},{10,8},{12,10},{14... | collective-permute-start | bytes 393224 | tf_op jit(solution)/shard_map/ppermute | solution.py:295
  17.8 0.0 collective-permute-done.6.refs_0_.refs_6_
  17.8 0.5 %collective-permute-start.9 = (bf16[128,512]{1,0:T(8,128)(2,1)S(1)}, bf16[128,512]{1,0:T(8,128)(2,1)S(1)}, u32[]{:S(2)}, u32[]{:S(2)}) collective-permute-start(bf16[128,512]{1,0:T(8,128)(2,1)S(1)} %collective-permute-done.6.refs_0_.refs_6_), channel_id=1, source_target_pairs={{0,2},{2,4},{4,6},{6,7},{7,5},{5,3},{3,1},{1,0},{8,10},{10,12},{12... | collective-permute-start | bytes 393224 | tf_op jit(solution)/shard_map/ppermute | solution.py:295
  18.3 0.2 collective-permute-done.7.refs_1_.refs_7_
  18.5 0.3 collective-permute-start.10
  18.7 0.5 %collective-permute-done.11.refs_3_ = bf16[528,128]{1,0:T(8,128)(2,1)S(1)} collective-permute-done((bf16[528,128]{1,0:T(8,128)(2,1)S(1)}, bf16[528,128]{1,0:T(8,128)(2,1)S(1)}, u32[]{:S(2)}, u32[]{:S(2)}) %collective-permute-start.11) | collective-permute-done | bytes 135200 | tf_op jit(solution)/shard_map/ppermute | solution.py:295
  19.2 1.6 %collective-permute-start.13 = (bf16[528,128]{1,0:T(8,128)(2,1)S(1)}, bf16[528,128]{1,0:T(8,128)(2,1)S(1)}, u32[]{:S(2)}, u32[]{:S(2)}) collective-permute-start(bf16[528,128]{1,0:T(8,128)(2,1)S(1)} %collective-permute-done.11.refs_3_), channel_id=1, source_target_pairs={{2,0},{4,2},{6,4},{7,6},{5,7},{3,5},{1,3},{0,1},{10,8},{12,10},{14... | collective-permute-start | bytes 405512 | tf_op jit(solution)/shard_map/ppermute | solution.py:295
  20.8 0.8 %query_more.3 = (f32[512,256]{1,0:T(8,128)S(1)}, f32[8,256]{1,0:T(8,128)S(1)}) custom-call(bf16[1024,128]{1,0:T(8,128)(2,1)S(1)} %get-tuple-element.40.stacked, f32[512,256]{1,0:T(8,128)S(1)} %get-tuple-element.30.acc_in, f32[8,256]{1,0:T(8,128)S(1)} %get-tuple-element.31.stat_in, ...), custom_call_target="tpu_custom_call", output_to_operand_aliasing={{0}: (1, {}), {1}: (2, {})} | custom-call | tf_op jit(solution)/shard_map/query_more/pallas_call | solution.py:154
  21.6 1.0 %collective-permute-done.1.refs_2_.refs_8_ = bf16[128,512]{1,0:T(8,128)(2,1)S(1)} collective-permute-done((bf16[128,512]{1,0:T(8,128)(2,1)S(1)}, bf16[128,512]{1,0:T(8,128)(2,1)S(1)}, u32[]{:S(2)}, u32[]{:S(2)}) %collective-permute-start.1) | collective-permute-done | bytes 131104 | tf_op jit(solution)/shard_map/ppermute | solution.py:295
  22.6 1.6 %collective-permute-start.5 = (bf16[128,512]{1,0:T(8,128)(2,1)S(1)}, bf16[128,512]{1,0:T(8,128)(2,1)S(1)}, u32[]{:S(2)}, u32[]{:S(2)}) collective-permute-start(bf16[128,512]{1,0:T(8,128)(2,1)S(1)} %collective-permute-done.1.refs_2_.refs_8_), channel_id=1, source_target_pairs={{2,0},{4,2},{6,4},{7,6},{5,7},{3,5},{1,3},{0,1},{10,8},{12,10},{14... | collective-permute-start | bytes 393224 | tf_op jit(solution)/shard_map/ppermute | solution.py:295
  24.2 0.0 collective-permute-done.9.refs_0_
  24.2 0.5 %collective-permute-start.12 = (bf16[128,512]{1,0:T(8,128)(2,1)S(1)}, bf16[128,512]{1,0:T(8,128)(2,1)S(1)}, u32[]{:S(2)}, u32[]{:S(2)}) collective-permute-start(bf16[128,512]{1,0:T(8,128)(2,1)S(1)} %collective-permute-done.9.refs_0_), channel_id=1, source_target_pairs={{0,2},{2,4},{4,6},{6,7},{7,5},{5,3},{3,1},{1,0},{8,10},{10,12},{12... | collective-permute-start | bytes 393224 | tf_op jit(solution)/shard_map/ppermute | solution.py:295
  24.6 0.0 copy-done.1
  24.7 0.8 %query_more.4 = (f32[512,256]{1,0:T(8,128)S(1)}, f32[8,256]{1,0:T(8,128)S(1)}) custom-call(bf16[1024,128]{1,0:T(8,128)(2,1)S(1)} %get-tuple-element.40.stacked, f32[512,256]{1,0:T(8,128)S(1)} %get-tuple-element.36.acc_in, f32[8,256]{1,0:T(8,128)S(1)} %get-tuple-element.37.stat_in, ...), custom_call_target="tpu_custom_call", output_to_operand_aliasing={{0}: (1, {}), {1}: (2, {})} | custom-call | tf_op jit(solution)/shard_map/query_more/pallas_call | solution.py:154
  25.5 2.0 %collective-permute-done.5.refs_2_ = bf16[128,512]{1,0:T(8,128)(2,1)S(1)} collective-permute-done((bf16[128,512]{1,0:T(8,128)(2,1)S(1)}, bf16[128,512]{1,0:T(8,128)(2,1)S(1)}, u32[]{:S(2)}, u32[]{:S(2)}) %collective-permute-start.5) | collective-permute-done | bytes 131104 | tf_op jit(solution)/shard_map/ppermute | solution.py:295
  27.6 0.0 collective-permute-done.10.refs_1_
  27.6 2.9 %context.3.refs_2_ = bf16[128,4096]{1,0:T(8,128)(2,1)} custom-call(bf16[128,4096]{1,0:T(8,128)(2,1)S(1)} %copy-done.1, bf16[128,512]{1,0:T(8,128)(2,1)S(1)} %copy-done.2, bf16[528,128]{1,0:T(8,128)(2,1)S(1)} %pad_maximum_fusion.v_ref.own_v.refs_1_, bf16[128,512]{1,0:T(8,128)(2,1)S(1)} %collective-permute-done.9.refs_0_, ...), custom_call_target="tpu_custom_call", output_to_operand_aliasing={{}: (7, {})} | custom-call | tf_op jit(solution)/shard_map/context/pallas_call | solution.py:216
  30.5 0.8 %query_more.5 = (f32[512,256]{1,0:T(8,128)S(1)}, f32[8,256]{1,0:T(8,128)S(1)}) custom-call(bf16[1024,128]{1,0:T(8,128)(2,1)S(1)} %get-tuple-element.40.stacked, f32[512,256]{1,0:T(8,128)S(1)} %get-tuple-element.41.acc_in, f32[8,256]{1,0:T(8,128)S(1)} %get-tuple-element.42.stat_in, ...), custom_call_target="tpu_custom_call", output_to_operand_aliasing={{0}: (1, {}), {1}: (2, {})} | custom-call | tf_op jit(solution)/shard_map/query_more/pallas_call | solution.py:154
  31.3 0.0 collective-permute-done.12.refs_0_
  31.3 0.0 collective-permute-done.13.refs_1_
  31.3 1.5 %finish.1 = (bf16[32,4096]{1,0:T(8,128)(2,1)}, bf16[128,4096]{1,0:T(8,128)(2,1)}) custom-call(bf16[1024,128]{1,0:T(8,128)(2,1)S(1)} %get-tuple-element.40.stacked, f32[512,256]{1,0:T(8,128)S(1)} %get-tuple-element.44.acc, f32[8,256]{1,0:T(8,128)S(1)} %get-tuple-element.45.stat, bf16[128,4096]{1,0:T(8,128)(2,1)S(1)} %copy-done.1, ...), custom_call_target="tpu_custom_call", output_to_operand_aliasing={{1}: (8, {})} | custom-call | tf_op jit(solution)/shard_map/finish/pallas_call | solution.py:267
  (5 shorter events, 0.1 us)
Async XLA Ops:
  0.6 0.9 %copy-start = (bf16[128,512]{1,0:T(8,128)(2,1)S(1)}, bf16[128,512]{1,0:T(8,128)(2,1)}, u32[]{:S(2)}) copy-start(bf16[128,512]{1,0:T(8,128)(2,1)} %param.8) | copy-start | bytes 393220
  1.3 0.7 %copy-start.4 = (s32[128]{0:T(128)S(1)}, s32[128]{0:T(128)}, u32[]{:S(2)}) copy-start(s32[128]{0:T(128)} %param.10) | copy-start | bytes 1540
  1.6 13.5 %copy-start.3 = (bf16[32,4096]{1,0:T(8,128)(2,1)S(1)}, bf16[32,4096]{1,0:T(8,128)(2,1)}, u32[]{:S(2)}) copy-start(bf16[32,4096]{1,0:T(8,128)(2,1)} %q_ref.4) | copy-start | bytes 786436
  2.0 1.7 %copy-start.2 = (bf16[128,512]{1,0:T(8,128)(2,1)S(1)}, bf16[128,512]{1,0:T(8,128)(2,1)}, u32[]{:S(2)}) copy-start(bf16[128,512]{1,0:T(8,128)(2,1)} %own_k.5) | copy-start | bytes 393220
  2.1 22.5 %copy-start.1 = (bf16[128,4096]{1,0:T(8,128)(2,1)S(1)}, bf16[128,4096]{1,0:T(8,128)(2,1)}, u32[]{:S(2)}) copy-start(bf16[128,4096]{1,0:T(8,128)(2,1)} %q_ref.7) | copy-start | bytes 3145732
  2.1 5.4 %collective-permute-start.4 = (bf16[528,128]{1,0:T(8,128)(2,1)S(1)}, bf16[528,128]{1,0:T(8,128)(2,1)S(1)}, u32[]{:S(2)}, u32[]{:S(2)}) collective-permute-start(bf16[528,128]{1,0:T(8,128)(2,1)S(1)} %pad_maximum_fusion.v_ref.own_v.refs_1_), channel_id=1, source_target_pairs={{2,0},{4,2},{6,4},{7,6},{5,7},{3,5},{1,3},{0,1},{10,8},{12,10},{14... | collective-permute-start | bytes 405512 | tf_op jit(solution)/shard_map/ppermute | solution.py:295
  3.8 6.4 %collective-permute-start.2 = (bf16[128,512]{1,0:T(8,128)(2,1)S(1)}, bf16[128,512]{1,0:T(8,128)(2,1)S(1)}, u32[]{:S(2)}, u32[]{:S(2)}) collective-permute-start(bf16[128,512]{1,0:T(8,128)(2,1)S(1)} %copy-done.2), channel_id=1, source_target_pairs={{0,2},{2,4},{4,6},{6,7},{7,5},{5,3},{3,1},{1,0},{8,10},{10,12},{12... | collective-permute-start | bytes 393224 | tf_op jit(solution)/shard_map/ppermute | solution.py:295
  4.2 8.3 %collective-permute-start.3 = (bf16[528,128]{1,0:T(8,128)(2,1)S(1)}, bf16[528,128]{1,0:T(8,128)(2,1)S(1)}, u32[]{:S(2)}, u32[]{:S(2)}) collective-permute-start(bf16[528,128]{1,0:T(8,128)(2,1)S(1)} %pad_maximum_fusion.v_ref.own_v.refs_1_), channel_id=1, source_target_pairs={{0,2},{2,4},{4,6},{6,7},{7,5},{5,3},{3,1},{1,0},{8,10},{10,12},{12... | collective-permute-start | bytes 405512 | tf_op jit(solution)/shard_map/ppermute | solution.py:295
  7.5 5.9 %collective-permute-start.8 = (bf16[528,128]{1,0:T(8,128)(2,1)S(1)}, bf16[528,128]{1,0:T(8,128)(2,1)S(1)}, u32[]{:S(2)}, u32[]{:S(2)}) collective-permute-start(bf16[528,128]{1,0:T(8,128)(2,1)S(1)} %collective-permute-done.4.refs_3_.refs_5_), channel_id=1, source_target_pairs={{2,0},{4,2},{6,4},{7,6},{5,7},{3,5},{1,3},{0,1},{10,8},{12,10},{14... | collective-permute-start | bytes 405512 | tf_op jit(solution)/shard_map/ppermute | solution.py:295
  9.1 7.2 %collective-permute-start = (bf16[128,512]{1,0:T(8,128)(2,1)S(1)}, bf16[128,512]{1,0:T(8,128)(2,1)S(1)}, u32[]{:S(2)}, u32[]{:S(2)}) collective-permute-start(bf16[128,512]{1,0:T(8,128)(2,1)S(1)} %copy-done.2), channel_id=1, source_target_pairs={{2,0},{4,2},{6,4},{7,6},{5,7},{3,5},{1,3},{0,1},{10,8},{12,10},{14... | collective-permute-start | bytes 393224 | tf_op jit(solution)/shard_map/ppermute | solution.py:295
  10.2 7.7 %collective-permute-start.6 = (bf16[128,512]{1,0:T(8,128)(2,1)S(1)}, bf16[128,512]{1,0:T(8,128)(2,1)S(1)}, u32[]{:S(2)}, u32[]{:S(2)}) collective-permute-start(bf16[128,512]{1,0:T(8,128)(2,1)S(1)} %collective-permute-done.2.refs_0_.refs_2_), channel_id=1, source_target_pairs={{0,2},{2,4},{4,6},{6,7},{7,5},{5,3},{3,1},{1,0},{8,10},{10,12},{12... | collective-permute-start | bytes 393224 | tf_op jit(solution)/shard_map/ppermute | solution.py:295
  12.5 5.9 %collective-permute-start.7 = (bf16[528,128]{1,0:T(8,128)(2,1)S(1)}, bf16[528,128]{1,0:T(8,128)(2,1)S(1)}, u32[]{:S(2)}, u32[]{:S(2)}) collective-permute-start(bf16[528,128]{1,0:T(8,128)(2,1)S(1)} %collective-permute-done.3.refs_1_.refs_3_), channel_id=1, source_target_pairs={{0,2},{2,4},{4,6},{6,7},{7,5},{5,3},{3,1},{1,0},{8,10},{10,12},{12... | collective-permute-start | bytes 405512 | tf_op jit(solution)/shard_map/ppermute | solution.py:295
  13.4 5.7 %collective-permute-start.11 = (bf16[528,128]{1,0:T(8,128)(2,1)S(1)}, bf16[528,128]{1,0:T(8,128)(2,1)S(1)}, u32[]{:S(2)}, u32[]{:S(2)}) collective-permute-start(bf16[528,128]{1,0:T(8,128)(2,1)S(1)} %collective-permute-done.8.refs_3_.refs_9_), channel_id=1, source_target_pairs={{2,0},{4,2},{6,4},{7,6},{5,7},{3,5},{1,3},{0,1},{10,8},{12,10},{14... | collective-permute-start | bytes 405512 | tf_op jit(solution)/shard_map/ppermute | solution.py:295
  16.2 6.4 %collective-permute-start.1 = (bf16[128,512]{1,0:T(8,128)(2,1)S(1)}, bf16[128,512]{1,0:T(8,128)(2,1)S(1)}, u32[]{:S(2)}, u32[]{:S(2)}) collective-permute-start(bf16[128,512]{1,0:T(8,128)(2,1)S(1)} %collective-permute-done.refs_2_.refs_4_), channel_id=1, source_target_pairs={{2,0},{4,2},{6,4},{7,6},{5,7},{3,5},{1,3},{0,1},{10,8},{12,10},{14... | collective-permute-start | bytes 393224 | tf_op jit(solution)/shard_map/ppermute | solution.py:295
  17.8 6.4 %collective-permute-start.9 = (bf16[128,512]{1,0:T(8,128)(2,1)S(1)}, bf16[128,512]{1,0:T(8,128)(2,1)S(1)}, u32[]{:S(2)}, u32[]{:S(2)}) collective-permute-start(bf16[128,512]{1,0:T(8,128)(2,1)S(1)} %collective-permute-done.6.refs_0_.refs_6_), channel_id=1, source_target_pairs={{0,2},{2,4},{4,6},{6,7},{7,5},{5,3},{3,1},{1,0},{8,10},{10,12},{12... | collective-permute-start | bytes 393224 | tf_op jit(solution)/shard_map/ppermute | solution.py:295
  18.5 9.1 %collective-permute-start.10 = (bf16[528,128]{1,0:T(8,128)(2,1)S(1)}, bf16[528,128]{1,0:T(8,128)(2,1)S(1)}, u32[]{:S(2)}, u32[]{:S(2)}) collective-permute-start(bf16[528,128]{1,0:T(8,128)(2,1)S(1)} %collective-permute-done.7.refs_1_.refs_7_), channel_id=1, source_target_pairs={{0,2},{2,4},{4,6},{6,7},{7,5},{5,3},{3,1},{1,0},{8,10},{10,12},{12... | collective-permute-start | bytes 405512 | tf_op jit(solution)/shard_map/ppermute | solution.py:295
  19.2 12.1 %collective-permute-start.13 = (bf16[528,128]{1,0:T(8,128)(2,1)S(1)}, bf16[528,128]{1,0:T(8,128)(2,1)S(1)}, u32[]{:S(2)}, u32[]{:S(2)}) collective-permute-start(bf16[528,128]{1,0:T(8,128)(2,1)S(1)} %collective-permute-done.11.refs_3_), channel_id=1, source_target_pairs={{2,0},{4,2},{6,4},{7,6},{5,7},{3,5},{1,3},{0,1},{10,8},{12,10},{14... | collective-permute-start | bytes 405512 | tf_op jit(solution)/shard_map/ppermute | solution.py:295
  22.6 5.0 %collective-permute-start.5 = (bf16[128,512]{1,0:T(8,128)(2,1)S(1)}, bf16[128,512]{1,0:T(8,128)(2,1)S(1)}, u32[]{:S(2)}, u32[]{:S(2)}) collective-permute-start(bf16[128,512]{1,0:T(8,128)(2,1)S(1)} %collective-permute-done.1.refs_2_.refs_8_), channel_id=1, source_target_pairs={{2,0},{4,2},{6,4},{7,6},{5,7},{3,5},{1,3},{0,1},{10,8},{12,10},{14... | collective-permute-start | bytes 393224 | tf_op jit(solution)/shard_map/ppermute | solution.py:295
  24.2 7.1 %collective-permute-start.12 = (bf16[128,512]{1,0:T(8,128)(2,1)S(1)}, bf16[128,512]{1,0:T(8,128)(2,1)S(1)}, u32[]{:S(2)}, u32[]{:S(2)}) collective-permute-start(bf16[128,512]{1,0:T(8,128)(2,1)S(1)} %collective-permute-done.9.refs_0_), channel_id=1, source_target_pairs={{0,2},{2,4},{4,6},{6,7},{7,5},{5,3},{3,1},{1,0},{8,10},{10,12},{12... | collective-permute-start | bytes 393224 | tf_op jit(solution)/shard_map/ppermute | solution.py:295

commit v5 on v4

v5 whole, which is shorter than its diff:
```python
import functools
import math

import jax
import jax.numpy as jnp
from jax import lax
from jax.experimental import pallas as pl
from jax.experimental.pallas import tpu as pltpu
from jax.sharding import PartitionSpec as P

HEAD = 128
FLAG_ROWS = 16
HIDDEN = -1e30
SCALE = HEAD**-0.5 / math.log(2.0)
NT = (((1,), (1,)), ((), ()))
F32 = jnp.float32
BF16 = jnp.bfloat16
LIMIT = pltpu.CompilerParams(vmem_limit_bytes=24 * 1024 * 1024)


def whole():
    return pl.BlockSpec(memory_space=pltpu.VMEM)


class Block:
    def __init__(self, refs, groups, rows):
        self.groups, self.rows = groups, rows
        self.k_ref, self.v_ref = refs[0], refs[-1]
        self.v_base = groups * rows if len(refs) == 1 else 0

    def keys(self, g):
        if self.k_ref.shape[1] > HEAD:
            return self.k_ref[:, g * HEAD : (g + 1) * HEAD]
        return self.k_ref[g * self.rows : (g + 1) * self.rows, :]

    def values(self, g):
        at = self.v_base + g * self.rows
        return jnp.transpose(self.v_ref[at : at + self.rows, :])

    def flags(self):
        at = self.v_base + self.groups * self.rows
        flags = self.v_ref[at : at + FLAG_ROWS, :].astype(F32)[:1]
        return jnp.transpose(jnp.broadcast_to(flags, (self.rows, self.rows)))

    def bias(self, lanes, alive):
        flags = self.flags()
        while flags.shape[1] < lanes:
            flags = jnp.concatenate([flags, flags], 1)
        return jnp.where(flags[:, :lanes] > jnp.where(alive, 0.5, 2.0), 0.0, HIDDEN)


def scalar():
    return pl.BlockSpec(memory_space=pltpu.SMEM)


def ring_device(n, shift):
    here = lax.axis_index("ctx")
    place = jnp.where(lax.rem(here, 2) == 0, lax.div(here, 2), n - 1 - lax.div(here, 2))
    place = lax.rem(place + shift + n, n)
    return jnp.where(place < n // 2, 2 * place, 2 * (n - 1 - place) + 1)


def outside():
    return pl.BlockSpec(memory_space=pltpu.HBM)


def take(refs, parts, groups, rows):
    blocks, at = [], 0
    for count in parts:
        blocks.append(Block(refs[at : at + count], groups, rows))
        at += count
    return blocks, refs[at:]


def pack(token_mask, v):
    rows, width = v.shape
    groups = width // HEAD
    block = lax.axis_index("ctx")
    token = lax.broadcasted_iota(jnp.int32, (FLAG_ROWS, rows), 1)
    flags = ((token_mask[None, :] != 0) | ((block == 0) & (token == 0))).astype(BF16)
    by_head = v.reshape(rows, groups, HEAD).transpose(1, 0, 2).reshape(groups * rows, HEAD)
    return jnp.concatenate([by_head, flags], 0)


def attend(blocks, g, q, biases):
    keys = jnp.concatenate([block.keys(g) for block in blocks], 0)
    scores = lax.dot_general(keys, q, NT, preferred_element_type=F32)
    results = []
    for i, (block, bias) in enumerate(zip(blocks, biases)):
        s = scores[i * block.rows : (i + 1) * block.rows] + bias
        m = jnp.max(s, axis=0, keepdims=True)
        p = jnp.exp2((s - m) * SCALE)
        l = jnp.sum(p, axis=0, keepdims=True)
        results.append((m, l, jnp.dot(block.values(g), p.astype(BF16), preferred_element_type=F32)))
    return results


def merge(parts):
    top = functools.reduce(jnp.maximum, [m for m, _, _ in parts])
    factors = [jnp.exp2((m - top) * SCALE) for m, _, _ in parts]
    total = sum(l * f for (_, l, _), f in zip(parts, factors))
    return top, total, sum(a * f for (_, _, a), f in zip(parts, factors))


def load_state(acc_ref, stat_ref, g, at):
    rows = slice(g * HEAD, (g + 1) * HEAD)
    return stat_ref[2 * g : 2 * g + 1, at], stat_ref[2 * g + 1 : 2 * g + 2, at], acc_ref[rows, at]


def store_state(acc_ref, stat_ref, g, at, state):
    stat_ref[2 * g : 2 * g + 1, at] = state[0]
    stat_ref[2 * g + 1 : 2 * g + 2, at] = state[1]
    acc_ref[g * HEAD : (g + 1) * HEAD, at] = state[2]


def first_kernel(groups, rows, live_ref, q_ref, k_ref, v_ref, stacked, acc, stat):
    n_q, width = q_ref.shape
    heads = width // HEAD // groups
    lanes = heads * n_q
    block = Block([k_ref, v_ref], groups, rows)
    bias = block.bias(lanes, lax.axis_index("ctx") < live_ref[0])
    for g in range(groups):
        q = jnp.concatenate(
            [q_ref[:, (g * heads + h) * HEAD : (g * heads + h + 1) * HEAD].astype(F32) for h in range(heads)], 0
        ).astype(BF16)
        stacked[g * lanes : (g + 1) * lanes, :] = q
        store_state(acc, stat, g, slice(None), attend([block], g, q, [bias])[0])


def state_shapes(groups, lanes):
    return [
        jax.ShapeDtypeStruct((groups * HEAD, lanes), F32),
        jax.ShapeDtypeStruct((2 * groups, lanes), F32),
    ]


def query_first(live_blocks, q, k, v, groups, rows):
    n_q, width = q.shape
    lanes = n_q * width // HEAD // groups
    return pl.pallas_call(
        functools.partial(first_kernel, groups, rows),
        out_shape=[jax.ShapeDtypeStruct((groups * lanes, HEAD), BF16)] + state_shapes(groups, lanes),
        in_specs=[scalar()] + [whole()] * 3,
        out_specs=[whole()] * 3,
        cost_estimate=pl.CostEstimate(flops=0, bytes_accessed=0, transcendentals=0),
        compiler_params=LIMIT,
        name="query_first",
    )(live_blocks, q, k, v)


def query_body(blocks, shifts, n, live_ref, groups, stacked, acc_in, stat_in, acc, stat):
    lanes = stacked.shape[0] // groups
    step = min(lanes, HEAD)
    biases = [block.bias(step, ring_device(n, shift) < live_ref[0]) for block, shift in zip(blocks, shifts)]
    for g in range(groups):
        for first in range(0, lanes, step):
            at = slice(first, first + step)
            q = stacked[g * lanes + first : g * lanes + first + step, :]
            parts = [load_state(acc_in, stat_in, g, at)] + attend(blocks, g, q, biases)
            store_state(acc, stat, g, at, merge(parts))


def more_kernel(groups, rows, parts, shifts, n, live_ref, stacked, acc_in, stat_in, *refs):
    blocks, (acc, stat) = take(refs, parts, groups, rows)
    query_body(blocks, shifts, n, live_ref, groups, stacked, acc_in, stat_in, acc, stat)


def query_more(live_blocks, stacked, acc, stat, pieces, shifts, n, groups, rows):
    operands = [part for piece in pieces for part in piece]
    return pl.pallas_call(
        functools.partial(more_kernel, groups, rows, [len(piece) for piece in pieces], shifts, n),
        out_shape=state_shapes(groups, stacked.shape[0] // groups),
        in_specs=[scalar()] + [whole()] * (3 + len(operands)),
        out_specs=[whole()] * 2,
        input_output_aliases={2: 0, 3: 1},
        compiler_params=LIMIT,
        name="query_more",
    )(live_blocks, stacked, acc, stat, *operands)


def context_body(groups, rows, live_ref, q_ref, anchor, own, o_ref, o_buf, out_sems):
    here = lax.axis_index("ctx")
    share = q_ref.shape[1] // groups
    spans = [pl.ds(g * share, share) for g in range(groups)]
    stores = [pltpu.make_async_copy(o_buf.at[:, at], o_ref.at[:, at], out_sems.at[g]) for g, at in enumerate(spans)]
    key = lax.broadcasted_iota(jnp.int32, (rows, rows), 0)
    row = lax.broadcasted_iota(jnp.int32, (rows, rows), 1)
    see_anchor = anchor.flags() * jnp.where(here > 0, 1.0, 0.0)
    see_own = jnp.where(key < row, own.flags(), jnp.where(key == row, 1.0, 0.0))
    bias = jnp.where(jnp.concatenate([see_anchor, see_own], 0) > 0.5, 0.0, HIDDEN)
    alive = jnp.where(here < live_ref[0], 1.0, 0.0)
    for g in range(groups):
        keys = jnp.concatenate([anchor.keys(g), own.keys(g)], 0)
        values = jnp.concatenate([anchor.values(g), own.values(g)], 1)
        for h in range(share // HEAD):
            at = slice(g * share + h * HEAD, g * share + (h + 1) * HEAD)
            s = lax.dot_general(keys, q_ref[:, at], NT, preferred_element_type=F32)
            s = s + bias
            m = jnp.max(s, axis=0, keepdims=True)
            p = jnp.exp2((s - m) * SCALE)
            l = jnp.sum(p, axis=0, keepdims=True)
            a = jnp.dot(values, p.astype(BF16), preferred_element_type=F32)
            o_buf[:, at] = jnp.transpose((a * (alive / l)).astype(BF16))
        stores[g].start()
    return stores


def both_kernel(groups, rows, devices, parts, shifts, n, aliased, live_ref, stacked, acc_in, stat_in, q_ref, own_k, own_v, *refs):
    blocks, rest = take(refs, parts, groups, rows)
    acc, stat, o_ref, anchor_k, anchor_v, o_buf, out_sems = rest[aliased:]
    here = lax.axis_index("ctx")
    for device, block in zip(devices, blocks):

        @pl.when(here == device)
        def _():
            anchor_k[...] = block.k_ref[...]
            anchor_v[...] = block.v_ref[...]

    mine = functools.reduce(jnp.logical_or, [here == device for device in devices])
    first, own = Block([anchor_k, anchor_v], groups, rows), Block([own_k, own_v], groups, rows)

    @pl.when(mine)
    def _():
        stores = context_body(groups, rows, live_ref, q_ref, first, own, o_ref, o_buf, out_sems)
        query_body(blocks[-len(shifts) :], shifts, n, live_ref, groups, stacked, acc_in, stat_in, acc, stat)
        for store in stores:
            store.wait()

    @pl.when(jnp.logical_not(mine))
    def _():
        query_body(blocks[-len(shifts) :], shifts, n, live_ref, groups, stacked, acc_in, stat_in, acc, stat)


def both(live_blocks, stacked, acc, stat, q, own, anchors, shifts, n, groups, before=None):
    rows = own[0].shape[0]
    devices, pieces = zip(*anchors)
    parts = [len(piece) for piece in pieces]
    operands = [part for piece in pieces for part in piece]
    extra = [] if before is None else [before]
    return pl.pallas_call(
        functools.partial(both_kernel, groups, rows, devices, parts, shifts, n, len(extra)),
        out_shape=state_shapes(groups, stacked.shape[0] // groups) + [jax.ShapeDtypeStruct(q.shape, q.dtype)],
        in_specs=[scalar()] + [whole()] * (6 + len(operands)) + [outside()] * len(extra),
        out_specs=[whole()] * 2 + [outside()],
        input_output_aliases={2: 0, 3: 1} | ({7 + len(operands): 2} if extra else {}),
        scratch_shapes=[
            pltpu.VMEM(own[0].shape, BF16),
            pltpu.VMEM(own[1].shape, BF16),
            pltpu.VMEM(q.shape, q.dtype),
            pltpu.SemaphoreType.DMA((groups,)),
        ],
        compiler_params=LIMIT,
        name="both",
    )(live_blocks, stacked, acc, stat, q, *own, *operands, *extra)


def finish_kernel(
    groups, rows, device, parts, n, live_ref, stacked, acc, stat, q_ref, own_k, own_v, *refs
):
    (block,), rest = take(refs, parts, groups, rows)
    _, query_ref, context_ref, buffer, out_sems, *buffers = rest
    lanes = stacked.shape[0] // groups
    n_q, width = buffer.shape
    heads = width // HEAD // groups
    share = heads * HEAD
    spans = [pl.ds(g * share, share) for g in range(groups)]
    stores = [
        pltpu.make_async_copy(buffer.at[:, at], query_ref.at[:, at], out_sems.at[g]) for g, at in enumerate(spans)
    ]
    bias = block.bias(lanes, ring_device(n, n // 2) < live_ref[0])
    for g in range(groups):
        q = stacked[g * lanes : (g + 1) * lanes, :]
        state = load_state(acc, stat, g, slice(None))
        _, total, part = merge([state] + attend([block], g, q, [bias]))
        out = jnp.transpose(part / total)
        for h in range(heads):
            at = g * share + h * HEAD
            buffer[:, at : at + HEAD] = out[h * n_q : (h + 1) * n_q].astype(BF16)
        stores[g].start()

    @pl.when(lax.axis_index("ctx") == device)
    def _():
        own = Block([own_k, own_v], groups, rows)
        for store in context_body(groups, rows, live_ref, q_ref, block, own, context_ref, *buffers):
            store.wait()

    for store in stores:
        store.wait()


def finish(live_blocks, stacked, acc, stat, q, own, last, n, groups, shape, before):
    rows, width = q.shape
    device, piece = last
    return pl.pallas_call(
        functools.partial(finish_kernel, groups, rows, device, [len(piece)], n),
        out_shape=[shape, jax.ShapeDtypeStruct(q.shape, q.dtype)],
        in_specs=[scalar()] + [whole()] * (6 + len(piece)) + [outside()],
        out_specs=[outside()] * 2,
        input_output_aliases={7 + len(piece): 1},
        scratch_shapes=[
            pltpu.VMEM(shape.shape, shape.dtype),
            pltpu.SemaphoreType.DMA((groups,)),
            pltpu.VMEM(q.shape, q.dtype),
            pltpu.SemaphoreType.DMA((groups,)),
        ],
        compiler_params=LIMIT,
        name="finish",
    )(live_blocks, stacked, acc, stat, q, *own, *piece, before)


def local(context_q, context_k, context_v, question_q, token_mask, live_blocks):
    n = lax.axis_size("ctx")
    rows, width = context_k.shape
    groups = width // HEAD
    ring = list(range(0, n, 2)) + list(range(n - 1, 0, -2))
    forth = [(ring[i], ring[(i + 1) % n]) for i in range(n)]
    back = [(b, a) for a, b in forth]

    half = n // 2

    def send(value, pairs):
        return lax.ppermute(value, "ctx", pairs)

    packed = pack(token_mask, context_v)
    own = (context_k, packed)
    left_k = right_k = context_k
    left_v = right_v = packed
    state = context_output = None
    arrived, anchors = [], [(ring[0], own)]
    for step in range(1, half + 1):
        left_k, right_v = send(left_k, forth), send(right_v, back)
        if step < half:
            left_v, right_k = send(left_v, forth), send(right_k, back)
        pieces = [piece for _, piece in arrived]
        if step == 1:
            state = query_first(live_blocks, question_q, *own, groups, rows)
        elif step < half - 1:
            state = [state[0], *query_more(live_blocks, *state, pieces, (1 - step, step - 1), n, groups, rows)]
        else:
            new = anchors + arrived if step == half - 1 else arrived
            *update, context_output = both(
                live_blocks, *state, context_q, own, new, (1 - step, step - 1), n, groups, context_output
            )
            state = [state[0], *update]
        anchors += arrived
        if step < half:
            right_k, state = lax.optimization_barrier((right_k, state))
            arrived = [(ring[step], (left_k, left_v)), (ring[n - step], (right_k, right_v))]
    left, right = left_k, right_v
    query_output, context_output = finish(
        live_blocks,
        *state,
        context_q,
        own,
        (ring[half], (left, right)),
        n,
        groups,
        jax.ShapeDtypeStruct(question_q.shape, BF16),
        context_output,
    )
    return context_output, query_output


def solution(mesh):
    rows = P(("dp", "ctx"), None)
    return jax.shard_map(
        local,
        mesh=mesh,
        in_specs=(rows, rows, rows, rows, P(("dp", "ctx")), P("dp")),
        out_specs=(rows, rows),
        check_vma=False,
    )
```

time: 33 us -> 32.7 us (level)
  local copies, waits for them, and re-layouts: 0.68 us -> 1.63 us
  Pallas kernels: 7.57 us -> 6.65 us
  waiting for transfers between devices: 9.95 us -> 9.58 us
    pallas_call x3 -> x1, Pallas kernels: 2.54 us -> 0.67 us  [query_more(): pl.pallas_call(functools.partial(more_kernel, groups, rows, [len(piece) f...]
    unnamed x10, local copies, waits for them, and re-layouts: 0.65 us -> 1.6 us
    pallas_call x2, Pallas kernels: 2.91 us -> 3.85 us  [both(): pl.pallas_call(functools.partial(both_kernel, groups, rows, devices, part...]
    ppermute x14, waiting for transfers between devices: 9.95 us -> 9.58 us  [send(): return lax.ppermute(value, 'ctx', pairs)]
  transfers between devices with their start and end apart: 14 -> 14, of which waited for: 9 -> 7; matrix products, arithmetic and copies ran while one was open for 0% -> 0% of each run, Pallas kernels for 19% -> 16%
where the time goes in v5:
time: 32.7 us; the launch traced here: 32.6 us
  starting transfers between devices  13.3 us (41%)
  waiting for transfers between devices  9.58 us (29%)
  Pallas kernels  6.65 us (20%)
  local copies, waits for them, and re-layouts  1.63 us (5%)
  between operations  1.4 us (4%)
    ppermute x14, starting transfers between devices, send(): return lax.ppermute(value, 'ctx', pairs)  13.3 us
    ppermute x14, waiting for transfers between devices, send(): return lax.ppermute(value, 'ctx', pairs)  9.58 us
    pallas_call x2, Pallas kernels, both(): pl.pallas_call(functools.partial(both_kernel, groups, rows, devices, part...  3.85 us
    unnamed x10, local copies, waits for them, and re-layouts  1.6 us
    pallas_call x1, Pallas kernels, finish(): pl.pallas_call(functools.partial(finish_kernel, groups, rows, device, [le...  1.47 us
    pallas_call x1, Pallas kernels, query_more(): pl.pallas_call(functools.partial(more_kernel, groups, rows, [len(piece) f...  0.67 us
    pallas_call x1, Pallas kernels, query_first(): pl.pallas_call(functools.partial(first_kernel, groups, rows), out_shape=[...  0.66 us
  transfers between devices with their start and end apart: 14, of which 7 were waited for; matrix products, arithmetic and copies ran while one was open for 0% of the time, Pallas kernels for 16%

profile of v5, /device:TPU:18, one launch (start us, length us, event | category | flops | bytes accessed | tf_op | source)
XLA Modules:
  0.0 32.6 jit_solution(15649926764440296004)
XLA Ops:
  0.6 0.0 copy-start
  0.6 0.9 %copy-done = bf16[128,512]{1,0:T(8,128)(2,1)S(1)} copy-done((bf16[128,512]{1,0:T(8,128)(2,1)S(1)}, bf16[128,512]{1,0:T(8,128)(2,1)}, u32[]{:S(2)}) %copy-start) | copy-done | bytes 131096
  1.5 0.0 copy-start.3
  1.6 0.0 copy-start.4
  1.6 0.7 %copy-done.4 = s32[128]{0:T(128)S(1)} copy-done((s32[128]{0:T(128)S(1)}, s32[128]{0:T(128)}, u32[]{:S(2)}) %copy-start.4) | copy-done | bytes 536
  2.3 0.0 copy-start.2
  2.3 0.0 copy-start.1
  2.3 1.6 %collective-permute-start.4 = (bf16[528,128]{1,0:T(8,128)(2,1)S(1)}, bf16[528,128]{1,0:T(8,128)(2,1)S(1)}, u32[]{:S(2)}, u32[]{:S(2)}) collective-permute-start(bf16[528,128]{1,0:T(8,128)(2,1)S(1)} %pad_maximum_fusion.v_ref.own_v.refs_1_), channel_id=1, source_target_pairs={{2,0},{4,2},{6,4},{7,6},{5,7},{3,5},{1,3},{0,1},{10,8},{12,10},{14... | collective-permute-start | bytes 405512 | tf_op jit(solution)/shard_map/ppermute | solution.py:322
  3.9 0.0 copy-done.2
  3.9 0.4 %collective-permute-start.2 = (bf16[128,512]{1,0:T(8,128)(2,1)S(1)}, bf16[128,512]{1,0:T(8,128)(2,1)S(1)}, u32[]{:S(2)}, u32[]{:S(2)}) collective-permute-start(bf16[128,512]{1,0:T(8,128)(2,1)S(1)} %copy-done.2), channel_id=1, source_target_pairs={{0,2},{2,4},{4,6},{6,7},{7,5},{5,3},{3,1},{1,0},{8,10},{10,12},{12... | collective-permute-start | bytes 393224 | tf_op jit(solution)/shard_map/ppermute | solution.py:322
  4.4 0.4 %collective-permute-start.3 = (bf16[528,128]{1,0:T(8,128)(2,1)S(1)}, bf16[528,128]{1,0:T(8,128)(2,1)S(1)}, u32[]{:S(2)}, u32[]{:S(2)}) collective-permute-start(bf16[528,128]{1,0:T(8,128)(2,1)S(1)} %pad_maximum_fusion.v_ref.own_v.refs_1_), channel_id=1, source_target_pairs={{0,2},{2,4},{4,6},{6,7},{7,5},{5,3},{3,1},{1,0},{8,10},{10,12},{12... | collective-permute-start | bytes 405512 | tf_op jit(solution)/shard_map/ppermute | solution.py:322
  4.8 2.8 %collective-permute-done.4.refs_3_.refs_5_ = bf16[528,128]{1,0:T(8,128)(2,1)S(1)} collective-permute-done((bf16[528,128]{1,0:T(8,128)(2,1)S(1)}, bf16[528,128]{1,0:T(8,128)(2,1)S(1)}, u32[]{:S(2)}, u32[]{:S(2)}) %collective-permute-start.4) | collective-permute-done | bytes 135200 | tf_op jit(solution)/shard_map/ppermute | solution.py:322
  7.7 1.6 %collective-permute-start.8 = (bf16[528,128]{1,0:T(8,128)(2,1)S(1)}, bf16[528,128]{1,0:T(8,128)(2,1)S(1)}, u32[]{:S(2)}, u32[]{:S(2)}) collective-permute-start(bf16[528,128]{1,0:T(8,128)(2,1)S(1)} %collective-permute-done.4.refs_3_.refs_5_), channel_id=1, source_target_pairs={{2,0},{4,2},{6,4},{7,6},{5,7},{3,5},{1,3},{0,1},{10,8},{12,10},{14... | collective-permute-start | bytes 405512 | tf_op jit(solution)/shard_map/ppermute | solution.py:322
  9.3 0.5 %collective-permute-start = (bf16[128,512]{1,0:T(8,128)(2,1)S(1)}, bf16[128,512]{1,0:T(8,128)(2,1)S(1)}, u32[]{:S(2)}, u32[]{:S(2)}) collective-permute-start(bf16[128,512]{1,0:T(8,128)(2,1)S(1)} %copy-done.2), channel_id=1, source_target_pairs={{2,0},{4,2},{6,4},{7,6},{5,7},{3,5},{1,3},{0,1},{10,8},{12,10},{14... | collective-permute-start | bytes 393224 | tf_op jit(solution)/shard_map/ppermute | solution.py:322
  9.8 0.5 %collective-permute-done.2.refs_0_.refs_2_ = bf16[128,512]{1,0:T(8,128)(2,1)S(1)} collective-permute-done((bf16[128,512]{1,0:T(8,128)(2,1)S(1)}, bf16[128,512]{1,0:T(8,128)(2,1)S(1)}, u32[]{:S(2)}, u32[]{:S(2)}) %collective-permute-start.2) | collective-permute-done | bytes 131104 | tf_op jit(solution)/shard_map/ppermute | solution.py:322
  10.4 0.9 %collective-permute-start.6 = (bf16[128,512]{1,0:T(8,128)(2,1)S(1)}, bf16[128,512]{1,0:T(8,128)(2,1)S(1)}, u32[]{:S(2)}, u32[]{:S(2)}) collective-permute-start(bf16[128,512]{1,0:T(8,128)(2,1)S(1)} %collective-permute-done.2.refs_0_.refs_2_), channel_id=1, source_target_pairs={{0,2},{2,4},{4,6},{6,7},{7,5},{5,3},{3,1},{1,0},{8,10},{10,12},{12... | collective-permute-start | bytes 393224 | tf_op jit(solution)/shard_map/ppermute | solution.py:322
  11.3 1.4 %collective-permute-done.3.refs_1_.refs_3_ = bf16[528,128]{1,0:T(8,128)(2,1)S(1)} collective-permute-done((bf16[528,128]{1,0:T(8,128)(2,1)S(1)}, bf16[528,128]{1,0:T(8,128)(2,1)S(1)}, u32[]{:S(2)}, u32[]{:S(2)}) %collective-permute-start.3) | collective-permute-done | bytes 135200 | tf_op jit(solution)/shard_map/ppermute | solution.py:322
  12.7 0.0 collective-permute-start.7
  12.7 0.9 %collective-permute-done.8.refs_9_ = bf16[528,128]{1,0:T(8,128)(2,1)S(1)} collective-permute-done((bf16[528,128]{1,0:T(8,128)(2,1)S(1)}, bf16[528,128]{1,0:T(8,128)(2,1)S(1)}, u32[]{:S(2)}, u32[]{:S(2)}) %collective-permute-start.8) | collective-permute-done | bytes 135200 | tf_op jit(solution)/shard_map/ppermute | solution.py:322
  13.6 1.6 %collective-permute-start.11 = (bf16[528,128]{1,0:T(8,128)(2,1)S(1)}, bf16[528,128]{1,0:T(8,128)(2,1)S(1)}, u32[]{:S(2)}, u32[]{:S(2)}) collective-permute-start(bf16[528,128]{1,0:T(8,128)(2,1)S(1)} %collective-permute-done.8.refs_9_), channel_id=1, source_target_pairs={{2,0},{4,2},{6,4},{7,6},{5,7},{3,5},{1,3},{0,1},{10,8},{12,10},{14... | collective-permute-start | bytes 405512 | tf_op jit(solution)/shard_map/ppermute | solution.py:322
  15.9 0.0 copy-done.3
  15.9 0.7 %query_first.1 = (bf16[1024,128]{1,0:T(8,128)(2,1)S(1)}, f32[512,256]{1,0:T(8,128)S(1)}, f32[8,256]{1,0:T(8,128)S(1)}) custom-call(s32[1]{0:T(128)S(6)} %copy.27.live_ref, bf16[32,4096]{1,0:T(8,128)(2,1)S(1)} %copy-done.3, bf16[128,512]{1,0:T(8,128)(2,1)S(1)} %copy-done.2, bf16[528,128]{1,0:T(8,128)(2,1)S(1)} %pad_maximum_fusion.v_ref.own_v.refs_1_), custom_call_target="tpu_custom_call" | custom-call | tf_op jit(solution)/shard_map/query_first/pallas_call | solution.py:140
  16.5 0.0 collective-permute-done.refs_2_.refs_4_
  16.5 1.5 %collective-permute-start.1 = (bf16[128,512]{1,0:T(8,128)(2,1)S(1)}, bf16[128,512]{1,0:T(8,128)(2,1)S(1)}, u32[]{:S(2)}, u32[]{:S(2)}) collective-permute-start(bf16[128,512]{1,0:T(8,128)(2,1)S(1)} %collective-permute-done.refs_2_.refs_4_), channel_id=1, source_target_pairs={{2,0},{4,2},{6,4},{7,6},{5,7},{3,5},{1,3},{0,1},{10,8},{12,10},{14... | collective-permute-start | bytes 393224 | tf_op jit(solution)/shard_map/ppermute | solution.py:322
  18.0 0.0 collective-permute-done.6.refs_6_
  18.0 0.6 %collective-permute-start.9 = (bf16[128,512]{1,0:T(8,128)(2,1)S(1)}, bf16[128,512]{1,0:T(8,128)(2,1)S(1)}, u32[]{:S(2)}, u32[]{:S(2)}) collective-permute-start(bf16[128,512]{1,0:T(8,128)(2,1)S(1)} %collective-permute-done.6.refs_6_), channel_id=1, source_target_pairs={{0,2},{2,4},{4,6},{6,7},{7,5},{5,3},{3,1},{1,0},{8,10},{10,12},{12... | collective-permute-start | bytes 393224 | tf_op jit(solution)/shard_map/ppermute | solution.py:322
  18.6 0.0 collective-permute-done.7.refs_7_
  18.6 0.4 %collective-permute-start.10 = (bf16[528,128]{1,0:T(8,128)(2,1)S(1)}, bf16[528,128]{1,0:T(8,128)(2,1)S(1)}, u32[]{:S(2)}, u32[]{:S(2)}) collective-permute-start(bf16[528,128]{1,0:T(8,128)(2,1)S(1)} %collective-permute-done.7.refs_7_), channel_id=1, source_target_pairs={{0,2},{2,4},{4,6},{6,7},{7,5},{5,3},{3,1},{1,0},{8,10},{10,12},{12... | collective-permute-start | bytes 405512 | tf_op jit(solution)/shard_map/ppermute | solution.py:322
  19.1 0.3 collective-permute-done.11.refs_3_
  19.4 1.6 %collective-permute-start.13 = (bf16[528,128]{1,0:T(8,128)(2,1)S(1)}, bf16[528,128]{1,0:T(8,128)(2,1)S(1)}, u32[]{:S(2)}, u32[]{:S(2)}) collective-permute-start(bf16[528,128]{1,0:T(8,128)(2,1)S(1)} %collective-permute-done.11.refs_3_), channel_id=1, source_target_pairs={{2,0},{4,2},{6,4},{7,6},{5,7},{3,5},{1,3},{0,1},{10,8},{12,10},{14... | collective-permute-start | bytes 405512 | tf_op jit(solution)/shard_map/ppermute | solution.py:322
  20.9 0.7 %query_more.1 = (f32[512,256]{1,0:T(8,128)S(1)}, f32[8,256]{1,0:T(8,128)S(1)}) custom-call(s32[1]{0:T(128)S(6)} %copy.27.live_ref, bf16[1024,128]{1,0:T(8,128)(2,1)S(1)} %get-tuple-element.42.stacked, f32[512,256]{1,0:T(8,128)S(1)} %get-tuple-element.32.acc_in, ...), custom_call_target="tpu_custom_call", output_to_operand_aliasing={{0}: (2, {}), {1}: (3, {})} | custom-call | tf_op jit(solution)/shard_map/query_more/pallas_call | solution.py:170
  21.6 1.4 %collective-permute-done.1.refs_8_ = bf16[128,512]{1,0:T(8,128)(2,1)S(1)} collective-permute-done((bf16[128,512]{1,0:T(8,128)(2,1)S(1)}, bf16[128,512]{1,0:T(8,128)(2,1)S(1)}, u32[]{:S(2)}, u32[]{:S(2)}) %collective-permute-start.1) | collective-permute-done | bytes 131104 | tf_op jit(solution)/shard_map/ppermute | solution.py:322
  23.0 1.4 %collective-permute-start.5 = (bf16[128,512]{1,0:T(8,128)(2,1)S(1)}, bf16[128,512]{1,0:T(8,128)(2,1)S(1)}, u32[]{:S(2)}, u32[]{:S(2)}) collective-permute-start(bf16[128,512]{1,0:T(8,128)(2,1)S(1)} %collective-permute-done.1.refs_8_), channel_id=1, source_target_pairs={{2,0},{4,2},{6,4},{7,6},{5,7},{3,5},{1,3},{0,1},{10,8},{12,10},{14... | collective-permute-start | bytes 393224 | tf_op jit(solution)/shard_map/ppermute | solution.py:322
  24.4 0.0 collective-permute-done.9.refs_0_
  24.4 0.6 %collective-permute-start.12 = (bf16[128,512]{1,0:T(8,128)(2,1)S(1)}, bf16[128,512]{1,0:T(8,128)(2,1)S(1)}, u32[]{:S(2)}, u32[]{:S(2)}) collective-permute-start(bf16[128,512]{1,0:T(8,128)(2,1)S(1)} %collective-permute-done.9.refs_0_), channel_id=1, source_target_pairs={{0,2},{2,4},{4,6},{6,7},{7,5},{5,3},{3,1},{1,0},{8,10},{10,12},{12... | collective-permute-start | bytes 393224 | tf_op jit(solution)/shard_map/ppermute | solution.py:322
  25.0 0.0 copy-done.1
  25.0 0.7 %both.2 = (f32[512,256]{1,0:T(8,128)S(1)}, f32[8,256]{1,0:T(8,128)S(1)}, bf16[128,4096]{1,0:T(8,128)(2,1)}) custom-call(s32[1]{0:T(128)S(6)} %copy.27.live_ref, bf16[1024,128]{1,0:T(8,128)(2,1)S(1)} %get-tuple-element.42.stacked, f32[512,256]{1,0:T(8,128)S(1)} %get-tuple-element.38.acc_in, ...), custom_call_target="tpu_custom_call", output_to_operand_aliasing={{0}: (2, {}), {1}: (3, {})} | custom-call | tf_op jit(solution)/shard_map/both/pallas_call | solution.py:240
  25.7 2.2 %collective-permute-done.5.refs_2_ = bf16[128,512]{1,0:T(8,128)(2,1)S(1)} collective-permute-done((bf16[128,512]{1,0:T(8,128)(2,1)S(1)}, bf16[128,512]{1,0:T(8,128)(2,1)S(1)}, u32[]{:S(2)}, u32[]{:S(2)}) %collective-permute-start.5) | collective-permute-done | bytes 131104 | tf_op jit(solution)/shard_map/ppermute | solution.py:322
  27.9 0.0 collective-permute-done.10.refs_1_
  28.0 3.1 %both.3 = (f32[512,256]{1,0:T(8,128)S(1)}, f32[8,256]{1,0:T(8,128)S(1)}, bf16[128,4096]{1,0:T(8,128)(2,1)}) custom-call(s32[1]{0:T(128)S(6)} %copy.27.live_ref, bf16[1024,128]{1,0:T(8,128)(2,1)S(1)} %get-tuple-element.42.stacked, f32[512,256]{1,0:T(8,128)S(1)} %get-tuple-element.43.acc_in, ...), custom_call_target="tpu_custom_call", output_to_operand_aliasing={{0}: (2, {}), {1}: (3, {}), {2}: (11, {})} | custom-call | tf_op jit(solution)/shard_map/both/pallas_call | solution.py:240
  31.1 0.0 collective-permute-done.12.refs_0_
  31.1 0.0 collective-permute-done.13.refs_1_
  31.1 1.5 %finish.1 = (bf16[32,4096]{1,0:T(8,128)(2,1)}, bf16[128,4096]{1,0:T(8,128)(2,1)}) custom-call(s32[1]{0:T(128)S(6)} %copy.27.live_ref, bf16[1024,128]{1,0:T(8,128)(2,1)S(1)} %get-tuple-element.42.stacked, f32[512,256]{1,0:T(8,128)S(1)} %get-tuple-element.47.acc, f32[8,256]{1,0:T(8,128)S(1)} %get-tuple-element.48.stat, ...), custom_call_target="tpu_custom_call", output_to_operand_aliasing={{1}: (9, {})} | custom-call | tf_op jit(solution)/shard_map/finish/pallas_call | solution.py:294
  (4 shorter events, 0.0 us)
Async XLA Ops:
  0.6 0.9 %copy-start = (bf16[128,512]{1,0:T(8,128)(2,1)S(1)}, bf16[128,512]{1,0:T(8,128)(2,1)}, u32[]{:S(2)}) copy-start(bf16[128,512]{1,0:T(8,128)(2,1)} %param.8) | copy-start | bytes 393220
  1.5 14.3 %copy-start.3 = (bf16[32,4096]{1,0:T(8,128)(2,1)S(1)}, bf16[32,4096]{1,0:T(8,128)(2,1)}, u32[]{:S(2)}) copy-start(bf16[32,4096]{1,0:T(8,128)(2,1)} %q_ref.4) | copy-start | bytes 786436
  1.6 0.7 %copy-start.4 = (s32[128]{0:T(128)S(1)}, s32[128]{0:T(128)}, u32[]{:S(2)}) copy-start(s32[128]{0:T(128)} %param.10) | copy-start | bytes 1540
  2.3 1.7 %copy-start.2 = (bf16[128,512]{1,0:T(8,128)(2,1)S(1)}, bf16[128,512]{1,0:T(8,128)(2,1)}, u32[]{:S(2)}) copy-start(bf16[128,512]{1,0:T(8,128)(2,1)} %own_k.5) | copy-start | bytes 393220
  2.3 22.7 %copy-start.1 = (bf16[128,4096]{1,0:T(8,128)(2,1)S(1)}, bf16[128,4096]{1,0:T(8,128)(2,1)}, u32[]{:S(2)}) copy-start(bf16[128,4096]{1,0:T(8,128)(2,1)} %q_ref.7) | copy-start | bytes 3145732
  2.3 5.4 %collective-permute-start.4 = (bf16[528,128]{1,0:T(8,128)(2,1)S(1)}, bf16[528,128]{1,0:T(8,128)(2,1)S(1)}, u32[]{:S(2)}, u32[]{:S(2)}) collective-permute-start(bf16[528,128]{1,0:T(8,128)(2,1)S(1)} %pad_maximum_fusion.v_ref.own_v.refs_1_), channel_id=1, source_target_pairs={{2,0},{4,2},{6,4},{7,6},{5,7},{3,5},{1,3},{0,1},{10,8},{12,10},{14... | collective-permute-start | bytes 405512 | tf_op jit(solution)/shard_map/ppermute | solution.py:322
  3.9 6.4 %collective-permute-start.2 = (bf16[128,512]{1,0:T(8,128)(2,1)S(1)}, bf16[128,512]{1,0:T(8,128)(2,1)S(1)}, u32[]{:S(2)}, u32[]{:S(2)}) collective-permute-start(bf16[128,512]{1,0:T(8,128)(2,1)S(1)} %copy-done.2), channel_id=1, source_target_pairs={{0,2},{2,4},{4,6},{6,7},{7,5},{5,3},{3,1},{1,0},{8,10},{10,12},{12... | collective-permute-start | bytes 393224 | tf_op jit(solution)/shard_map/ppermute | solution.py:322
  4.4 8.3 %collective-permute-start.3 = (bf16[528,128]{1,0:T(8,128)(2,1)S(1)}, bf16[528,128]{1,0:T(8,128)(2,1)S(1)}, u32[]{:S(2)}, u32[]{:S(2)}) collective-permute-start(bf16[528,128]{1,0:T(8,128)(2,1)S(1)} %pad_maximum_fusion.v_ref.own_v.refs_1_), channel_id=1, source_target_pairs={{0,2},{2,4},{4,6},{6,7},{7,5},{5,3},{3,1},{1,0},{8,10},{10,12},{12... | collective-permute-start | bytes 405512 | tf_op jit(solution)/shard_map/ppermute | solution.py:322
  7.7 5.9 %collective-permute-start.8 = (bf16[528,128]{1,0:T(8,128)(2,1)S(1)}, bf16[528,128]{1,0:T(8,128)(2,1)S(1)}, u32[]{:S(2)}, u32[]{:S(2)}) collective-permute-start(bf16[528,128]{1,0:T(8,128)(2,1)S(1)} %collective-permute-done.4.refs_3_.refs_5_), channel_id=1, source_target_pairs={{2,0},{4,2},{6,4},{7,6},{5,7},{3,5},{1,3},{0,1},{10,8},{12,10},{14... | collective-permute-start | bytes 405512 | tf_op jit(solution)/shard_map/ppermute | solution.py:322
  9.3 7.3 %collective-permute-start = (bf16[128,512]{1,0:T(8,128)(2,1)S(1)}, bf16[128,512]{1,0:T(8,128)(2,1)S(1)}, u32[]{:S(2)}, u32[]{:S(2)}) collective-permute-start(bf16[128,512]{1,0:T(8,128)(2,1)S(1)} %copy-done.2), channel_id=1, source_target_pairs={{2,0},{4,2},{6,4},{7,6},{5,7},{3,5},{1,3},{0,1},{10,8},{12,10},{14... | collective-permute-start | bytes 393224 | tf_op jit(solution)/shard_map/ppermute | solution.py:322
  10.4 7.7 %collective-permute-start.6 = (bf16[128,512]{1,0:T(8,128)(2,1)S(1)}, bf16[128,512]{1,0:T(8,128)(2,1)S(1)}, u32[]{:S(2)}, u32[]{:S(2)}) collective-permute-start(bf16[128,512]{1,0:T(8,128)(2,1)S(1)} %collective-permute-done.2.refs_0_.refs_2_), channel_id=1, source_target_pairs={{0,2},{2,4},{4,6},{6,7},{7,5},{5,3},{3,1},{1,0},{8,10},{10,12},{12... | collective-permute-start | bytes 393224 | tf_op jit(solution)/shard_map/ppermute | solution.py:322
  12.7 5.9 %collective-permute-start.7 = (bf16[528,128]{1,0:T(8,128)(2,1)S(1)}, bf16[528,128]{1,0:T(8,128)(2,1)S(1)}, u32[]{:S(2)}, u32[]{:S(2)}) collective-permute-start(bf16[528,128]{1,0:T(8,128)(2,1)S(1)} %collective-permute-done.3.refs_1_.refs_3_), channel_id=1, source_target_pairs={{0,2},{2,4},{4,6},{6,7},{7,5},{5,3},{3,1},{1,0},{8,10},{10,12},{12... | collective-permute-start | bytes 405512 | tf_op jit(solution)/shard_map/ppermute | solution.py:322
  13.6 5.7 %collective-permute-start.11 = (bf16[528,128]{1,0:T(8,128)(2,1)S(1)}, bf16[528,128]{1,0:T(8,128)(2,1)S(1)}, u32[]{:S(2)}, u32[]{:S(2)}) collective-permute-start(bf16[528,128]{1,0:T(8,128)(2,1)S(1)} %collective-permute-done.8.refs_9_), channel_id=1, source_target_pairs={{2,0},{4,2},{6,4},{7,6},{5,7},{3,5},{1,3},{0,1},{10,8},{12,10},{14... | collective-permute-start | bytes 405512 | tf_op jit(solution)/shard_map/ppermute | solution.py:322
  16.5 6.4 %collective-permute-start.1 = (bf16[128,512]{1,0:T(8,128)(2,1)S(1)}, bf16[128,512]{1,0:T(8,128)(2,1)S(1)}, u32[]{:S(2)}, u32[]{:S(2)}) collective-permute-start(bf16[128,512]{1,0:T(8,128)(2,1)S(1)} %collective-permute-done.refs_2_.refs_4_), channel_id=1, source_target_pairs={{2,0},{4,2},{6,4},{7,6},{5,7},{3,5},{1,3},{0,1},{10,8},{12,10},{14... | collective-permute-start | bytes 393224 | tf_op jit(solution)/shard_map/ppermute | solution.py:322
  18.0 6.4 %collective-permute-start.9 = (bf16[128,512]{1,0:T(8,128)(2,1)S(1)}, bf16[128,512]{1,0:T(8,128)(2,1)S(1)}, u32[]{:S(2)}, u32[]{:S(2)}) collective-permute-start(bf16[128,512]{1,0:T(8,128)(2,1)S(1)} %collective-permute-done.6.refs_6_), channel_id=1, source_target_pairs={{0,2},{2,4},{4,6},{6,7},{7,5},{5,3},{3,1},{1,0},{8,10},{10,12},{12... | collective-permute-start | bytes 393224 | tf_op jit(solution)/shard_map/ppermute | solution.py:322
  18.6 9.3 %collective-permute-start.10 = (bf16[528,128]{1,0:T(8,128)(2,1)S(1)}, bf16[528,128]{1,0:T(8,128)(2,1)S(1)}, u32[]{:S(2)}, u32[]{:S(2)}) collective-permute-start(bf16[528,128]{1,0:T(8,128)(2,1)S(1)} %collective-permute-done.7.refs_7_), channel_id=1, source_target_pairs={{0,2},{2,4},{4,6},{6,7},{7,5},{5,3},{3,1},{1,0},{8,10},{10,12},{12... | collective-permute-start | bytes 405512 | tf_op jit(solution)/shard_map/ppermute | solution.py:322
  19.4 11.7 %collective-permute-start.13 = (bf16[528,128]{1,0:T(8,128)(2,1)S(1)}, bf16[528,128]{1,0:T(8,128)(2,1)S(1)}, u32[]{:S(2)}, u32[]{:S(2)}) collective-permute-start(bf16[528,128]{1,0:T(8,128)(2,1)S(1)} %collective-permute-done.11.refs_3_), channel_id=1, source_target_pairs={{2,0},{4,2},{6,4},{7,6},{5,7},{3,5},{1,3},{0,1},{10,8},{12,10},{14... | collective-permute-start | bytes 405512 | tf_op jit(solution)/shard_map/ppermute | solution.py:322
  23.0 5.0 %collective-permute-start.5 = (bf16[128,512]{1,0:T(8,128)(2,1)S(1)}, bf16[128,512]{1,0:T(8,128)(2,1)S(1)}, u32[]{:S(2)}, u32[]{:S(2)}) collective-permute-start(bf16[128,512]{1,0:T(8,128)(2,1)S(1)} %collective-permute-done.1.refs_8_), channel_id=1, source_target_pairs={{2,0},{4,2},{6,4},{7,6},{5,7},{3,5},{1,3},{0,1},{10,8},{12,10},{14... | collective-permute-start | bytes 393224 | tf_op jit(solution)/shard_map/ppermute | solution.py:322
  24.4 6.7 %collective-permute-start.12 = (bf16[128,512]{1,0:T(8,128)(2,1)S(1)}, bf16[128,512]{1,0:T(8,128)(2,1)S(1)}, u32[]{:S(2)}, u32[]{:S(2)}) collective-permute-start(bf16[128,512]{1,0:T(8,128)(2,1)S(1)} %collective-permute-done.9.refs_0_), channel_id=1, source_target_pairs={{0,2},{2,4},{4,6},{6,7},{7,5},{5,3},{3,1},{1,0},{8,10},{10,12},{12... | collective-permute-start | bytes 393224 | tf_op jit(solution)/shard_map/ppermute | solution.py:322

commit v6 on v5

--- a/solution.py
+++ b/solution.py
@@ -78,8 +78,27 @@
     block = lax.axis_index("ctx")
     token = lax.broadcasted_iota(jnp.int32, (FLAG_ROWS, rows), 1)
     flags = ((token_mask[None, :] != 0) | ((block == 0) & (token == 0))).astype(BF16)
+    v, flags = lax.optimization_barrier((v, flags))
     by_head = v.reshape(rows, groups, HEAD).transpose(1, 0, 2).reshape(groups * rows, HEAD)
     return jnp.concatenate([by_head, flags], 0)
+
+
+def by_head_kernel(x_ref, o_ref):
+    rows, width = x_ref.shape
+    for g in range(width // HEAD):
+        o_ref[g * rows : (g + 1) * rows, :] = x_ref[:, g * HEAD : (g + 1) * HEAD]
+
+
+def by_head(x):
+    return pl.pallas_call(
+        by_head_kernel,
+        out_shape=jax.ShapeDtypeStruct((x.size // HEAD, HEAD), BF16),
+        in_specs=[whole()],
+        out_specs=whole(),
+        cost_estimate=pl.CostEstimate(flops=4 * 10**9, bytes_accessed=0, transcendentals=0),
+        compiler_params=LIMIT,
+        name="by_head",
+    )(x)
 
 
 def attend(blocks, g, q, biases):
@@ -213,7 +232,7 @@
 
         @pl.when(here == device)
         def _():
-            anchor_k[...] = block.k_ref[...]
+            anchor_k[...] = jnp.concatenate([block.keys(g) for g in range(groups)], 0)
             anchor_v[...] = block.v_ref[...]
 
     mine = functools.reduce(jnp.logical_or, [here == device for device in devices])
@@ -244,7 +263,7 @@
         out_specs=[whole()] * 2 + [outside()],
         input_output_aliases={2: 0, 3: 1} | ({7 + len(operands): 2} if extra else {}),
         scratch_shapes=[
-            pltpu.VMEM(own[0].shape, BF16),
+            pltpu.VMEM((own[0].size // HEAD, HEAD), BF16),
             pltpu.VMEM(own[1].shape, BF16),
             pltpu.VMEM(q.shape, q.dtype),
             pltpu.SemaphoreType.DMA((groups,)),
@@ -272,7 +291,8 @@
         q = stacked[g * lanes : (g + 1) * lanes, :]
         state = load_state(acc, stat, g, slice(None))
         _, total, part = merge([state] + attend([block], g, q, [bias]))
-        out = jnp.transpose(part / total)
+        out = part * (1.0 / total)
+        out = jnp.transpose(out.astype(BF16)) if n_q % 16 == 0 else jnp.transpose(out)
         for h in range(heads):
             at = g * share + h * HEAD
             buffer[:, at : at + HEAD] = out[h * n_q : (h + 1) * n_q].astype(BF16)
@@ -344,6 +364,9 @@
             state = [state[0], *update]
         anchors += arrived
         if step < half:
+            if step == 1:
+                left_k = by_head(left_k)
+                right_k = by_head(right_k)
             right_k, state = lax.optimization_barrier((right_k, state))
             arrived = [(ring[step], (left_k, left_v)), (ring[n - step], (right_k, right_v))]
     left, right = left_k, right_v

time: 32.7 us -> 31.2 us (0.954)
  waiting for transfers between devices: 9.58 us -> 7.59 us
  starting transfers between devices: 13.3 us -> 14.4 us
  local copies, waits for them, and re-layouts: 1.63 us -> 0.94 us
    ppermute x14, waiting for transfers between devices: 9.58 us -> 7.59 us  [send(): return lax.ppermute(value, 'ctx', pairs)]
    ppermute x14, starting transfers between devices: 13.3 us -> 14.4 us  [send(): return lax.ppermute(value, 'ctx', pairs)]
    unnamed x10, local copies, waits for them, and re-layouts: 1.6 us -> 0.91 us
  transfers between devices with their start and end apart: 14 -> 14, of which waited for: 7 -> 5; matrix products, arithmetic and copies ran while one was open for 0% -> 0% of each run, Pallas kernels for 16% -> 17%
where the time goes in v6:
time: 31.2 us; the launch traced here: 31 us
  starting transfers between devices  14.4 us (46%)
  waiting for transfers between devices  7.59 us (24%)
  Pallas kernels  6.69 us (21%)
  between operations  1.41 us (5%)
  local copies, waits for them, and re-layouts  0.94 us (3%)
    ppermute x14, starting transfers between devices, send(): return lax.ppermute(value, 'ctx', pairs)  14.4 us
    ppermute x14, waiting for transfers between devices, send(): return lax.ppermute(value, 'ctx', pairs)  7.59 us
    pallas_call x2, Pallas kernels, both(): pl.pallas_call(functools.partial(both_kernel, groups, rows, devices, part...  3.86 us
    pallas_call x1, Pallas kernels, finish(): pl.pallas_call(functools.partial(finish_kernel, groups, rows, device, [le...  1.44 us
    unnamed x10, local copies, waits for them, and re-layouts  0.91 us
    pallas_call x1, Pallas kernels, query_more(): pl.pallas_call(functools.partial(more_kernel, groups, rows, [len(piece) f...  0.68 us
    pallas_call x1, Pallas kernels, query_first(): pl.pallas_call(functools.partial(first_kernel, groups, rows), out_shape=[...  0.66 us
  transfers between devices with their start and end apart: 14, of which 5 were waited for; matrix products, arithmetic and copies ran while one was open for 0% of the time, Pallas kernels for 17%

profile of v6, /device:TPU:18, one launch (start us, length us, event | category | flops | bytes accessed | tf_op | source)
XLA Modules:
  0.0 31.0 jit_solution(1757762490928420561)
XLA Ops:
  0.6 0.0 copy-start
  0.6 0.0 copy-start.4
  0.7 0.7 %copy-done.4 = s32[128]{0:T(128)S(1)} copy-done((s32[128]{0:T(128)S(1)}, s32[128]{0:T(128)}, u32[]{:S(2)}) %copy-start.4) | copy-done | bytes 536
  1.4 0.2 copy-done
  1.6 0.0 copy-start.3
  1.6 0.0 copy-start.2
  1.6 1.6 %collective-permute-start.4 = (bf16[528,128]{1,0:T(8,128)(2,1)S(1)}, bf16[528,128]{1,0:T(8,128)(2,1)S(1)}, u32[]{:S(2)}, u32[]{:S(2)}) collective-permute-start(bf16[528,128]{1,0:T(8,128)(2,1)S(1)} %pad_maximum_fusion.v_ref.own_v.refs_1_), channel_id=1, source_target_pairs={{2,0},{4,2},{6,4},{7,6},{5,7},{3,5},{1,3},{0,1},{10,8},{12,10},{14... | collective-permute-start | bytes 405512 | tf_op jit(solution)/shard_map/ppermute | solution.py:342
  3.2 0.0 copy-done.2
  3.2 0.4 %collective-permute-start.2 = (bf16[128,512]{1,0:T(8,128)(2,1)S(1)}, bf16[128,512]{1,0:T(8,128)(2,1)S(1)}, u32[]{:S(2)}, u32[]{:S(2)}) collective-permute-start(bf16[128,512]{1,0:T(8,128)(2,1)S(1)} %copy-done.2), channel_id=1, source_target_pairs={{0,2},{2,4},{4,6},{6,7},{7,5},{5,3},{3,1},{1,0},{8,10},{10,12},{12... | collective-permute-start | bytes 393224 | tf_op jit(solution)/shard_map/ppermute | solution.py:342
  3.7 1.6 %collective-permute-start = (bf16[128,512]{1,0:T(8,128)(2,1)S(1)}, bf16[128,512]{1,0:T(8,128)(2,1)S(1)}, u32[]{:S(2)}, u32[]{:S(2)}) collective-permute-start(bf16[128,512]{1,0:T(8,128)(2,1)S(1)} %copy-done.2), channel_id=1, source_target_pairs={{2,0},{4,2},{6,4},{7,6},{5,7},{3,5},{1,3},{0,1},{10,8},{12,10},{14... | collective-permute-start | bytes 393224 | tf_op jit(solution)/shard_map/ppermute | solution.py:342
  5.3 0.4 %collective-permute-start.3 = (bf16[528,128]{1,0:T(8,128)(2,1)S(1)}, bf16[528,128]{1,0:T(8,128)(2,1)S(1)}, u32[]{:S(2)}, u32[]{:S(2)}) collective-permute-start(bf16[528,128]{1,0:T(8,128)(2,1)S(1)} %pad_maximum_fusion.v_ref.own_v.refs_1_), channel_id=1, source_target_pairs={{0,2},{2,4},{4,6},{6,7},{7,5},{5,3},{3,1},{1,0},{8,10},{10,12},{12... | collective-permute-start | bytes 405512 | tf_op jit(solution)/shard_map/ppermute | solution.py:342
  6.4 0.0 copy-done.3
  6.4 0.7 %query_first.1 = (bf16[1024,128]{1,0:T(8,128)(2,1)S(1)}, f32[512,256]{1,0:T(8,128)S(1)}, f32[8,256]{1,0:T(8,128)S(1)}) custom-call(s32[1]{0:T(128)S(6)} %copy.27.live_ref, bf16[32,4096]{1,0:T(8,128)(2,1)S(1)} %copy-done.3, bf16[128,512]{1,0:T(8,128)(2,1)S(1)} %copy-done.2, bf16[528,128]{1,0:T(8,128)(2,1)S(1)} %pad_maximum_fusion.v_ref.own_v.refs_1_), custom_call_target="tpu_custom_call" | custom-call | tf_op jit(solution)/shard_map/query_first/pallas_call | solution.py:159
  7.1 1.1 %collective-permute-done.4.refs_3_.refs_5_ = bf16[528,128]{1,0:T(8,128)(2,1)S(1)} collective-permute-done((bf16[528,128]{1,0:T(8,128)(2,1)S(1)}, bf16[528,128]{1,0:T(8,128)(2,1)S(1)}, u32[]{:S(2)}, u32[]{:S(2)}) %collective-permute-start.4) | collective-permute-done | bytes 135200 | tf_op jit(solution)/shard_map/ppermute | solution.py:342
  8.1 1.6 %collective-permute-start.8 = (bf16[528,128]{1,0:T(8,128)(2,1)S(1)}, bf16[528,128]{1,0:T(8,128)(2,1)S(1)}, u32[]{:S(2)}, u32[]{:S(2)}) collective-permute-start(bf16[528,128]{1,0:T(8,128)(2,1)S(1)} %collective-permute-done.4.refs_3_.refs_5_), channel_id=1, source_target_pairs={{2,0},{4,2},{6,4},{7,6},{5,7},{3,5},{1,3},{0,1},{10,8},{12,10},{14... | collective-permute-start | bytes 405512 | tf_op jit(solution)/shard_map/ppermute | solution.py:342
  9.7 0.0 collective-permute-done.2.x_ref
  9.7 0.5 %collective-permute-start.6 = (bf16[512,128]{1,0:T(8,128)(2,1)S(1)}, bf16[512,128]{1,0:T(8,128)(2,1)S(1)}, u32[]{:S(2)}, u32[]{:S(2)}) collective-permute-start(bf16[512,128]{1,0:T(8,128)(2,1)S(1)} %by_head.3.refs_0_.refs_2_), channel_id=1, source_target_pairs={{0,2},{2,4},{4,6},{6,7},{7,5},{5,3},{3,1},{1,0},{8,10},{10,12},{12... | collective-permute-start | bytes 393224 | tf_op jit(solution)/shard_map/ppermute | solution.py:342
  10.3 2.0 %collective-permute-done.3.refs_1_.refs_3_ = bf16[528,128]{1,0:T(8,128)(2,1)S(1)} collective-permute-done((bf16[528,128]{1,0:T(8,128)(2,1)S(1)}, bf16[528,128]{1,0:T(8,128)(2,1)S(1)}, u32[]{:S(2)}, u32[]{:S(2)}) %collective-permute-start.3) | collective-permute-done | bytes 135200 | tf_op jit(solution)/shard_map/ppermute | solution.py:342
  12.2 0.4 %collective-permute-start.7 = (bf16[528,128]{1,0:T(8,128)(2,1)S(1)}, bf16[528,128]{1,0:T(8,128)(2,1)S(1)}, u32[]{:S(2)}, u32[]{:S(2)}) collective-permute-start(bf16[528,128]{1,0:T(8,128)(2,1)S(1)} %collective-permute-done.3.refs_1_.refs_3_), channel_id=1, source_target_pairs={{0,2},{2,4},{4,6},{6,7},{7,5},{5,3},{3,1},{1,0},{8,10},{10,12},{12... | collective-permute-start | bytes 405512 | tf_op jit(solution)/shard_map/ppermute | solution.py:342
  12.7 0.5 %collective-permute-done.8.refs_9_ = bf16[528,128]{1,0:T(8,128)(2,1)S(1)} collective-permute-done((bf16[528,128]{1,0:T(8,128)(2,1)S(1)}, bf16[528,128]{1,0:T(8,128)(2,1)S(1)}, u32[]{:S(2)}, u32[]{:S(2)}) %collective-permute-start.8) | collective-permute-done | bytes 135200 | tf_op jit(solution)/shard_map/ppermute | solution.py:342
  13.2 1.6 %collective-permute-start.11 = (bf16[528,128]{1,0:T(8,128)(2,1)S(1)}, bf16[528,128]{1,0:T(8,128)(2,1)S(1)}, u32[]{:S(2)}, u32[]{:S(2)}) collective-permute-start(bf16[528,128]{1,0:T(8,128)(2,1)S(1)} %collective-permute-done.8.refs_9_), channel_id=1, source_target_pairs={{2,0},{4,2},{6,4},{7,6},{5,7},{3,5},{1,3},{0,1},{10,8},{12,10},{14... | collective-permute-start | bytes 405512 | tf_op jit(solution)/shard_map/ppermute | solution.py:342
  14.7 0.0 collective-permute-done.x_ref
  14.8 0.0 copy-start.1
  14.8 0.8 %collective-permute-start.1 = (bf16[512,128]{1,0:T(8,128)(2,1)S(1)}, bf16[512,128]{1,0:T(8,128)(2,1)S(1)}, u32[]{:S(2)}, u32[]{:S(2)}) collective-permute-start(bf16[512,128]{1,0:T(8,128)(2,1)S(1)} %by_head.2.refs_2_.refs_4_), channel_id=1, source_target_pairs={{2,0},{4,2},{6,4},{7,6},{5,7},{3,5},{1,3},{0,1},{10,8},{12,10},{14... | collective-permute-start | bytes 393224 | tf_op jit(solution)/shard_map/ppermute | solution.py:342
  15.5 0.0 collective-permute-done.6.refs_6_
  15.5 1.3 %collective-permute-start.9 = (bf16[512,128]{1,0:T(8,128)(2,1)S(1)}, bf16[512,128]{1,0:T(8,128)(2,1)S(1)}, u32[]{:S(2)}, u32[]{:S(2)}) collective-permute-start(bf16[512,128]{1,0:T(8,128)(2,1)S(1)} %collective-permute-done.6.refs_6_), channel_id=1, source_target_pairs={{0,2},{2,4},{4,6},{6,7},{7,5},{5,3},{3,1},{1,0},{8,10},{10,12},{12... | collective-permute-start | bytes 393224 | tf_op jit(solution)/shard_map/ppermute | solution.py:342
  16.9 1.8 %collective-permute-done.7.refs_7_ = bf16[528,128]{1,0:T(8,128)(2,1)S(1)} collective-permute-done((bf16[528,128]{1,0:T(8,128)(2,1)S(1)}, bf16[528,128]{1,0:T(8,128)(2,1)S(1)}, u32[]{:S(2)}, u32[]{:S(2)}) %collective-permute-start.7) | collective-permute-done | bytes 135200 | tf_op jit(solution)/shard_map/ppermute | solution.py:342
  18.7 0.0 collective-permute-start.10
  18.7 0.0 collective-permute-done.11.refs_3_
  18.7 2.0 %collective-permute-start.13 = (bf16[528,128]{1,0:T(8,128)(2,1)S(1)}, bf16[528,128]{1,0:T(8,128)(2,1)S(1)}, u32[]{:S(2)}, u32[]{:S(2)}) collective-permute-start(bf16[528,128]{1,0:T(8,128)(2,1)S(1)} %collective-permute-done.11.refs_3_), channel_id=1, source_target_pairs={{2,0},{4,2},{6,4},{7,6},{5,7},{3,5},{1,3},{0,1},{10,8},{12,10},{14... | collective-permute-start | bytes 405512 | tf_op jit(solution)/shard_map/ppermute | solution.py:342
  20.7 0.7 %query_more.1 = (f32[512,256]{1,0:T(8,128)S(1)}, f32[8,256]{1,0:T(8,128)S(1)}) custom-call(s32[1]{0:T(128)S(6)} %copy.27.live_ref, bf16[1024,128]{1,0:T(8,128)(2,1)S(1)} %get-tuple-element.46.stacked, f32[512,256]{1,0:T(8,128)S(1)} %get-tuple-element.36.acc_in, ...), custom_call_target="tpu_custom_call", output_to_operand_aliasing={{0}: (2, {}), {1}: (3, {})} | custom-call | tf_op jit(solution)/shard_map/query_more/pallas_call | solution.py:189
  21.4 0.0 collective-permute-done.1.refs_8_
  21.4 1.4 %collective-permute-start.5 = (bf16[512,128]{1,0:T(8,128)(2,1)S(1)}, bf16[512,128]{1,0:T(8,128)(2,1)S(1)}, u32[]{:S(2)}, u32[]{:S(2)}) collective-permute-start(bf16[512,128]{1,0:T(8,128)(2,1)S(1)} %collective-permute-done.1.refs_8_), channel_id=1, source_target_pairs={{2,0},{4,2},{6,4},{7,6},{5,7},{3,5},{1,3},{0,1},{10,8},{12,10},{14... | collective-permute-start | bytes 393224 | tf_op jit(solution)/shard_map/ppermute | solution.py:342
  22.8 0.0 collective-permute-done.9.refs_0_
  22.8 0.7 %collective-permute-start.12 = (bf16[512,128]{1,0:T(8,128)(2,1)S(1)}, bf16[512,128]{1,0:T(8,128)(2,1)S(1)}, u32[]{:S(2)}, u32[]{:S(2)}) collective-permute-start(bf16[512,128]{1,0:T(8,128)(2,1)S(1)} %collective-permute-done.9.refs_0_), channel_id=1, source_target_pairs={{0,2},{2,4},{4,6},{6,7},{7,5},{5,3},{3,1},{1,0},{8,10},{10,12},{12... | collective-permute-start | bytes 393224 | tf_op jit(solution)/shard_map/ppermute | solution.py:342
  23.5 0.0 copy-done.1
  23.5 0.7 %both.2 = (f32[512,256]{1,0:T(8,128)S(1)}, f32[8,256]{1,0:T(8,128)S(1)}, bf16[128,4096]{1,0:T(8,128)(2,1)}) custom-call(s32[1]{0:T(128)S(6)} %copy.27.live_ref, bf16[1024,128]{1,0:T(8,128)(2,1)S(1)} %get-tuple-element.46.stacked, f32[512,256]{1,0:T(8,128)S(1)} %get-tuple-element.42.acc_in, ...), custom_call_target="tpu_custom_call", output_to_operand_aliasing={{0}: (2, {}), {1}: (3, {})} | custom-call | tf_op jit(solution)/shard_map/both/pallas_call | solution.py:259
  24.2 2.2 %collective-permute-done.5.refs_2_ = bf16[512,128]{1,0:T(8,128)(2,1)S(1)} collective-permute-done((bf16[512,128]{1,0:T(8,128)(2,1)S(1)}, bf16[512,128]{1,0:T(8,128)(2,1)S(1)}, u32[]{:S(2)}, u32[]{:S(2)}) %collective-permute-start.5) | collective-permute-done | bytes 131104 | tf_op jit(solution)/shard_map/ppermute | solution.py:342
  26.4 0.0 collective-permute-done.10.refs_1_
  26.4 3.1 %both.3 = (f32[512,256]{1,0:T(8,128)S(1)}, f32[8,256]{1,0:T(8,128)S(1)}, bf16[128,4096]{1,0:T(8,128)(2,1)}) custom-call(s32[1]{0:T(128)S(6)} %copy.27.live_ref, bf16[1024,128]{1,0:T(8,128)(2,1)S(1)} %get-tuple-element.46.stacked, f32[512,256]{1,0:T(8,128)S(1)} %get-tuple-element.47.acc_in, ...), custom_call_target="tpu_custom_call", output_to_operand_aliasing={{0}: (2, {}), {1}: (3, {}), {2}: (11, {})} | custom-call | tf_op jit(solution)/shard_map/both/pallas_call | solution.py:259
  29.6 0.0 collective-permute-done.12.refs_0_
  29.6 0.0 collective-permute-done.13.refs_1_
  29.6 1.4 %finish.1 = (bf16[32,4096]{1,0:T(8,128)(2,1)}, bf16[128,4096]{1,0:T(8,128)(2,1)}) custom-call(s32[1]{0:T(128)S(6)} %copy.27.live_ref, bf16[1024,128]{1,0:T(8,128)(2,1)S(1)} %get-tuple-element.46.stacked, f32[512,256]{1,0:T(8,128)S(1)} %get-tuple-element.51.acc, f32[8,256]{1,0:T(8,128)S(1)} %get-tuple-element.52.stat, ...), custom_call_target="tpu_custom_call", output_to_operand_aliasing={{1}: (9, {})} | custom-call | tf_op jit(solution)/shard_map/finish/pallas_call | solution.py:314
  (6 shorter events, 0.1 us)
Async XLA Ops:
  0.6 0.9 %copy-start = (bf16[128,512]{1,0:T(8,128)(2,1)S(1)}, bf16[128,512]{1,0:T(8,128)(2,1)}, u32[]{:S(2)}) copy-start(bf16[128,512]{1,0:T(8,128)(2,1)} %param.8) | copy-start | bytes 393220
  0.6 0.7 %copy-start.4 = (s32[128]{0:T(128)S(1)}, s32[128]{0:T(128)}, u32[]{:S(2)}) copy-start(s32[128]{0:T(128)} %param.10) | copy-start | bytes 1540
  1.6 4.8 %copy-start.3 = (bf16[32,4096]{1,0:T(8,128)(2,1)S(1)}, bf16[32,4096]{1,0:T(8,128)(2,1)}, u32[]{:S(2)}) copy-start(bf16[32,4096]{1,0:T(8,128)(2,1)} %q_ref.4) | copy-start | bytes 786436
  1.6 1.7 %copy-start.2 = (bf16[128,512]{1,0:T(8,128)(2,1)S(1)}, bf16[128,512]{1,0:T(8,128)(2,1)}, u32[]{:S(2)}) copy-start(bf16[128,512]{1,0:T(8,128)(2,1)} %own_k.5) | copy-start | bytes 393220
  1.6 6.5 %collective-permute-start.4 = (bf16[528,128]{1,0:T(8,128)(2,1)S(1)}, bf16[528,128]{1,0:T(8,128)(2,1)S(1)}, u32[]{:S(2)}, u32[]{:S(2)}) collective-permute-start(bf16[528,128]{1,0:T(8,128)(2,1)S(1)} %pad_maximum_fusion.v_ref.own_v.refs_1_), channel_id=1, source_target_pairs={{2,0},{4,2},{6,4},{7,6},{5,7},{3,5},{1,3},{0,1},{10,8},{12,10},{14... | collective-permute-start | bytes 405512 | tf_op jit(solution)/shard_map/ppermute | solution.py:342
  3.2 6.5 %collective-permute-start.2 = (bf16[128,512]{1,0:T(8,128)(2,1)S(1)}, bf16[128,512]{1,0:T(8,128)(2,1)S(1)}, u32[]{:S(2)}, u32[]{:S(2)}) collective-permute-start(bf16[128,512]{1,0:T(8,128)(2,1)S(1)} %copy-done.2), channel_id=1, source_target_pairs={{0,2},{2,4},{4,6},{6,7},{7,5},{5,3},{3,1},{1,0},{8,10},{10,12},{12... | collective-permute-start | bytes 393224 | tf_op jit(solution)/shard_map/ppermute | solution.py:342
  3.7 11.0 %collective-permute-start = (bf16[128,512]{1,0:T(8,128)(2,1)S(1)}, bf16[128,512]{1,0:T(8,128)(2,1)S(1)}, u32[]{:S(2)}, u32[]{:S(2)}) collective-permute-start(bf16[128,512]{1,0:T(8,128)(2,1)S(1)} %copy-done.2), channel_id=1, source_target_pairs={{2,0},{4,2},{6,4},{7,6},{5,7},{3,5},{1,3},{0,1},{10,8},{12,10},{14... | collective-permute-start | bytes 393224 | tf_op jit(solution)/shard_map/ppermute | solution.py:342
  5.3 7.0 %collective-permute-start.3 = (bf16[528,128]{1,0:T(8,128)(2,1)S(1)}, bf16[528,128]{1,0:T(8,128)(2,1)S(1)}, u32[]{:S(2)}, u32[]{:S(2)}) collective-permute-start(bf16[528,128]{1,0:T(8,128)(2,1)S(1)} %pad_maximum_fusion.v_ref.own_v.refs_1_), channel_id=1, source_target_pairs={{0,2},{2,4},{4,6},{6,7},{7,5},{5,3},{3,1},{1,0},{8,10},{10,12},{12... | collective-permute-start | bytes 405512 | tf_op jit(solution)/shard_map/ppermute | solution.py:342
  8.1 5.0 %collective-permute-start.8 = (bf16[528,128]{1,0:T(8,128)(2,1)S(1)}, bf16[528,128]{1,0:T(8,128)(2,1)S(1)}, u32[]{:S(2)}, u32[]{:S(2)}) collective-permute-start(bf16[528,128]{1,0:T(8,128)(2,1)S(1)} %collective-permute-done.4.refs_3_.refs_5_), channel_id=1, source_target_pairs={{2,0},{4,2},{6,4},{7,6},{5,7},{3,5},{1,3},{0,1},{10,8},{12,10},{14... | collective-permute-start | bytes 405512 | tf_op jit(solution)/shard_map/ppermute | solution.py:342
  9.7 5.8 %collective-permute-start.6 = (bf16[512,128]{1,0:T(8,128)(2,1)S(1)}, bf16[512,128]{1,0:T(8,128)(2,1)S(1)}, u32[]{:S(2)}, u32[]{:S(2)}) collective-permute-start(bf16[512,128]{1,0:T(8,128)(2,1)S(1)} %by_head.3.refs_0_.refs_2_), channel_id=1, source_target_pairs={{0,2},{2,4},{4,6},{6,7},{7,5},{5,3},{3,1},{1,0},{8,10},{10,12},{12... | collective-permute-start | bytes 393224 | tf_op jit(solution)/shard_map/ppermute | solution.py:342
  12.2 6.5 %collective-permute-start.7 = (bf16[528,128]{1,0:T(8,128)(2,1)S(1)}, bf16[528,128]{1,0:T(8,128)(2,1)S(1)}, u32[]{:S(2)}, u32[]{:S(2)}) collective-permute-start(bf16[528,128]{1,0:T(8,128)(2,1)S(1)} %collective-permute-done.3.refs_1_.refs_3_), channel_id=1, source_target_pairs={{0,2},{2,4},{4,6},{6,7},{7,5},{5,3},{3,1},{1,0},{8,10},{10,12},{12... | collective-permute-start | bytes 405512 | tf_op jit(solution)/shard_map/ppermute | solution.py:342
  13.2 5.5 %collective-permute-start.11 = (bf16[528,128]{1,0:T(8,128)(2,1)S(1)}, bf16[528,128]{1,0:T(8,128)(2,1)S(1)}, u32[]{:S(2)}, u32[]{:S(2)}) collective-permute-start(bf16[528,128]{1,0:T(8,128)(2,1)S(1)} %collective-permute-done.8.refs_9_), channel_id=1, source_target_pairs={{2,0},{4,2},{6,4},{7,6},{5,7},{3,5},{1,3},{0,1},{10,8},{12,10},{14... | collective-permute-start | bytes 405512 | tf_op jit(solution)/shard_map/ppermute | solution.py:342
  14.8 8.7 %copy-start.1 = (bf16[128,4096]{1,0:T(8,128)(2,1)S(1)}, bf16[128,4096]{1,0:T(8,128)(2,1)}, u32[]{:S(2)}) copy-start(bf16[128,4096]{1,0:T(8,128)(2,1)} %q_ref.7) | copy-start | bytes 3145732
  14.8 6.6 %collective-permute-start.1 = (bf16[512,128]{1,0:T(8,128)(2,1)S(1)}, bf16[512,128]{1,0:T(8,128)(2,1)S(1)}, u32[]{:S(2)}, u32[]{:S(2)}) collective-permute-start(bf16[512,128]{1,0:T(8,128)(2,1)S(1)} %by_head.2.refs_2_.refs_4_), channel_id=1, source_target_pairs={{2,0},{4,2},{6,4},{7,6},{5,7},{3,5},{1,3},{0,1},{10,8},{12,10},{14... | collective-permute-start | bytes 393224 | tf_op jit(solution)/shard_map/ppermute | solution.py:342
  15.5 7.3 %collective-permute-start.9 = (bf16[512,128]{1,0:T(8,128)(2,1)S(1)}, bf16[512,128]{1,0:T(8,128)(2,1)S(1)}, u32[]{:S(2)}, u32[]{:S(2)}) collective-permute-start(bf16[512,128]{1,0:T(8,128)(2,1)S(1)} %collective-permute-done.6.refs_6_), channel_id=1, source_target_pairs={{0,2},{2,4},{4,6},{6,7},{7,5},{5,3},{3,1},{1,0},{8,10},{10,12},{12... | collective-permute-start | bytes 393224 | tf_op jit(solution)/shard_map/ppermute | solution.py:342
  18.7 7.7 %collective-permute-start.10 = (bf16[528,128]{1,0:T(8,128)(2,1)S(1)}, bf16[528,128]{1,0:T(8,128)(2,1)S(1)}, u32[]{:S(2)}, u32[]{:S(2)}) collective-permute-start(bf16[528,128]{1,0:T(8,128)(2,1)S(1)} %collective-permute-done.7.refs_7_), channel_id=1, source_target_pairs={{0,2},{2,4},{4,6},{6,7},{7,5},{5,3},{3,1},{1,0},{8,10},{10,12},{12... | collective-permute-start | bytes 405512 | tf_op jit(solution)/shard_map/ppermute | solution.py:342
  18.7 10.9 %collective-permute-start.13 = (bf16[528,128]{1,0:T(8,128)(2,1)S(1)}, bf16[528,128]{1,0:T(8,128)(2,1)S(1)}, u32[]{:S(2)}, u32[]{:S(2)}) collective-permute-start(bf16[528,128]{1,0:T(8,128)(2,1)S(1)} %collective-permute-done.11.refs_3_), channel_id=1, source_target_pairs={{2,0},{4,2},{6,4},{7,6},{5,7},{3,5},{1,3},{0,1},{10,8},{12,10},{14... | collective-permute-start | bytes 405512 | tf_op jit(solution)/shard_map/ppermute | solution.py:342
  21.4 5.0 %collective-permute-start.5 = (bf16[512,128]{1,0:T(8,128)(2,1)S(1)}, bf16[512,128]{1,0:T(8,128)(2,1)S(1)}, u32[]{:S(2)}, u32[]{:S(2)}) collective-permute-start(bf16[512,128]{1,0:T(8,128)(2,1)S(1)} %collective-permute-done.1.refs_8_), channel_id=1, source_target_pairs={{2,0},{4,2},{6,4},{7,6},{5,7},{3,5},{1,3},{0,1},{10,8},{12,10},{14... | collective-permute-start | bytes 393224 | tf_op jit(solution)/shard_map/ppermute | solution.py:342
  22.8 6.8 %collective-permute-start.12 = (bf16[512,128]{1,0:T(8,128)(2,1)S(1)}, bf16[512,128]{1,0:T(8,128)(2,1)S(1)}, u32[]{:S(2)}, u32[]{:S(2)}) collective-permute-start(bf16[512,128]{1,0:T(8,128)(2,1)S(1)} %collective-permute-done.9.refs_0_), channel_id=1, source_target_pairs={{0,2},{2,4},{4,6},{6,7},{7,5},{5,3},{3,1},{1,0},{8,10},{10,12},{12... | collective-permute-start | bytes 393224 | tf_op jit(solution)/shard_map/ppermute | solution.py:342

commit v7 on v6

--- a/solution.py
+++ b/solution.py
@@ -98,6 +98,22 @@
         cost_estimate=pl.CostEstimate(flops=4 * 10**9, bytes_accessed=0, transcendentals=0),
         compiler_params=LIMIT,
         name="by_head",
+    )(x)
+
+
+def relay_kernel(x_ref, o_ref):
+    o_ref[...] = x_ref[...]
+
+
+def relay(x):
+    return pl.pallas_call(
+        relay_kernel,
+        out_shape=jax.ShapeDtypeStruct(x.shape, x.dtype),
+        in_specs=[whole()],
+        out_specs=whole(),
+        cost_estimate=pl.CostEstimate(flops=4 * 10**9, bytes_accessed=0, transcendentals=0),
+        compiler_params=LIMIT,
+        name="relay",
     )(x)
 
 
@@ -208,9 +224,11 @@
     see_own = jnp.where(key < row, own.flags(), jnp.where(key == row, 1.0, 0.0))
     bias = jnp.where(jnp.concatenate([see_anchor, see_own], 0) > 0.5, 0.0, HIDDEN)
     alive = jnp.where(here < live_ref[0], 1.0, 0.0)
+    all_keys = [jnp.concatenate([anchor.keys(g), own.keys(g)], 0) for g in range(groups)]
+    all_values = [jnp.concatenate([anchor.values(g), own.values(g)], 1) for g in range(groups)]
     for g in range(groups):
-        keys = jnp.concatenate([anchor.keys(g), own.keys(g)], 0)
-        values = jnp.concatenate([anchor.values(g), own.values(g)], 1)
+        keys = all_keys[g]
+        values = all_values[g]
         for h in range(share // HEAD):
             at = slice(g * share + h * HEAD, g * share + (h + 1) * HEAD)
             s = lax.dot_general(keys, q_ref[:, at], NT, preferred_element_type=F32)
@@ -367,6 +385,8 @@
             if step == 1:
                 left_k = by_head(left_k)
                 right_k = by_head(right_k)
+            if step == 2:
+                right_k = relay(right_k)
             right_k, state = lax.optimization_barrier((right_k, state))
             arrived = [(ring[step], (left_k, left_v)), (ring[n - step], (right_k, right_v))]
     left, right = left_k, right_v

time: 31.2 us -> 31 us (level)
  transfers between devices with their start and end apart: 14 -> 14, of which waited for: 5 -> 7; matrix products, arithmetic and copies ran while one was open for 0% -> 0% of each run, Pallas kernels for 17% -> 17%
where the time goes in v7:
time: 31 us; the launch traced here: 30.9 us
  starting transfers between devices  14.2 us (46%)
  waiting for transfers between devices  7.54 us (24%)
  Pallas kernels  6.73 us (22%)
  between operations  1.42 us (5%)
  local copies, waits for them, and re-layouts  0.94 us (3%)
    ppermute x14, starting transfers between devices, send(): return lax.ppermute(value, 'ctx', pairs)  14.2 us
    ppermute x14, waiting for transfers between devices, send(): return lax.ppermute(value, 'ctx', pairs)  7.54 us
    pallas_call x2, Pallas kernels, both(): pl.pallas_call(functools.partial(both_kernel, groups, rows, devices, part...  3.89 us
    pallas_call x1, Pallas kernels, finish(): pl.pallas_call(functools.partial(finish_kernel, groups, rows, device, [le...  1.44 us
    unnamed x10, local copies, waits for them, and re-layouts  0.91 us
    pallas_call x1, Pallas kernels, query_more(): pl.pallas_call(functools.partial(more_kernel, groups, rows, [len(piece) f...  0.68 us
    pallas_call x1, Pallas kernels, query_first(): pl.pallas_call(functools.partial(first_kernel, groups, rows), out_shape=[...  0.66 us
  transfers between devices with their start and end apart: 14, of which 7 were waited for; matrix products, arithmetic and copies ran while one was open for 0% of the time, Pallas kernels for 17%

profile of v7, /device:TPU:18, one launch (start us, length us, event | category | flops | bytes accessed | tf_op | source)
XLA Modules:
  0.0 30.9 jit_solution(941965617872436630)
XLA Ops:
  0.6 0.0 copy-start
  0.6 0.0 copy-start.4
  0.7 0.7 %copy-done.4 = s32[128]{0:T(128)S(1)} copy-done((s32[128]{0:T(128)S(1)}, s32[128]{0:T(128)}, u32[]{:S(2)}) %copy-start.4) | copy-done | bytes 536
  1.4 0.2 copy-done
  1.6 0.0 copy-start.3
  1.6 0.0 copy-start.2
  1.6 1.6 %collective-permute-start.4 = (bf16[528,128]{1,0:T(8,128)(2,1)S(1)}, bf16[528,128]{1,0:T(8,128)(2,1)S(1)}, u32[]{:S(2)}, u32[]{:S(2)}) collective-permute-start(bf16[528,128]{1,0:T(8,128)(2,1)S(1)} %pad_maximum_fusion.v_ref.own_v.refs_1_), channel_id=1, source_target_pairs={{2,0},{4,2},{6,4},{7,6},{5,7},{3,5},{1,3},{0,1},{10,8},{12,10},{14... | collective-permute-start | bytes 405512 | tf_op jit(solution)/shard_map/ppermute | solution.py:360
  3.2 0.0 copy-done.2
  3.2 0.4 %collective-permute-start.2 = (bf16[128,512]{1,0:T(8,128)(2,1)S(1)}, bf16[128,512]{1,0:T(8,128)(2,1)S(1)}, u32[]{:S(2)}, u32[]{:S(2)}) collective-permute-start(bf16[128,512]{1,0:T(8,128)(2,1)S(1)} %copy-done.2), channel_id=1, source_target_pairs={{0,2},{2,4},{4,6},{6,7},{7,5},{5,3},{3,1},{1,0},{8,10},{10,12},{12... | collective-permute-start | bytes 393224 | tf_op jit(solution)/shard_map/ppermute | solution.py:360
  3.7 1.6 %collective-permute-start = (bf16[128,512]{1,0:T(8,128)(2,1)S(1)}, bf16[128,512]{1,0:T(8,128)(2,1)S(1)}, u32[]{:S(2)}, u32[]{:S(2)}) collective-permute-start(bf16[128,512]{1,0:T(8,128)(2,1)S(1)} %copy-done.2), channel_id=1, source_target_pairs={{2,0},{4,2},{6,4},{7,6},{5,7},{3,5},{1,3},{0,1},{10,8},{12,10},{14... | collective-permute-start | bytes 393224 | tf_op jit(solution)/shard_map/ppermute | solution.py:360
  5.3 0.4 %collective-permute-start.3 = (bf16[528,128]{1,0:T(8,128)(2,1)S(1)}, bf16[528,128]{1,0:T(8,128)(2,1)S(1)}, u32[]{:S(2)}, u32[]{:S(2)}) collective-permute-start(bf16[528,128]{1,0:T(8,128)(2,1)S(1)} %pad_maximum_fusion.v_ref.own_v.refs_1_), channel_id=1, source_target_pairs={{0,2},{2,4},{4,6},{6,7},{7,5},{5,3},{3,1},{1,0},{8,10},{10,12},{12... | collective-permute-start | bytes 405512 | tf_op jit(solution)/shard_map/ppermute | solution.py:360
  6.4 0.0 copy-done.3
  6.4 0.7 %query_first.1 = (bf16[1024,128]{1,0:T(8,128)(2,1)S(1)}, f32[512,256]{1,0:T(8,128)S(1)}, f32[8,256]{1,0:T(8,128)S(1)}) custom-call(s32[1]{0:T(128)S(6)} %copy.27.live_ref, bf16[32,4096]{1,0:T(8,128)(2,1)S(1)} %copy-done.3, bf16[128,512]{1,0:T(8,128)(2,1)S(1)} %copy-done.2, bf16[528,128]{1,0:T(8,128)(2,1)S(1)} %pad_maximum_fusion.v_ref.own_v.refs_1_), custom_call_target="tpu_custom_call" | custom-call | tf_op jit(solution)/shard_map/query_first/pallas_call | solution.py:175
  7.1 1.1 %collective-permute-done.4.refs_3_.refs_5_ = bf16[528,128]{1,0:T(8,128)(2,1)S(1)} collective-permute-done((bf16[528,128]{1,0:T(8,128)(2,1)S(1)}, bf16[528,128]{1,0:T(8,128)(2,1)S(1)}, u32[]{:S(2)}, u32[]{:S(2)}) %collective-permute-start.4) | collective-permute-done | bytes 135200 | tf_op jit(solution)/shard_map/ppermute | solution.py:360
  8.1 1.6 %collective-permute-start.8 = (bf16[528,128]{1,0:T(8,128)(2,1)S(1)}, bf16[528,128]{1,0:T(8,128)(2,1)S(1)}, u32[]{:S(2)}, u32[]{:S(2)}) collective-permute-start(bf16[528,128]{1,0:T(8,128)(2,1)S(1)} %collective-permute-done.4.refs_3_.refs_5_), channel_id=1, source_target_pairs={{2,0},{4,2},{6,4},{7,6},{5,7},{3,5},{1,3},{0,1},{10,8},{12,10},{14... | collective-permute-start | bytes 405512 | tf_op jit(solution)/shard_map/ppermute | solution.py:360
  9.7 0.0 collective-permute-done.2.x_ref
  9.7 0.5 %collective-permute-start.6 = (bf16[512,128]{1,0:T(8,128)(2,1)S(1)}, bf16[512,128]{1,0:T(8,128)(2,1)S(1)}, u32[]{:S(2)}, u32[]{:S(2)}) collective-permute-start(bf16[512,128]{1,0:T(8,128)(2,1)S(1)} %by_head.3.refs_0_.refs_2_), channel_id=1, source_target_pairs={{0,2},{2,4},{4,6},{6,7},{7,5},{5,3},{3,1},{1,0},{8,10},{10,12},{12... | collective-permute-start | bytes 393224 | tf_op jit(solution)/shard_map/ppermute | solution.py:360
  10.3 2.0 %collective-permute-done.3.refs_1_.refs_3_ = bf16[528,128]{1,0:T(8,128)(2,1)S(1)} collective-permute-done((bf16[528,128]{1,0:T(8,128)(2,1)S(1)}, bf16[528,128]{1,0:T(8,128)(2,1)S(1)}, u32[]{:S(2)}, u32[]{:S(2)}) %collective-permute-start.3) | collective-permute-done | bytes 135200 | tf_op jit(solution)/shard_map/ppermute | solution.py:360
  12.2 0.4 %collective-permute-start.7 = (bf16[528,128]{1,0:T(8,128)(2,1)S(1)}, bf16[528,128]{1,0:T(8,128)(2,1)S(1)}, u32[]{:S(2)}, u32[]{:S(2)}) collective-permute-start(bf16[528,128]{1,0:T(8,128)(2,1)S(1)} %collective-permute-done.3.refs_1_.refs_3_), channel_id=1, source_target_pairs={{0,2},{2,4},{4,6},{6,7},{7,5},{5,3},{3,1},{1,0},{8,10},{10,12},{12... | collective-permute-start | bytes 405512 | tf_op jit(solution)/shard_map/ppermute | solution.py:360
  12.7 0.5 %collective-permute-done.8.refs_9_ = bf16[528,128]{1,0:T(8,128)(2,1)S(1)} collective-permute-done((bf16[528,128]{1,0:T(8,128)(2,1)S(1)}, bf16[528,128]{1,0:T(8,128)(2,1)S(1)}, u32[]{:S(2)}, u32[]{:S(2)}) %collective-permute-start.8) | collective-permute-done | bytes 135200 | tf_op jit(solution)/shard_map/ppermute | solution.py:360
  13.2 1.6 %collective-permute-start.11 = (bf16[528,128]{1,0:T(8,128)(2,1)S(1)}, bf16[528,128]{1,0:T(8,128)(2,1)S(1)}, u32[]{:S(2)}, u32[]{:S(2)}) collective-permute-start(bf16[528,128]{1,0:T(8,128)(2,1)S(1)} %collective-permute-done.8.refs_9_), channel_id=1, source_target_pairs={{2,0},{4,2},{6,4},{7,6},{5,7},{3,5},{1,3},{0,1},{10,8},{12,10},{14... | collective-permute-start | bytes 405512 | tf_op jit(solution)/shard_map/ppermute | solution.py:360
  14.7 0.0 collective-permute-done.x_ref
  14.8 0.7 %collective-permute-start.1 = (bf16[512,128]{1,0:T(8,128)(2,1)S(1)}, bf16[512,128]{1,0:T(8,128)(2,1)S(1)}, u32[]{:S(2)}, u32[]{:S(2)}) collective-permute-start(bf16[512,128]{1,0:T(8,128)(2,1)S(1)} %by_head.2.refs_2_.refs_4_), channel_id=1, source_target_pairs={{2,0},{4,2},{6,4},{7,6},{5,7},{3,5},{1,3},{0,1},{10,8},{12,10},{14... | collective-permute-start | bytes 393224 | tf_op jit(solution)/shard_map/ppermute | solution.py:360
  15.5 0.7 %query_more.1 = (f32[512,256]{1,0:T(8,128)S(1)}, f32[8,256]{1,0:T(8,128)S(1)}) custom-call(s32[1]{0:T(128)S(6)} %copy.27.live_ref, bf16[1024,128]{1,0:T(8,128)(2,1)S(1)} %get-tuple-element.46.stacked, f32[512,256]{1,0:T(8,128)S(1)} %get-tuple-element.36.acc_in, ...), custom_call_target="tpu_custom_call", output_to_operand_aliasing={{0}: (2, {}), {1}: (3, {})} | custom-call | tf_op jit(solution)/shard_map/query_more/pallas_call | solution.py:205
  16.2 0.0 copy-start.1
  16.2 0.0 collective-permute-done.6.refs_6_
  16.2 1.4 %collective-permute-start.9 = (bf16[512,128]{1,0:T(8,128)(2,1)S(1)}, bf16[512,128]{1,0:T(8,128)(2,1)S(1)}, u32[]{:S(2)}, u32[]{:S(2)}) collective-permute-start(bf16[512,128]{1,0:T(8,128)(2,1)S(1)} %collective-permute-done.6.refs_6_), channel_id=1, source_target_pairs={{0,2},{2,4},{4,6},{6,7},{7,5},{5,3},{3,1},{1,0},{8,10},{10,12},{12... | collective-permute-start | bytes 393224 | tf_op jit(solution)/shard_map/ppermute | solution.py:360
  17.6 0.6 %collective-permute-done.7.refs_7_ = bf16[528,128]{1,0:T(8,128)(2,1)S(1)} collective-permute-done((bf16[528,128]{1,0:T(8,128)(2,1)S(1)}, bf16[528,128]{1,0:T(8,128)(2,1)S(1)}, u32[]{:S(2)}, u32[]{:S(2)}) %collective-permute-start.7) | collective-permute-done | bytes 135200 | tf_op jit(solution)/shard_map/ppermute | solution.py:360
  18.2 0.0 collective-permute-start.10
  18.2 0.2 collective-permute-done.11.refs_3_
  18.4 1.8 %collective-permute-start.13 = (bf16[528,128]{1,0:T(8,128)(2,1)S(1)}, bf16[528,128]{1,0:T(8,128)(2,1)S(1)}, u32[]{:S(2)}, u32[]{:S(2)}) collective-permute-start(bf16[528,128]{1,0:T(8,128)(2,1)S(1)} %collective-permute-done.11.refs_3_), channel_id=1, source_target_pairs={{2,0},{4,2},{6,4},{7,6},{5,7},{3,5},{1,3},{0,1},{10,8},{12,10},{14... | collective-permute-start | bytes 405512 | tf_op jit(solution)/shard_map/ppermute | solution.py:360
  20.2 1.0 %collective-permute-done.1.x_ref = bf16[512,128]{1,0:T(8,128)(2,1)S(1)} collective-permute-done((bf16[512,128]{1,0:T(8,128)(2,1)S(1)}, bf16[512,128]{1,0:T(8,128)(2,1)S(1)}, u32[]{:S(2)}, u32[]{:S(2)}) %collective-permute-start.1) | collective-permute-done | bytes 131104 | tf_op jit(solution)/shard_map/ppermute | solution.py:360
  21.2 1.6 %collective-permute-start.5 = (bf16[512,128]{1,0:T(8,128)(2,1)S(1)}, bf16[512,128]{1,0:T(8,128)(2,1)S(1)}, u32[]{:S(2)}, u32[]{:S(2)}) collective-permute-start(bf16[512,128]{1,0:T(8,128)(2,1)S(1)} %relay.1.refs_8_), channel_id=1, source_target_pairs={{2,0},{4,2},{6,4},{7,6},{5,7},{3,5},{1,3},{0,1},{10,8},{12,10},{14... | collective-permute-start | bytes 393224 | tf_op jit(solution)/shard_map/ppermute | solution.py:360
  22.8 0.0 collective-permute-done.9.refs_0_
  22.8 0.5 %collective-permute-start.12 = (bf16[512,128]{1,0:T(8,128)(2,1)S(1)}, bf16[512,128]{1,0:T(8,128)(2,1)S(1)}, u32[]{:S(2)}, u32[]{:S(2)}) collective-permute-start(bf16[512,128]{1,0:T(8,128)(2,1)S(1)} %collective-permute-done.9.refs_0_), channel_id=1, source_target_pairs={{0,2},{2,4},{4,6},{6,7},{7,5},{5,3},{3,1},{1,0},{8,10},{10,12},{12... | collective-permute-start | bytes 393224 | tf_op jit(solution)/shard_map/ppermute | solution.py:360
  23.3 0.0 copy-done.1
  23.3 0.7 %both.2 = (f32[512,256]{1,0:T(8,128)S(1)}, f32[8,256]{1,0:T(8,128)S(1)}, bf16[128,4096]{1,0:T(8,128)(2,1)}) custom-call(s32[1]{0:T(128)S(6)} %copy.27.live_ref, bf16[1024,128]{1,0:T(8,128)(2,1)S(1)} %get-tuple-element.46.stacked, f32[512,256]{1,0:T(8,128)S(1)} %get-tuple-element.42.acc_in, ...), custom_call_target="tpu_custom_call", output_to_operand_aliasing={{0}: (2, {}), {1}: (3, {})} | custom-call | tf_op jit(solution)/shard_map/both/pallas_call | solution.py:277
  24.0 2.2 %collective-permute-done.5.refs_2_ = bf16[512,128]{1,0:T(8,128)(2,1)S(1)} collective-permute-done((bf16[512,128]{1,0:T(8,128)(2,1)S(1)}, bf16[512,128]{1,0:T(8,128)(2,1)S(1)}, u32[]{:S(2)}, u32[]{:S(2)}) %collective-permute-start.5) | collective-permute-done | bytes 131104 | tf_op jit(solution)/shard_map/ppermute | solution.py:360
  26.2 0.0 collective-permute-done.10.refs_1_
  26.2 3.2 %both.3 = (f32[512,256]{1,0:T(8,128)S(1)}, f32[8,256]{1,0:T(8,128)S(1)}, bf16[128,4096]{1,0:T(8,128)(2,1)}) custom-call(s32[1]{0:T(128)S(6)} %copy.27.live_ref, bf16[1024,128]{1,0:T(8,128)(2,1)S(1)} %get-tuple-element.46.stacked, f32[512,256]{1,0:T(8,128)S(1)} %get-tuple-element.47.acc_in, ...), custom_call_target="tpu_custom_call", output_to_operand_aliasing={{0}: (2, {}), {1}: (3, {}), {2}: (11, {})} | custom-call | tf_op jit(solution)/shard_map/both/pallas_call | solution.py:277
  29.4 0.0 collective-permute-done.12.refs_0_
  29.4 0.0 collective-permute-done.13.refs_1_
  29.4 1.4 %finish.1 = (bf16[32,4096]{1,0:T(8,128)(2,1)}, bf16[128,4096]{1,0:T(8,128)(2,1)}) custom-call(s32[1]{0:T(128)S(6)} %copy.27.live_ref, bf16[1024,128]{1,0:T(8,128)(2,1)S(1)} %get-tuple-element.46.stacked, f32[512,256]{1,0:T(8,128)S(1)} %get-tuple-element.51.acc, f32[8,256]{1,0:T(8,128)S(1)} %get-tuple-element.52.stat, ...), custom_call_target="tpu_custom_call", output_to_operand_aliasing={{1}: (9, {})} | custom-call | tf_op jit(solution)/shard_map/finish/pallas_call | solution.py:332
  (7 shorter events, 0.1 us)
Async XLA Ops:
  0.6 0.9 %copy-start = (bf16[128,512]{1,0:T(8,128)(2,1)S(1)}, bf16[128,512]{1,0:T(8,128)(2,1)}, u32[]{:S(2)}) copy-start(bf16[128,512]{1,0:T(8,128)(2,1)} %param.8) | copy-start | bytes 393220
  0.6 0.7 %copy-start.4 = (s32[128]{0:T(128)S(1)}, s32[128]{0:T(128)}, u32[]{:S(2)}) copy-start(s32[128]{0:T(128)} %param.10) | copy-start | bytes 1540
  1.6 4.8 %copy-start.3 = (bf16[32,4096]{1,0:T(8,128)(2,1)S(1)}, bf16[32,4096]{1,0:T(8,128)(2,1)}, u32[]{:S(2)}) copy-start(bf16[32,4096]{1,0:T(8,128)(2,1)} %q_ref.4) | copy-start | bytes 786436
  1.6 1.7 %copy-start.2 = (bf16[128,512]{1,0:T(8,128)(2,1)S(1)}, bf16[128,512]{1,0:T(8,128)(2,1)}, u32[]{:S(2)}) copy-start(bf16[128,512]{1,0:T(8,128)(2,1)} %own_k.5) | copy-start | bytes 393220
  1.6 6.5 %collective-permute-start.4 = (bf16[528,128]{1,0:T(8,128)(2,1)S(1)}, bf16[528,128]{1,0:T(8,128)(2,1)S(1)}, u32[]{:S(2)}, u32[]{:S(2)}) collective-permute-start(bf16[528,128]{1,0:T(8,128)(2,1)S(1)} %pad_maximum_fusion.v_ref.own_v.refs_1_), channel_id=1, source_target_pairs={{2,0},{4,2},{6,4},{7,6},{5,7},{3,5},{1,3},{0,1},{10,8},{12,10},{14... | collective-permute-start | bytes 405512 | tf_op jit(solution)/shard_map/ppermute | solution.py:360
  3.2 6.5 %collective-permute-start.2 = (bf16[128,512]{1,0:T(8,128)(2,1)S(1)}, bf16[128,512]{1,0:T(8,128)(2,1)S(1)}, u32[]{:S(2)}, u32[]{:S(2)}) collective-permute-start(bf16[128,512]{1,0:T(8,128)(2,1)S(1)} %copy-done.2), channel_id=1, source_target_pairs={{0,2},{2,4},{4,6},{6,7},{7,5},{5,3},{3,1},{1,0},{8,10},{10,12},{12... | collective-permute-start | bytes 393224 | tf_op jit(solution)/shard_map/ppermute | solution.py:360
  3.7 11.0 %collective-permute-start = (bf16[128,512]{1,0:T(8,128)(2,1)S(1)}, bf16[128,512]{1,0:T(8,128)(2,1)S(1)}, u32[]{:S(2)}, u32[]{:S(2)}) collective-permute-start(bf16[128,512]{1,0:T(8,128)(2,1)S(1)} %copy-done.2), channel_id=1, source_target_pairs={{2,0},{4,2},{6,4},{7,6},{5,7},{3,5},{1,3},{0,1},{10,8},{12,10},{14... | collective-permute-start | bytes 393224 | tf_op jit(solution)/shard_map/ppermute | solution.py:360
  5.3 7.0 %collective-permute-start.3 = (bf16[528,128]{1,0:T(8,128)(2,1)S(1)}, bf16[528,128]{1,0:T(8,128)(2,1)S(1)}, u32[]{:S(2)}, u32[]{:S(2)}) collective-permute-start(bf16[528,128]{1,0:T(8,128)(2,1)S(1)} %pad_maximum_fusion.v_ref.own_v.refs_1_), channel_id=1, source_target_pairs={{0,2},{2,4},{4,6},{6,7},{7,5},{5,3},{3,1},{1,0},{8,10},{10,12},{12... | collective-permute-start | bytes 405512 | tf_op jit(solution)/shard_map/ppermute | solution.py:360
  8.1 5.0 %collective-permute-start.8 = (bf16[528,128]{1,0:T(8,128)(2,1)S(1)}, bf16[528,128]{1,0:T(8,128)(2,1)S(1)}, u32[]{:S(2)}, u32[]{:S(2)}) collective-permute-start(bf16[528,128]{1,0:T(8,128)(2,1)S(1)} %collective-permute-done.4.refs_3_.refs_5_), channel_id=1, source_target_pairs={{2,0},{4,2},{6,4},{7,6},{5,7},{3,5},{1,3},{0,1},{10,8},{12,10},{14... | collective-permute-start | bytes 405512 | tf_op jit(solution)/shard_map/ppermute | solution.py:360
  9.7 6.5 %collective-permute-start.6 = (bf16[512,128]{1,0:T(8,128)(2,1)S(1)}, bf16[512,128]{1,0:T(8,128)(2,1)S(1)}, u32[]{:S(2)}, u32[]{:S(2)}) collective-permute-start(bf16[512,128]{1,0:T(8,128)(2,1)S(1)} %by_head.3.refs_0_.refs_2_), channel_id=1, source_target_pairs={{0,2},{2,4},{4,6},{6,7},{7,5},{5,3},{3,1},{1,0},{8,10},{10,12},{12... | collective-permute-start | bytes 393224 | tf_op jit(solution)/shard_map/ppermute | solution.py:360
  12.2 6.0 %collective-permute-start.7 = (bf16[528,128]{1,0:T(8,128)(2,1)S(1)}, bf16[528,128]{1,0:T(8,128)(2,1)S(1)}, u32[]{:S(2)}, u32[]{:S(2)}) collective-permute-start(bf16[528,128]{1,0:T(8,128)(2,1)S(1)} %collective-permute-done.3.refs_1_.refs_3_), channel_id=1, source_target_pairs={{0,2},{2,4},{4,6},{6,7},{7,5},{5,3},{3,1},{1,0},{8,10},{10,12},{12... | collective-permute-start | bytes 405512 | tf_op jit(solution)/shard_map/ppermute | solution.py:360
  13.2 5.2 %collective-permute-start.11 = (bf16[528,128]{1,0:T(8,128)(2,1)S(1)}, bf16[528,128]{1,0:T(8,128)(2,1)S(1)}, u32[]{:S(2)}, u32[]{:S(2)}) collective-permute-start(bf16[528,128]{1,0:T(8,128)(2,1)S(1)} %collective-permute-done.8.refs_9_), channel_id=1, source_target_pairs={{2,0},{4,2},{6,4},{7,6},{5,7},{3,5},{1,3},{0,1},{10,8},{12,10},{14... | collective-permute-start | bytes 405512 | tf_op jit(solution)/shard_map/ppermute | solution.py:360
  14.8 6.4 %collective-permute-start.1 = (bf16[512,128]{1,0:T(8,128)(2,1)S(1)}, bf16[512,128]{1,0:T(8,128)(2,1)S(1)}, u32[]{:S(2)}, u32[]{:S(2)}) collective-permute-start(bf16[512,128]{1,0:T(8,128)(2,1)S(1)} %by_head.2.refs_2_.refs_4_), channel_id=1, source_target_pairs={{2,0},{4,2},{6,4},{7,6},{5,7},{3,5},{1,3},{0,1},{10,8},{12,10},{14... | collective-permute-start | bytes 393224 | tf_op jit(solution)/shard_map/ppermute | solution.py:360
  16.2 7.1 %copy-start.1 = (bf16[128,4096]{1,0:T(8,128)(2,1)S(1)}, bf16[128,4096]{1,0:T(8,128)(2,1)}, u32[]{:S(2)}) copy-start(bf16[128,4096]{1,0:T(8,128)(2,1)} %q_ref.7) | copy-start | bytes 3145732
  16.2 6.6 %collective-permute-start.9 = (bf16[512,128]{1,0:T(8,128)(2,1)S(1)}, bf16[512,128]{1,0:T(8,128)(2,1)S(1)}, u32[]{:S(2)}, u32[]{:S(2)}) collective-permute-start(bf16[512,128]{1,0:T(8,128)(2,1)S(1)} %collective-permute-done.6.refs_6_), channel_id=1, source_target_pairs={{0,2},{2,4},{4,6},{6,7},{7,5},{5,3},{3,1},{1,0},{8,10},{10,12},{12... | collective-permute-start | bytes 393224 | tf_op jit(solution)/shard_map/ppermute | solution.py:360
  18.2 8.1 %collective-permute-start.10 = (bf16[528,128]{1,0:T(8,128)(2,1)S(1)}, bf16[528,128]{1,0:T(8,128)(2,1)S(1)}, u32[]{:S(2)}, u32[]{:S(2)}) collective-permute-start(bf16[528,128]{1,0:T(8,128)(2,1)S(1)} %collective-permute-done.7.refs_7_), channel_id=1, source_target_pairs={{0,2},{2,4},{4,6},{6,7},{7,5},{5,3},{3,1},{1,0},{8,10},{10,12},{12... | collective-permute-start | bytes 405512 | tf_op jit(solution)/shard_map/ppermute | solution.py:360
  18.4 11.0 %collective-permute-start.13 = (bf16[528,128]{1,0:T(8,128)(2,1)S(1)}, bf16[528,128]{1,0:T(8,128)(2,1)S(1)}, u32[]{:S(2)}, u32[]{:S(2)}) collective-permute-start(bf16[528,128]{1,0:T(8,128)(2,1)S(1)} %collective-permute-done.11.refs_3_), channel_id=1, source_target_pairs={{2,0},{4,2},{6,4},{7,6},{5,7},{3,5},{1,3},{0,1},{10,8},{12,10},{14... | collective-permute-start | bytes 405512 | tf_op jit(solution)/shard_map/ppermute | solution.py:360
  21.2 5.0 %collective-permute-start.5 = (bf16[512,128]{1,0:T(8,128)(2,1)S(1)}, bf16[512,128]{1,0:T(8,128)(2,1)S(1)}, u32[]{:S(2)}, u32[]{:S(2)}) collective-permute-start(bf16[512,128]{1,0:T(8,128)(2,1)S(1)} %relay.1.refs_8_), channel_id=1, source_target_pairs={{2,0},{4,2},{6,4},{7,6},{5,7},{3,5},{1,3},{0,1},{10,8},{12,10},{14... | collective-permute-start | bytes 393224 | tf_op jit(solution)/shard_map/ppermute | solution.py:360
  22.8 6.6 %collective-permute-start.12 = (bf16[512,128]{1,0:T(8,128)(2,1)S(1)}, bf16[512,128]{1,0:T(8,128)(2,1)S(1)}, u32[]{:S(2)}, u32[]{:S(2)}) collective-permute-start(bf16[512,128]{1,0:T(8,128)(2,1)S(1)} %collective-permute-done.9.refs_0_), channel_id=1, source_target_pairs={{0,2},{2,4},{4,6},{6,7},{7,5},{5,3},{3,1},{1,0},{8,10},{10,12},{12... | collective-permute-start | bytes 393224 | tf_op jit(solution)/shard_map/ppermute | solution.py:360

commit v8 on v6

--- a/solution.py
+++ b/solution.py
@@ -208,9 +208,11 @@
     see_own = jnp.where(key < row, own.flags(), jnp.where(key == row, 1.0, 0.0))
     bias = jnp.where(jnp.concatenate([see_anchor, see_own], 0) > 0.5, 0.0, HIDDEN)
     alive = jnp.where(here < live_ref[0], 1.0, 0.0)
+    all_keys = [jnp.concatenate([anchor.keys(g), own.keys(g)], 0) for g in range(groups)]
+    all_values = [jnp.concatenate([anchor.values(g), own.values(g)], 1) for g in range(groups)]
     for g in range(groups):
-        keys = jnp.concatenate([anchor.keys(g), own.keys(g)], 0)
-        values = jnp.concatenate([anchor.values(g), own.values(g)], 1)
+        keys = all_keys[g]
+        values = all_values[g]
         for h in range(share // HEAD):
             at = slice(g * share + h * HEAD, g * share + (h + 1) * HEAD)
             s = lax.dot_general(keys, q_ref[:, at], NT, preferred_element_type=F32)
@@ -228,22 +230,27 @@
     blocks, rest = take(refs, parts, groups, rows)
     acc, stat, o_ref, anchor_k, anchor_v, o_buf, out_sems = rest[aliased:]
     here = lax.axis_index("ctx")
-    for device, block in zip(devices, blocks):
-
-        @pl.when(here == device)
-        def _():
-            anchor_k[...] = jnp.concatenate([block.keys(g) for g in range(groups)], 0)
-            anchor_v[...] = block.v_ref[...]
-
+    own = Block([own_k, own_v], groups, rows)
     mine = functools.reduce(jnp.logical_or, [here == device for device in devices])
-    first, own = Block([anchor_k, anchor_v], groups, rows), Block([own_k, own_v], groups, rows)
-
-    @pl.when(mine)
-    def _():
+
+    def answer(first):
         stores = context_body(groups, rows, live_ref, q_ref, first, own, o_ref, o_buf, out_sems)
         query_body(blocks[-len(shifts) :], shifts, n, live_ref, groups, stacked, acc_in, stat_in, acc, stat)
         for store in stores:
             store.wait()
+
+    if len(blocks) == len(shifts):
+        for device, block in zip(devices, blocks):
+            pl.when(here == device)(functools.partial(answer, block))
+    else:
+        for device, block in zip(devices, blocks):
+
+            @pl.when(here == device)
+            def _():
+                anchor_k[...] = jnp.concatenate([block.keys(g) for g in range(groups)], 0)
+                anchor_v[...] = block.v_ref[...]
+
+        pl.when(mine)(functools.partial(answer, Block([anchor_k, anchor_v], groups, rows)))
 
     @pl.when(jnp.logical_not(mine))
     def _():

time: 31.2 us -> 31.2 us (level)
  no operation moved by 1% of the time
where the time goes in v8:
time: 31.2 us; the launch traced here: 31 us
  starting transfers between devices  14.4 us (46%)
  waiting for transfers between devices  7.59 us (24%)
  Pallas kernels  6.67 us (21%)
  between operations  1.41 us (5%)
  local copies, waits for them, and re-layouts  0.94 us (3%)
    ppermute x14, starting transfers between devices, send(): return lax.ppermute(value, 'ctx', pairs)  14.4 us
    ppermute x14, waiting for transfers between devices, send(): return lax.ppermute(value, 'ctx', pairs)  7.59 us
    pallas_call x2, Pallas kernels, both(): pl.pallas_call(functools.partial(both_kernel, groups, rows, devices, part...  3.84 us
    pallas_call x1, Pallas kernels, finish(): pl.pallas_call(functools.partial(finish_kernel, groups, rows, device, [le...  1.44 us
    unnamed x10, local copies, waits for them, and re-layouts  0.91 us
    pallas_call x1, Pallas kernels, query_more(): pl.pallas_call(functools.partial(more_kernel, groups, rows, [len(piece) f...  0.68 us
    pallas_call x1, Pallas kernels, query_first(): pl.pallas_call(functools.partial(first_kernel, groups, rows), out_shape=[...  0.66 us
  transfers between devices with their start and end apart: 14, of which 5 were waited for; matrix products, arithmetic and copies ran while one was open for 0% of the time, Pallas kernels for 17%

profile of v8, /device:TPU:18, one launch (start us, length us, event | category | flops | bytes accessed | tf_op | source)
XLA Modules:
  0.0 31.0 jit_solution(16308452684732755966)
XLA Ops:
  0.6 0.0 copy-start
  0.6 0.0 copy-start.4
  0.7 0.7 %copy-done.4 = s32[128]{0:T(128)S(1)} copy-done((s32[128]{0:T(128)S(1)}, s32[128]{0:T(128)}, u32[]{:S(2)}) %copy-start.4) | copy-done | bytes 536
  1.4 0.2 copy-done
  1.6 0.0 copy-start.3
  1.6 0.0 copy-start.2
  1.6 1.6 %collective-permute-start.4 = (bf16[528,128]{1,0:T(8,128)(2,1)S(1)}, bf16[528,128]{1,0:T(8,128)(2,1)S(1)}, u32[]{:S(2)}, u32[]{:S(2)}) collective-permute-start(bf16[528,128]{1,0:T(8,128)(2,1)S(1)} %pad_maximum_fusion.v_ref.own_v.refs_1_), channel_id=1, source_target_pairs={{2,0},{4,2},{6,4},{7,6},{5,7},{3,5},{1,3},{0,1},{10,8},{12,10},{14... | collective-permute-start | bytes 405512 | tf_op jit(solution)/shard_map/ppermute | solution.py:349
  3.2 0.0 copy-done.2
  3.2 0.4 %collective-permute-start.2 = (bf16[128,512]{1,0:T(8,128)(2,1)S(1)}, bf16[128,512]{1,0:T(8,128)(2,1)S(1)}, u32[]{:S(2)}, u32[]{:S(2)}) collective-permute-start(bf16[128,512]{1,0:T(8,128)(2,1)S(1)} %copy-done.2), channel_id=1, source_target_pairs={{0,2},{2,4},{4,6},{6,7},{7,5},{5,3},{3,1},{1,0},{8,10},{10,12},{12... | collective-permute-start | bytes 393224 | tf_op jit(solution)/shard_map/ppermute | solution.py:349
  3.7 1.6 %collective-permute-start = (bf16[128,512]{1,0:T(8,128)(2,1)S(1)}, bf16[128,512]{1,0:T(8,128)(2,1)S(1)}, u32[]{:S(2)}, u32[]{:S(2)}) collective-permute-start(bf16[128,512]{1,0:T(8,128)(2,1)S(1)} %copy-done.2), channel_id=1, source_target_pairs={{2,0},{4,2},{6,4},{7,6},{5,7},{3,5},{1,3},{0,1},{10,8},{12,10},{14... | collective-permute-start | bytes 393224 | tf_op jit(solution)/shard_map/ppermute | solution.py:349
  5.3 0.4 %collective-permute-start.3 = (bf16[528,128]{1,0:T(8,128)(2,1)S(1)}, bf16[528,128]{1,0:T(8,128)(2,1)S(1)}, u32[]{:S(2)}, u32[]{:S(2)}) collective-permute-start(bf16[528,128]{1,0:T(8,128)(2,1)S(1)} %pad_maximum_fusion.v_ref.own_v.refs_1_), channel_id=1, source_target_pairs={{0,2},{2,4},{4,6},{6,7},{7,5},{5,3},{3,1},{1,0},{8,10},{10,12},{12... | collective-permute-start | bytes 405512 | tf_op jit(solution)/shard_map/ppermute | solution.py:349
  6.4 0.0 copy-done.3
  6.4 0.7 %query_first.1 = (bf16[1024,128]{1,0:T(8,128)(2,1)S(1)}, f32[512,256]{1,0:T(8,128)S(1)}, f32[8,256]{1,0:T(8,128)S(1)}) custom-call(s32[1]{0:T(128)S(6)} %copy.27.live_ref, bf16[32,4096]{1,0:T(8,128)(2,1)S(1)} %copy-done.3, bf16[128,512]{1,0:T(8,128)(2,1)S(1)} %copy-done.2, bf16[528,128]{1,0:T(8,128)(2,1)S(1)} %pad_maximum_fusion.v_ref.own_v.refs_1_), custom_call_target="tpu_custom_call" | custom-call | tf_op jit(solution)/shard_map/query_first/pallas_call | solution.py:159
  7.1 1.1 %collective-permute-done.4.refs_3_.refs_5_ = bf16[528,128]{1,0:T(8,128)(2,1)S(1)} collective-permute-done((bf16[528,128]{1,0:T(8,128)(2,1)S(1)}, bf16[528,128]{1,0:T(8,128)(2,1)S(1)}, u32[]{:S(2)}, u32[]{:S(2)}) %collective-permute-start.4) | collective-permute-done | bytes 135200 | tf_op jit(solution)/shard_map/ppermute | solution.py:349
  8.1 1.6 %collective-permute-start.8 = (bf16[528,128]{1,0:T(8,128)(2,1)S(1)}, bf16[528,128]{1,0:T(8,128)(2,1)S(1)}, u32[]{:S(2)}, u32[]{:S(2)}) collective-permute-start(bf16[528,128]{1,0:T(8,128)(2,1)S(1)} %collective-permute-done.4.refs_3_.refs_5_), channel_id=1, source_target_pairs={{2,0},{4,2},{6,4},{7,6},{5,7},{3,5},{1,3},{0,1},{10,8},{12,10},{14... | collective-permute-start | bytes 405512 | tf_op jit(solution)/shard_map/ppermute | solution.py:349
  9.7 0.0 collective-permute-done.2.x_ref
  9.7 0.5 %collective-permute-start.6 = (bf16[512,128]{1,0:T(8,128)(2,1)S(1)}, bf16[512,128]{1,0:T(8,128)(2,1)S(1)}, u32[]{:S(2)}, u32[]{:S(2)}) collective-permute-start(bf16[512,128]{1,0:T(8,128)(2,1)S(1)} %by_head.3.refs_0_.refs_2_), channel_id=1, source_target_pairs={{0,2},{2,4},{4,6},{6,7},{7,5},{5,3},{3,1},{1,0},{8,10},{10,12},{12... | collective-permute-start | bytes 393224 | tf_op jit(solution)/shard_map/ppermute | solution.py:349
  10.3 2.0 %collective-permute-done.3.refs_1_.refs_3_ = bf16[528,128]{1,0:T(8,128)(2,1)S(1)} collective-permute-done((bf16[528,128]{1,0:T(8,128)(2,1)S(1)}, bf16[528,128]{1,0:T(8,128)(2,1)S(1)}, u32[]{:S(2)}, u32[]{:S(2)}) %collective-permute-start.3) | collective-permute-done | bytes 135200 | tf_op jit(solution)/shard_map/ppermute | solution.py:349
  12.2 0.4 %collective-permute-start.7 = (bf16[528,128]{1,0:T(8,128)(2,1)S(1)}, bf16[528,128]{1,0:T(8,128)(2,1)S(1)}, u32[]{:S(2)}, u32[]{:S(2)}) collective-permute-start(bf16[528,128]{1,0:T(8,128)(2,1)S(1)} %collective-permute-done.3.refs_1_.refs_3_), channel_id=1, source_target_pairs={{0,2},{2,4},{4,6},{6,7},{7,5},{5,3},{3,1},{1,0},{8,10},{10,12},{12... | collective-permute-start | bytes 405512 | tf_op jit(solution)/shard_map/ppermute | solution.py:349
  12.7 0.5 %collective-permute-done.8.refs_9_ = bf16[528,128]{1,0:T(8,128)(2,1)S(1)} collective-permute-done((bf16[528,128]{1,0:T(8,128)(2,1)S(1)}, bf16[528,128]{1,0:T(8,128)(2,1)S(1)}, u32[]{:S(2)}, u32[]{:S(2)}) %collective-permute-start.8) | collective-permute-done | bytes 135200 | tf_op jit(solution)/shard_map/ppermute | solution.py:349
  13.2 1.6 %collective-permute-start.11 = (bf16[528,128]{1,0:T(8,128)(2,1)S(1)}, bf16[528,128]{1,0:T(8,128)(2,1)S(1)}, u32[]{:S(2)}, u32[]{:S(2)}) collective-permute-start(bf16[528,128]{1,0:T(8,128)(2,1)S(1)} %collective-permute-done.8.refs_9_), channel_id=1, source_target_pairs={{2,0},{4,2},{6,4},{7,6},{5,7},{3,5},{1,3},{0,1},{10,8},{12,10},{14... | collective-permute-start | bytes 405512 | tf_op jit(solution)/shard_map/ppermute | solution.py:349
  14.7 0.0 collective-permute-done.x_ref
  14.8 0.0 copy-start.1
  14.8 0.8 %collective-permute-start.1 = (bf16[512,128]{1,0:T(8,128)(2,1)S(1)}, bf16[512,128]{1,0:T(8,128)(2,1)S(1)}, u32[]{:S(2)}, u32[]{:S(2)}) collective-permute-start(bf16[512,128]{1,0:T(8,128)(2,1)S(1)} %by_head.2.refs_2_.refs_4_), channel_id=1, source_target_pairs={{2,0},{4,2},{6,4},{7,6},{5,7},{3,5},{1,3},{0,1},{10,8},{12,10},{14... | collective-permute-start | bytes 393224 | tf_op jit(solution)/shard_map/ppermute | solution.py:349
  15.5 0.0 collective-permute-done.6.refs_6_
  15.5 1.3 %collective-permute-start.9 = (bf16[512,128]{1,0:T(8,128)(2,1)S(1)}, bf16[512,128]{1,0:T(8,128)(2,1)S(1)}, u32[]{:S(2)}, u32[]{:S(2)}) collective-permute-start(bf16[512,128]{1,0:T(8,128)(2,1)S(1)} %collective-permute-done.6.refs_6_), channel_id=1, source_target_pairs={{0,2},{2,4},{4,6},{6,7},{7,5},{5,3},{3,1},{1,0},{8,10},{10,12},{12... | collective-permute-start | bytes 393224 | tf_op jit(solution)/shard_map/ppermute | solution.py:349
  16.9 1.8 %collective-permute-done.7.refs_7_ = bf16[528,128]{1,0:T(8,128)(2,1)S(1)} collective-permute-done((bf16[528,128]{1,0:T(8,128)(2,1)S(1)}, bf16[528,128]{1,0:T(8,128)(2,1)S(1)}, u32[]{:S(2)}, u32[]{:S(2)}) %collective-permute-start.7) | collective-permute-done | bytes 135200 | tf_op jit(solution)/shard_map/ppermute | solution.py:349
  18.7 0.0 collective-permute-start.10
  18.7 0.0 collective-permute-done.11.refs_3_
  18.7 2.0 %collective-permute-start.13 = (bf16[528,128]{1,0:T(8,128)(2,1)S(1)}, bf16[528,128]{1,0:T(8,128)(2,1)S(1)}, u32[]{:S(2)}, u32[]{:S(2)}) collective-permute-start(bf16[528,128]{1,0:T(8,128)(2,1)S(1)} %collective-permute-done.11.refs_3_), channel_id=1, source_target_pairs={{2,0},{4,2},{6,4},{7,6},{5,7},{3,5},{1,3},{0,1},{10,8},{12,10},{14... | collective-permute-start | bytes 405512 | tf_op jit(solution)/shard_map/ppermute | solution.py:349
  20.7 0.7 %query_more.1 = (f32[512,256]{1,0:T(8,128)S(1)}, f32[8,256]{1,0:T(8,128)S(1)}) custom-call(s32[1]{0:T(128)S(6)} %copy.27.live_ref, bf16[1024,128]{1,0:T(8,128)(2,1)S(1)} %get-tuple-element.46.stacked, f32[512,256]{1,0:T(8,128)S(1)} %get-tuple-element.36.acc_in, ...), custom_call_target="tpu_custom_call", output_to_operand_aliasing={{0}: (2, {}), {1}: (3, {})} | custom-call | tf_op jit(solution)/shard_map/query_more/pallas_call | solution.py:189
  21.4 0.0 collective-permute-done.1.refs_8_
  21.4 1.4 %collective-permute-start.5 = (bf16[512,128]{1,0:T(8,128)(2,1)S(1)}, bf16[512,128]{1,0:T(8,128)(2,1)S(1)}, u32[]{:S(2)}, u32[]{:S(2)}) collective-permute-start(bf16[512,128]{1,0:T(8,128)(2,1)S(1)} %collective-permute-done.1.refs_8_), channel_id=1, source_target_pairs={{2,0},{4,2},{6,4},{7,6},{5,7},{3,5},{1,3},{0,1},{10,8},{12,10},{14... | collective-permute-start | bytes 393224 | tf_op jit(solution)/shard_map/ppermute | solution.py:349
  22.8 0.0 collective-permute-done.9.refs_0_
  22.8 0.7 %collective-permute-start.12 = (bf16[512,128]{1,0:T(8,128)(2,1)S(1)}, bf16[512,128]{1,0:T(8,128)(2,1)S(1)}, u32[]{:S(2)}, u32[]{:S(2)}) collective-permute-start(bf16[512,128]{1,0:T(8,128)(2,1)S(1)} %collective-permute-done.9.refs_0_), channel_id=1, source_target_pairs={{0,2},{2,4},{4,6},{6,7},{7,5},{5,3},{3,1},{1,0},{8,10},{10,12},{12... | collective-permute-start | bytes 393224 | tf_op jit(solution)/shard_map/ppermute | solution.py:349
  23.5 0.0 copy-done.1
  23.5 0.7 %both.2 = (f32[512,256]{1,0:T(8,128)S(1)}, f32[8,256]{1,0:T(8,128)S(1)}, bf16[128,4096]{1,0:T(8,128)(2,1)}) custom-call(s32[1]{0:T(128)S(6)} %copy.27.live_ref, bf16[1024,128]{1,0:T(8,128)(2,1)S(1)} %get-tuple-element.46.stacked, f32[512,256]{1,0:T(8,128)S(1)} %get-tuple-element.42.acc_in, ...), custom_call_target="tpu_custom_call", output_to_operand_aliasing={{0}: (2, {}), {1}: (3, {})} | custom-call | tf_op jit(solution)/shard_map/both/pallas_call | solution.py:266
  24.2 2.2 %collective-permute-done.5.refs_2_ = bf16[512,128]{1,0:T(8,128)(2,1)S(1)} collective-permute-done((bf16[512,128]{1,0:T(8,128)(2,1)S(1)}, bf16[512,128]{1,0:T(8,128)(2,1)S(1)}, u32[]{:S(2)}, u32[]{:S(2)}) %collective-permute-start.5) | collective-permute-done | bytes 131104 | tf_op jit(solution)/shard_map/ppermute | solution.py:349
  26.4 0.0 collective-permute-done.10.refs_1_
  26.4 3.1 %both.3 = (f32[512,256]{1,0:T(8,128)S(1)}, f32[8,256]{1,0:T(8,128)S(1)}, bf16[128,4096]{1,0:T(8,128)(2,1)}) custom-call(s32[1]{0:T(128)S(6)} %copy.27.live_ref, bf16[1024,128]{1,0:T(8,128)(2,1)S(1)} %get-tuple-element.46.stacked, f32[512,256]{1,0:T(8,128)S(1)} %get-tuple-element.47.acc_in, ...), custom_call_target="tpu_custom_call", output_to_operand_aliasing={{0}: (2, {}), {1}: (3, {}), {2}: (11, {})} | custom-call | tf_op jit(solution)/shard_map/both/pallas_call | solution.py:266
  29.6 0.0 collective-permute-done.12.refs_0_
  29.6 0.0 collective-permute-done.13.refs_1_
  29.6 1.4 %finish.1 = (bf16[32,4096]{1,0:T(8,128)(2,1)}, bf16[128,4096]{1,0:T(8,128)(2,1)}) custom-call(s32[1]{0:T(128)S(6)} %copy.27.live_ref, bf16[1024,128]{1,0:T(8,128)(2,1)S(1)} %get-tuple-element.46.stacked, f32[512,256]{1,0:T(8,128)S(1)} %get-tuple-element.51.acc, f32[8,256]{1,0:T(8,128)S(1)} %get-tuple-element.52.stat, ...), custom_call_target="tpu_custom_call", output_to_operand_aliasing={{1}: (9, {})} | custom-call | tf_op jit(solution)/shard_map/finish/pallas_call | solution.py:321
  (6 shorter events, 0.1 us)
Async XLA Ops:
  0.6 0.9 %copy-start = (bf16[128,512]{1,0:T(8,128)(2,1)S(1)}, bf16[128,512]{1,0:T(8,128)(2,1)}, u32[]{:S(2)}) copy-start(bf16[128,512]{1,0:T(8,128)(2,1)} %param.8) | copy-start | bytes 393220
  0.6 0.7 %copy-start.4 = (s32[128]{0:T(128)S(1)}, s32[128]{0:T(128)}, u32[]{:S(2)}) copy-start(s32[128]{0:T(128)} %param.10) | copy-start | bytes 1540
  1.6 4.8 %copy-start.3 = (bf16[32,4096]{1,0:T(8,128)(2,1)S(1)}, bf16[32,4096]{1,0:T(8,128)(2,1)}, u32[]{:S(2)}) copy-start(bf16[32,4096]{1,0:T(8,128)(2,1)} %q_ref.4) | copy-start | bytes 786436
  1.6 1.7 %copy-start.2 = (bf16[128,512]{1,0:T(8,128)(2,1)S(1)}, bf16[128,512]{1,0:T(8,128)(2,1)}, u32[]{:S(2)}) copy-start(bf16[128,512]{1,0:T(8,128)(2,1)} %own_k.5) | copy-start | bytes 393220
  1.6 6.5 %collective-permute-start.4 = (bf16[528,128]{1,0:T(8,128)(2,1)S(1)}, bf16[528,128]{1,0:T(8,128)(2,1)S(1)}, u32[]{:S(2)}, u32[]{:S(2)}) collective-permute-start(bf16[528,128]{1,0:T(8,128)(2,1)S(1)} %pad_maximum_fusion.v_ref.own_v.refs_1_), channel_id=1, source_target_pairs={{2,0},{4,2},{6,4},{7,6},{5,7},{3,5},{1,3},{0,1},{10,8},{12,10},{14... | collective-permute-start | bytes 405512 | tf_op jit(solution)/shard_map/ppermute | solution.py:349
  3.2 6.5 %collective-permute-start.2 = (bf16[128,512]{1,0:T(8,128)(2,1)S(1)}, bf16[128,512]{1,0:T(8,128)(2,1)S(1)}, u32[]{:S(2)}, u32[]{:S(2)}) collective-permute-start(bf16[128,512]{1,0:T(8,128)(2,1)S(1)} %copy-done.2), channel_id=1, source_target_pairs={{0,2},{2,4},{4,6},{6,7},{7,5},{5,3},{3,1},{1,0},{8,10},{10,12},{12... | collective-permute-start | bytes 393224 | tf_op jit(solution)/shard_map/ppermute | solution.py:349
  3.7 11.0 %collective-permute-start = (bf16[128,512]{1,0:T(8,128)(2,1)S(1)}, bf16[128,512]{1,0:T(8,128)(2,1)S(1)}, u32[]{:S(2)}, u32[]{:S(2)}) collective-permute-start(bf16[128,512]{1,0:T(8,128)(2,1)S(1)} %copy-done.2), channel_id=1, source_target_pairs={{2,0},{4,2},{6,4},{7,6},{5,7},{3,5},{1,3},{0,1},{10,8},{12,10},{14... | collective-permute-start | bytes 393224 | tf_op jit(solution)/shard_map/ppermute | solution.py:349
  5.3 7.0 %collective-permute-start.3 = (bf16[528,128]{1,0:T(8,128)(2,1)S(1)}, bf16[528,128]{1,0:T(8,128)(2,1)S(1)}, u32[]{:S(2)}, u32[]{:S(2)}) collective-permute-start(bf16[528,128]{1,0:T(8,128)(2,1)S(1)} %pad_maximum_fusion.v_ref.own_v.refs_1_), channel_id=1, source_target_pairs={{0,2},{2,4},{4,6},{6,7},{7,5},{5,3},{3,1},{1,0},{8,10},{10,12},{12... | collective-permute-start | bytes 405512 | tf_op jit(solution)/shard_map/ppermute | solution.py:349
  8.1 5.0 %collective-permute-start.8 = (bf16[528,128]{1,0:T(8,128)(2,1)S(1)}, bf16[528,128]{1,0:T(8,128)(2,1)S(1)}, u32[]{:S(2)}, u32[]{:S(2)}) collective-permute-start(bf16[528,128]{1,0:T(8,128)(2,1)S(1)} %collective-permute-done.4.refs_3_.refs_5_), channel_id=1, source_target_pairs={{2,0},{4,2},{6,4},{7,6},{5,7},{3,5},{1,3},{0,1},{10,8},{12,10},{14... | collective-permute-start | bytes 405512 | tf_op jit(solution)/shard_map/ppermute | solution.py:349
  9.7 5.8 %collective-permute-start.6 = (bf16[512,128]{1,0:T(8,128)(2,1)S(1)}, bf16[512,128]{1,0:T(8,128)(2,1)S(1)}, u32[]{:S(2)}, u32[]{:S(2)}) collective-permute-start(bf16[512,128]{1,0:T(8,128)(2,1)S(1)} %by_head.3.refs_0_.refs_2_), channel_id=1, source_target_pairs={{0,2},{2,4},{4,6},{6,7},{7,5},{5,3},{3,1},{1,0},{8,10},{10,12},{12... | collective-permute-start | bytes 393224 | tf_op jit(solution)/shard_map/ppermute | solution.py:349
  12.2 6.5 %collective-permute-start.7 = (bf16[528,128]{1,0:T(8,128)(2,1)S(1)}, bf16[528,128]{1,0:T(8,128)(2,1)S(1)}, u32[]{:S(2)}, u32[]{:S(2)}) collective-permute-start(bf16[528,128]{1,0:T(8,128)(2,1)S(1)} %collective-permute-done.3.refs_1_.refs_3_), channel_id=1, source_target_pairs={{0,2},{2,4},{4,6},{6,7},{7,5},{5,3},{3,1},{1,0},{8,10},{10,12},{12... | collective-permute-start | bytes 405512 | tf_op jit(solution)/shard_map/ppermute | solution.py:349
  13.2 5.5 %collective-permute-start.11 = (bf16[528,128]{1,0:T(8,128)(2,1)S(1)}, bf16[528,128]{1,0:T(8,128)(2,1)S(1)}, u32[]{:S(2)}, u32[]{:S(2)}) collective-permute-start(bf16[528,128]{1,0:T(8,128)(2,1)S(1)} %collective-permute-done.8.refs_9_), channel_id=1, source_target_pairs={{2,0},{4,2},{6,4},{7,6},{5,7},{3,5},{1,3},{0,1},{10,8},{12,10},{14... | collective-permute-start | bytes 405512 | tf_op jit(solution)/shard_map/ppermute | solution.py:349
  14.8 8.7 %copy-start.1 = (bf16[128,4096]{1,0:T(8,128)(2,1)S(1)}, bf16[128,4096]{1,0:T(8,128)(2,1)}, u32[]{:S(2)}) copy-start(bf16[128,4096]{1,0:T(8,128)(2,1)} %q_ref.7) | copy-start | bytes 3145732
  14.8 6.6 %collective-permute-start.1 = (bf16[512,128]{1,0:T(8,128)(2,1)S(1)}, bf16[512,128]{1,0:T(8,128)(2,1)S(1)}, u32[]{:S(2)}, u32[]{:S(2)}) collective-permute-start(bf16[512,128]{1,0:T(8,128)(2,1)S(1)} %by_head.2.refs_2_.refs_4_), channel_id=1, source_target_pairs={{2,0},{4,2},{6,4},{7,6},{5,7},{3,5},{1,3},{0,1},{10,8},{12,10},{14... | collective-permute-start | bytes 393224 | tf_op jit(solution)/shard_map/ppermute | solution.py:349
  15.5 7.3 %collective-permute-start.9 = (bf16[512,128]{1,0:T(8,128)(2,1)S(1)}, bf16[512,128]{1,0:T(8,128)(2,1)S(1)}, u32[]{:S(2)}, u32[]{:S(2)}) collective-permute-start(bf16[512,128]{1,0:T(8,128)(2,1)S(1)} %collective-permute-done.6.refs_6_), channel_id=1, source_target_pairs={{0,2},{2,4},{4,6},{6,7},{7,5},{5,3},{3,1},{1,0},{8,10},{10,12},{12... | collective-permute-start | bytes 393224 | tf_op jit(solution)/shard_map/ppermute | solution.py:349
  18.7 7.7 %collective-permute-start.10 = (bf16[528,128]{1,0:T(8,128)(2,1)S(1)}, bf16[528,128]{1,0:T(8,128)(2,1)S(1)}, u32[]{:S(2)}, u32[]{:S(2)}) collective-permute-start(bf16[528,128]{1,0:T(8,128)(2,1)S(1)} %collective-permute-done.7.refs_7_), channel_id=1, source_target_pairs={{0,2},{2,4},{4,6},{6,7},{7,5},{5,3},{3,1},{1,0},{8,10},{10,12},{12... | collective-permute-start | bytes 405512 | tf_op jit(solution)/shard_map/ppermute | solution.py:349
  18.7 10.9 %collective-permute-start.13 = (bf16[528,128]{1,0:T(8,128)(2,1)S(1)}, bf16[528,128]{1,0:T(8,128)(2,1)S(1)}, u32[]{:S(2)}, u32[]{:S(2)}) collective-permute-start(bf16[528,128]{1,0:T(8,128)(2,1)S(1)} %collective-permute-done.11.refs_3_), channel_id=1, source_target_pairs={{2,0},{4,2},{6,4},{7,6},{5,7},{3,5},{1,3},{0,1},{10,8},{12,10},{14... | collective-permute-start | bytes 405512 | tf_op jit(solution)/shard_map/ppermute | solution.py:349
  21.4 5.0 %collective-permute-start.5 = (bf16[512,128]{1,0:T(8,128)(2,1)S(1)}, bf16[512,128]{1,0:T(8,128)(2,1)S(1)}, u32[]{:S(2)}, u32[]{:S(2)}) collective-permute-start(bf16[512,128]{1,0:T(8,128)(2,1)S(1)} %collective-permute-done.1.refs_8_), channel_id=1, source_target_pairs={{2,0},{4,2},{6,4},{7,6},{5,7},{3,5},{1,3},{0,1},{10,8},{12,10},{14... | collective-permute-start | bytes 393224 | tf_op jit(solution)/shard_map/ppermute | solution.py:349
  22.8 6.8 %collective-permute-start.12 = (bf16[512,128]{1,0:T(8,128)(2,1)S(1)}, bf16[512,128]{1,0:T(8,128)(2,1)S(1)}, u32[]{:S(2)}, u32[]{:S(2)}) collective-permute-start(bf16[512,128]{1,0:T(8,128)(2,1)S(1)} %collective-permute-done.9.refs_0_), channel_id=1, source_target_pairs={{0,2},{2,4},{4,6},{6,7},{7,5},{5,3},{3,1},{1,0},{8,10},{10,12},{12... | collective-permute-start | bytes 393224 | tf_op jit(solution)/shard_map/ppermute | solution.py:349
